TPU v7x, 256 devices: a whole 4x4x8 slice. The times are simulated.
256 devices in a mesh: row: 16 (over y, x), col: 16 (over z, core).
Axes of the slice: x: 4, y: 4, z: 8, core: 2. Of those that a mesh axis runs over, the one named last changes fastest.
Arguments:
- slab: float32 [32768, 16384], P('row', 'col'), may hold values from -30 to 30, as said below
- test_matrix: float32 [16384, 128], P('col'), may hold values from -0.046875 to 0.046875
Outputs:
- basis: float32 [32768, 128], P(('row', 'col'))
- r_factor: float32 [128, 128], replicated
Inputs may be any that keep to these rules, and one draw needn't show every extreme that they name: `slab`: the sketch's condition number (largest over smallest singular value) is at most 2000.
All inputs are finite; a program needn't handle non-finite values.
Results may differ from a plain program's by a relative error of at most 0.0003.
Values sent between devices are 32-bit elements; how exact they have to be, the bound alone decides.
No kernel may reach another device: no remote copies, remote signals or barrier semaphores. Data moves between devices by JAX's collectives and lax.ppermute only.
A program may use at most 64 MiB of HBM per device.

v0:
```python
import math

import jax
import jax.numpy as jnp
from jax import lax
from jax.sharding import PartitionSpec as P

HIGHEST = lax.Precision.HIGHEST
CONTRACT = (((0,), (0,)), ((), ()))


def gram_of(matrix):
    return lax.dot_general(
        matrix, matrix, CONTRACT, precision=HIGHEST, preferred_element_type=jnp.float32
    )


def orthonormal(matrix, summed):
    lower_one = jnp.linalg.cholesky(summed(gram_of(matrix)))
    inner = lax.linalg.triangular_solve(
        lower_one, matrix, left_side=False, lower=True, transpose_a=True
    )
    lower_two = jnp.linalg.cholesky(summed(gram_of(inner)))
    result = lax.linalg.triangular_solve(
        lower_two, inner, left_side=False, lower=True, transpose_a=True
    )
    factor = jnp.dot(
        lower_two.T, lower_one.T, precision=HIGHEST, preferred_element_type=jnp.float32
    )
    return (result, factor)


def sum_everywhere(gram):
    return lax.psum(gram, ("row", "col"))


def local(slab, test_matrix):
    row_total = slab.shape[0] * lax.axis_size("row")
    root_rows = math.sqrt(row_total)
    partial_value = jnp.dot(
        slab, test_matrix, precision=HIGHEST, preferred_element_type=jnp.float32
    )
    sketch_one = lax.psum(partial_value, "col")
    pulled_part = lax.dot_general(
        slab, sketch_one, CONTRACT, precision=HIGHEST, preferred_element_type=jnp.float32
    )
    pulled = lax.psum(pulled_part, "row") / row_total
    owned = lax.psum_scatter(
        jnp.dot(slab, pulled, precision=HIGHEST, preferred_element_type=jnp.float32),
        "col",
        scatter_dimension=0,
        tiled=True,
    )
    result, factor = orthonormal(owned, sum_everywhere)
    return (result * root_rows, factor / root_rows)


def solution(mesh):
    in_specs = (P("row", "col"), P("col", None))
    out_specs = (P(("row", "col"), None), P())
    return jax.shard_map(local, mesh=mesh, in_specs=in_specs, out_specs=out_specs, check_vma=False)
```

profile of v0, /device:TPU:1, one launch (start us, length us, event | category | flops | bytes accessed | tf_op | source)
XLA Modules:
  0.0 847.2 jit_solution(4430770114689326085)
XLA Ops:
  7.2 0.0 all-reduce.5.cloned.1.call-start
  7.2 1.0 copy-done
  8.2 9.8 %fusion.22 = f32[2048,128]{1,0:T(8,128)} fusion(f32[2048,1024]{1,0:T(8,128)} %param.5, f32[1024,128]{1,0:T(8,128)S(1)} %copy-done), kind=kOutput, calls=%fused_computation.33 | convolution fusion | flops 3221225472 | bytes 9961472 | tf_op jit(solution)/shard_map/dot_general | solution.py:40
  18.1 0.0 all-reduce.7.cloned.1.call-start
  18.1 115.1 %all-reduce.5.cloned.1.call-done = f32[2048,128]{1,0:T(8,128)} async-done(((f32[2048,128]{1,0:T(8,128)}), f32[2048,128]{1,0:T(8,128)}) %all-reduce.5.cloned.1.call-update) | async-done | bytes 1048592 | tf_op jit(solution)/shard_map/psum | solution.py:43
  133.2 9.2 %convolution_bitcast_fusion.1 = f32[1024,128]{0,1:T(8,128)} fusion(f32[2048,128]{1,0:T(8,128)} %all-reduce.5.cloned.1.call-done, f32[2048,1024]{1,0:T(8,128)} %param.5), kind=kOutput, calls=%fused_computation.1 | convolution fusion | flops 3221225472 | bytes 9961472 | tf_op jit(solution)/shard_map/dot_general | solution.py:44
  142.4 0.2 reduce-scatter.2.cloned.1.call-start
  142.7 94.3 %all-reduce.7.cloned.1.call-done = f32[1024,128]{0,1:T(8,128)} async-done(((f32[1024,128]{0,1:T(8,128)}), f32[1024,128]{0,1:T(8,128)}) %all-reduce.7.cloned.1.call-update) | async-done | bytes 524304 | tf_op jit(solution)/shard_map/psum | solution.py:47
  236.9 13.0 %convolution_bitcast_fusion = f32[2048,128]{0,1:T(8,128)} fusion(f32[2048,1024]{1,0:T(8,128)} %param.5, f32[1024,128]{0,1:T(8,128)} %all-reduce.7.cloned.1.call-done), kind=kOutput, calls=%fused_computation | convolution fusion | flops 3221356544 | bytes 9961472 | tf_op jit(solution)/shard_map/dot_general | solution.py:49
  249.9 0.0 all-reduce.9.cloned.1.call-start
  250.0 55.4 %reduce-scatter.2.cloned.1.call-done = f32[128,128]{0,1:T(8,128)} async-done(((f32[2048,128]{0,1:T(8,128)}), f32[128,128]{0,1:T(8,128)}) %reduce-scatter.2.cloned.1.call-update) | async-done | bytes 65552 | tf_op jit(solution)/shard_map/reduce_scatter | solution.py:48
  305.3 1.8 fusion.23
  307.2 0.3 all-reduce.11.cloned.1.call-start
  307.4 244.3 %all-reduce.9.cloned.1.call-done = f32[128,128]{0,1:T(8,128)} async-done(((f32[128,128]{0,1:T(8,128)}), f32[128,128]{0,1:T(8,128)}) %all-reduce.9.cloned.1.call-update) | async-done | bytes 65552 | tf_op jit(solution)/shard_map/psum | solution.py:34
  551.7 0.9 copy.5
  552.7 0.9 fusion.6
  553.5 11.7 %cholesky.44 = f32[128,128]{1,0:T(8,128)S(1)} custom-call(f32[128,128]{1,0:T(8,128)S(1)} %fusion.6), custom_call_target="Cholesky" | custom-call | tf_op jit(solution)/shard_map/jit(cholesky)/cholesky | solution.py:19
  565.3 0.6 compare_reduce_fusion.1
  565.9 0.7 fusion.10
  566.6 9.8 %custom-call.6 = f32[1,128,128]{1,2,0:T(8,128)S(1)} custom-call(f32[1,128,128]{2,1,0:T(8,128)S(1)} %fusion.10), custom_call_target="InvertDiagBlocksLowerTriangular" | custom-call | tf_op jit(solution)/shard_map/triangular_solve/custom-call.0 | solution.py:20
  576.4 1.1 convolution_bitcast_fusion.3
  577.5 0.9 fusion.24
  578.4 234.2 %all-reduce.11.cloned.1.call-done = f32[128,128]{0,1:T(8,128)} async-done(((f32[128,128]{0,1:T(8,128)}), f32[128,128]{0,1:T(8,128)}) %all-reduce.11.cloned.1.call-update) | async-done | bytes 65552 | tf_op jit(solution)/shard_map/psum | solution.py:34
  812.6 0.9 copy.7
  813.5 0.9 fusion.4
  814.4 11.7 %cholesky.55 = f32[128,128]{1,0:T(8,128)S(1)} custom-call(f32[128,128]{1,0:T(8,128)S(1)} %fusion.4), custom_call_target="Cholesky" | custom-call | tf_op jit(solution)/shard_map/jit(cholesky)/cholesky | solution.py:23
  826.1 0.7 compare_reduce_fusion
  826.9 2.3 convolution_multiply_fusion
  829.1 0.7 select_bitcast_fusion
  829.8 9.8 %custom-call.7 = f32[1,128,128]{1,2,0:T(8,128)S(1)} custom-call(f32[1,128,128]{2,1,0:T(8,128)S(1)} %select_bitcast_fusion), custom_call_target="InvertDiagBlocksLowerTriangular" | custom-call | tf_op jit(solution)/shard_map/triangular_solve/custom-call.0 | solution.py:24
  839.6 0.3 fusion
  839.9 0.7 copy.8
  (8 shorter events, 0.2 us)
Async XLA Ops:
  7.2 1.0 copy-start
  7.2 126.1 %all-reduce.5.cloned.1.call-start = ((), (), s32[]{:S(2)}) async-start(), calls=%async_computation.1 | async-start | bytes 2097152 | tf_op jit(solution)/shard_map/psum | solution.py:43
  18.1 218.8 %all-reduce.7.cloned.1.call-start = ((), (), s32[]{:S(2)}) async-start(), calls=%async_computation.2 | async-start | bytes 1048576 | tf_op jit(solution)/shard_map/psum | solution.py:47
  142.4 162.9 %reduce-scatter.2.cloned.1.call-start = ((), (), s32[]{:S(2)}) async-start(), calls=%async_computation.3 | async-start | bytes 1114112 | tf_op jit(solution)/shard_map/reduce_scatter | solution.py:48
  249.9 301.8 %all-reduce.9.cloned.1.call-start = ((), (), s32[]{:S(2)}) async-start(), calls=%async_computation.4 | async-start | bytes 131072 | tf_op jit(solution)/shard_map/psum | solution.py:34
  307.2 505.4 %all-reduce.11.cloned.1.call-start = ((), (), s32[]{:S(2)}) async-start(), calls=%async_computation.5 | async-start | bytes 131072 | tf_op jit(solution)/shard_map/psum | solution.py:34
Sparse Core Ops, SparseCore 0:
  18.2 114.9 all-reduce.4
  142.5 94.3 all-reduce.6
  250.1 55.2 reduce-scatter.1
  312.2 239.4 all-reduce.8
  578.6 234.0 all-reduce.10
where the time goes:
time: 848 us; the launch traced here: 847 us
  waiting for transfers between devices  743 us (88%)
  other arithmetic  47.5 us (6%)
  matrix products  38.4 us (5%)
  between operations  13.9 us (2%)
    psum x2, waiting for transfers between devices, sum_everywhere(): return lax.psum(gram, ('row', 'col'))  478 us
    psum x1, waiting for transfers between devices, local(): sketch_one = lax.psum(partial_value, 'col')  115 us
    psum x1, waiting for transfers between devices, local(): pulled = lax.psum(pulled_part, 'row') / row_total  94.3 us
    reduce_scatter x1, waiting for transfers between devices, local(): lax.psum_scatter(jnp.dot(slab, pulled, precision=HIGHEST, preferred_eleme...  55.4 us
  transfers between devices with their start and end apart: 5, of which 5 were waited for; matrix products, arithmetic and copies ran while one was open for 0% of the time, Pallas kernels for 0%

commit v1 on v0

v1 whole, which is shorter than its diff:
```python
import math

import jax
import jax.numpy as jnp
from jax import lax
from jax.sharding import Mesh
from jax.sharding import PartitionSpec as P

HIGH = lax.Precision.HIGH
HIGHEST = lax.Precision.HIGHEST
CONTRACT = (((0,), (0,)), ((), ()))
ROW = ("y", "x")
SWAP = [(0, 1), (1, 0)]


def swap(value):
    return lax.ppermute(value, "core", SWAP)


def exchange(value, axes):
    return lax.all_to_all(value, axes, 0, 0, tiled=False)


def gathered(value, axes):
    count = lax.axis_size(axes)
    return exchange(jnp.broadcast_to(value, (count,) + value.shape), axes)


def halves(value):
    first, second = jnp.split(value, 2, axis=0)
    zero = lax.axis_index("core") == 0
    return jnp.where(zero, first, second), jnp.where(zero, second, first)


def whole(own, other):
    zero = lax.axis_index("core") == 0
    return jnp.concatenate([jnp.where(zero, own, other), jnp.where(zero, other, own)], axis=0)


def gram_of(matrix):
    return lax.dot_general(
        matrix, matrix, CONTRACT, precision=HIGHEST, preferred_element_type=jnp.float32
    )


def pack(gram):
    half = gram.shape[0] // 2
    last = gram[half:, half:]
    return jnp.concatenate(
        [gram[:half], jnp.concatenate([last[: half // 2], last[half // 2 :]], axis=1)], axis=0
    )


def unpack(packed):
    half = packed.shape[1] // 2
    top = packed[:half]
    tail = packed[half:]
    last = jnp.concatenate([tail[:, :half], tail[:, half:]], axis=0)
    return jnp.concatenate([top, jnp.concatenate([top[:, half:].T, last], axis=1)], axis=0)


def sum_gram(gram, stages):
    own, other = halves(pack(gram))
    value = own + swap(other)
    for axes in stages:
        value = jnp.sum(gathered(value, axes), axis=0)
    return unpack(whole(value, swap(value)))


def factor(gram):
    lower = jnp.linalg.cholesky(gram)
    eye = jnp.eye(gram.shape[0], dtype=gram.dtype)
    inverse = lax.linalg.triangular_solve(lower, eye, left_side=True, lower=True)
    return lower.T, inverse.T


def matmul(a, b, precision=HIGHEST):
    return jnp.dot(a, b, precision=precision, preferred_element_type=jnp.float32)


def local(slab, test_matrix):
    rows, columns = slab.shape
    wide = test_matrix.shape[1]
    zs = lax.axis_size("z")
    row_count = lax.axis_size(ROW)
    row_total = rows * row_count
    root_rows = math.sqrt(row_total)

    own, other = halves(matmul(slab, test_matrix, HIGH))
    part = (own + swap(other)).reshape(zs, -1, wide)
    piece = jnp.sum(exchange(part, "z"), axis=0)
    own = gathered(piece, "z").reshape(-1, wide)
    sketch_one = whole(own, swap(own))

    pulled_part = lax.dot_general(
        slab, sketch_one, CONTRACT, precision=HIGH, preferred_element_type=jnp.float32
    )
    piece = jnp.sum(exchange(pulled_part.reshape(row_count, -1, wide), ROW), axis=0) / row_total
    pulled = gathered(piece, ROW).reshape(-1, wide)

    before, before_inverse = factor(sum_gram(gram_of(pulled), ("z",)))

    product = matmul(slab, pulled).reshape(zs, 2, -1, wide)
    own, other = halves(jnp.swapaxes(product, 0, 1).reshape(rows, wide))
    part = (own + swap(other)).reshape(zs, -1, wide)
    sketch = jnp.sum(exchange(part, "z"), axis=0)

    inner = matmul(sketch, before_inverse)
    after, after_inverse = factor(sum_gram(gram_of(inner), (ROW, "z")))
    basis = matmul(inner, after_inverse) * root_rows
    return basis, matmul(after, before) / root_rows


def solution(mesh):
    sizes = dict(mesh.shape)
    chips = mesh.devices.reshape(4, sizes["row"] // 4, sizes["col"] // 2, 2)
    fine = Mesh(chips, ("y", "x", "z", "core"))
    col = ("z", "core")
    in_specs = (P(ROW, col), P(col, None))
    out_specs = (P(ROW + col, None), P())
    return jax.shard_map(local, mesh=fine, in_specs=in_specs, out_specs=out_specs, check_vma=False)
```

time: 848 us -> 214 us (0.25)
  waiting for transfers between devices: 743 us -> 7.19 us
  blocking collectives: 0 us -> 98.5 us
  starting transfers between devices: 0.61 us -> 24 us
  between operations: 13.9 us -> 1.07 us
  matrix products: 38.4 us -> 28.3 us
    psum x4 -> x0, waiting for transfers between devices: 688 us -> none  [the longest x2 478 us: sum_everywhere(): return lax.psum(gram, ('row', 'col'))]
    all_to_all x0 -> x6, blocking collectives: none -> 98.5 us  [exchange(): return lax.all_to_all(value, axes, 0, 0, tiled=False)]
    reduce_scatter x1 -> x0, waiting for transfers between devices: 55.4 us -> none  [local(): lax.psum_scatter(jnp.dot(slab, pulled, precision=HIGHEST, preferred_eleme...]
    ppermute x0 -> x7, starting transfers between devices: none -> 13.8 us  [swap(): return lax.ppermute(value, 'core', SWAP)]
    all_to_all x0 -> x2, starting transfers between devices: none -> 10.2 us  [exchange(): return lax.all_to_all(value, axes, 0, 0, tiled=False)]
    dot_general x4 -> x6, matrix products: 34.3 us -> 26.4 us  [the longest x5 20.4 us: matmul(): jnp.dot(a, b, precision=precision, preferred_element_type=jnp.float32)]
  transfers between devices with their start and end apart: 5 -> 9, of which waited for: 5 -> 6; matrix products, arithmetic and copies ran while one was open for 0% -> 18% of each run, Pallas kernels for 0% -> 0%
where the time goes in v1:
time: 214 us
  blocking collectives  98.5 us (46%)
  other arithmetic  48.3 us (23%)
  matrix products  28.3 us (13%)
  starting transfers between devices  24 us (11%)
  waiting for transfers between devices  7.19 us (3%)
  local copies, waits for them, and re-layouts  6.26 us (3%)
    all_to_all x6, blocking collectives, exchange(): return lax.all_to_all(value, axes, 0, 0, tiled=False)  98.5 us
    another operation x6, other arithmetic, factor(): lower = jnp.linalg.cholesky(gram)  24.9 us
    another operation x4, other arithmetic, factor(): lax.linalg.triangular_solve(lower, eye, left_side=True, lower=True)  21 us
    dot_general x5, matrix products, matmul(): jnp.dot(a, b, precision=precision, preferred_element_type=jnp.float32)  20.4 us
    ppermute x7, starting transfers between devices, swap(): return lax.ppermute(value, 'core', SWAP)  13.8 us
    all_to_all x2, starting transfers between devices, exchange(): return lax.all_to_all(value, axes, 0, 0, tiled=False)  10.2 us
    ppermute x7, waiting for transfers between devices, swap(): return lax.ppermute(value, 'core', SWAP)  7.18 us
    dot_general x1, matrix products, local(): lax.dot_general(slab, sketch_one, CONTRACT, precision=HIGH, preferred_ele...  5.96 us
  transfers between devices with their start and end apart: 9, of which 6 were waited for; matrix products, arithmetic and copies ran while one was open for 18% of the time, Pallas kernels for 0%

profile of v1, /device:TPU:1, one launch (start us, length us, event | category | flops | bytes accessed | tf_op | source)
XLA Modules:
  0.0 213.6 jit_solution(4463767177954841261)
XLA Ops:
  0.7 1.0 copy-done
  1.7 5.8 %fusion.26 = f32[2048,128]{1,0:T(8,128)S(1)} fusion(f32[2048,1024]{1,0:T(8,128)} %param.5, f32[1024,128]{1,0:T(8,128)S(1)} %copy-done), kind=kOutput, calls=%fused_computation.67 | convolution fusion | flops 1610612736 | bytes 9961472 | tf_op jit(solution)/shard_map/dot_general | solution.py:78
  7.6 3.3 %collective-permute-start = (f32[1024,128]{1,0:T(8,128)S(1)}, f32[1024,128]{1,0:T(8,128)S(1)}, u32[]{:S(2)}, u32[]{:S(2)}) collective-permute-start(f32[1024,128]{1,0:T(8,128)S(1)} %slice_select_fusion), channel_id=1, source_target_pairs={{0,1},{1,0},{2,3},{3,2},{4,5},{5,4},{6,7},{7,6},{8,9},{9,8},{10,11... | collective-permute-start | bytes 1572872 | tf_op jit(solution)/shard_map/ppermute | solution.py:17
  10.9 1.5 collective-permute-done
  12.5 22.9 %all_to_all.40 = f32[8,128,128]{2,1,0:T(8,128)S(1)} all-to-all(f32[8,128,128]{2,1,0:T(8,128)S(1)} %bitcast.57), channel_id=1, replica_groups=mesh['y'=4,'x'=4,'z'=8,'core'=2] {'z'}, dimensions={0} | all-to-all | bytes 1048576 | tf_op jit(solution)/shard_map/all_to_all | solution.py:21
  35.5 17.3 %all_to_all.41 = f32[8,128,128]{2,1,0:T(8,128)S(1)} all-to-all(f32[8,128,128]{2,1,0:T(8,128)S(1)} %broadcast_in_dim.16), channel_id=1, replica_groups=mesh['y'=4,'x'=4,'z'=8,'core'=2] {'z'}, dimensions={0} | all-to-all | bytes 1048576 | tf_op jit(solution)/shard_map/all_to_all | solution.py:21
  52.8 3.6 %collective-permute-start.1 = (f32[1024,128]{1,0:T(8,128)S(1)}, f32[1024,128]{1,0:T(8,128)S(1)}, u32[]{:S(2)}, u32[]{:S(2)}) collective-permute-start(f32[1024,128]{1,0:T(8,128)S(1)} %bitcast.56), channel_id=1, source_target_pairs={{0,1},{1,0},{2,3},{3,2},{4,5},{5,4},{6,7},{7,6},{8,9},{9,8},{10,11... | collective-permute-start | bytes 1572872 | tf_op jit(solution)/shard_map/ppermute | solution.py:17
  56.4 1.5 collective-permute-done.1
  58.0 6.0 %convolution_bitcast_fusion.1 = f32[1024,128]{0,1:T(8,128)S(1)} fusion(f32[2048,1024]{1,0:T(8,128)} %param.5, f32[1024,128]{1,0:T(8,128)S(1)} %get-tuple-element.7, f32[1024,128]{1,0:T(8,128)S(1)} %get-tuple-element.6), kind=kOutput, calls=%fused_computation.1 | convolution fusion | flops 1610874880 | bytes 9961472 | tf_op jit(solution)/shard_map/dot_general | solution.py:95
  64.2 17.3 %all_to_all.42 = f32[16,64,128]{2,1,0:T(8,128)S(1)} all-to-all(f32[16,64,128]{2,1,0:T(8,128)S(1)} %bitcast.59), channel_id=1, replica_groups=mesh['y'=4,'x'=4,'z'=8,'core'=2] {'y','x'}, dimensions={0} | all-to-all | bytes 1048576 | tf_op jit(solution)/shard_map/all_to_all | solution.py:21
  81.5 13.4 %all_to_all.43 = f32[16,64,128]{2,1,0:T(8,128)S(1)} all-to-all(f32[16,64,128]{2,1,0:T(8,128)S(1)} %broadcast_in_dim.17), channel_id=1, replica_groups=mesh['y'=4,'x'=4,'z'=8,'core'=2] {'y','x'}, dimensions={0} | all-to-all | bytes 1048576 | tf_op jit(solution)/shard_map/all_to_all | solution.py:21
  95.0 1.0 convolution_bitcast_fusion.2
  96.6 2.4 %collective-permute-start.3 = (f32[48,128]{0,1:T(8,128)S(1)}, f32[48,128]{0,1:T(8,128)S(1)}, u32[]{:S(2)}, u32[]{:S(2)}) collective-permute-start(f32[48,128]{0,1:T(8,128)S(1)} %broadcast_select_fusion.9), channel_id=1, source_target_pairs={{0,1},{1,0},{2,3},{3,2},{4,5},{5,4},{6,7},{7,6},{8,9},{9,8},{10,11... | collective-permute-start | bytes 73736 | tf_op jit(solution)/shard_map/ppermute | solution.py:17
  99.0 0.9 collective-permute-done.3
  100.8 3.6 %all-to-all-start.5 = ((f32[8,48,128]{2,1,0:T(8,128)}), f32[8,48,128]{2,1,0:T(8,128)S(1)}, u32[]{:S(2)}, u32[]{:S(2)}) async-start(f32[8,48,128]{2,1,0:T(8,128)} %broadcast_in_dim.18), calls=%async_computation.5 | async-start | bytes 393216 | tf_op jit(solution)/shard_map/all_to_all | solution.py:21
  104.3 11.2 %convolution_bitcast_fusion = f32[2048,128]{0,1:T(8,128)S(1)} fusion(f32[1024,128]{1,0:T(8,128)S(1)} %bitcast.54, f32[2048,1024]{1,0:T(8,128)} %param.5), kind=kOutput, calls=%fused_computation | convolution fusion | flops 3221225472 | bytes 9961472 | tf_op jit(solution)/shard_map/dot_general | solution.py:78
  115.5 0.9 reshape.44
  117.0 0.8 broadcast_select_fusion.1
  119.2 1.4 collective-permute-done.2
  120.6 1.0 copy.67
  121.6 6.7 %all-to-all-start.4 = ((f32[8,128,128]{1,2,0:T(8,128)}), f32[8,128,128]{1,2,0:T(8,128)S(1)}, u32[]{:S(2)}, u32[]{:S(2)}) async-start(f32[8,128,128]{1,2,0:T(8,128)} %copy.67), calls=%async_computation.4 | async-start | bytes 1048576 | tf_op jit(solution)/shard_map/all_to_all | solution.py:21
  128.6 11.7 %cholesky.44 = f32[128,128]{1,0:T(8,128)S(1)} custom-call(f32[128,128]{1,0:T(8,128)S(1)} %fusion.10), custom_call_target="Cholesky" | custom-call | tf_op jit(solution)/shard_map/jit(cholesky)/cholesky | solution.py:71
  141.6 9.8 %custom-call.6 = f32[1,128,128]{1,2,0:T(8,128)S(1)} custom-call(f32[1,128,128]{2,1,0:T(8,128)S(1)} %select_bitcast_fusion.1), custom_call_target="InvertDiagBlocksLowerTriangular" | custom-call | tf_op jit(solution)/shard_map/triangular_solve/custom-call.0 | solution.py:73
  153.5 0.9 collective-permute-done.5
  154.6 12.2 %all_to_all.44 = f32[16,48,128]{2,1,0:T(8,128)S(1)} all-to-all(f32[16,48,128]{2,1,0:T(8,128)S(1)} %broadcast_in_dim.19), channel_id=1, replica_groups=mesh['y'=4,'x'=4,'z'=8,'core'=2] {'y','x'}, dimensions={0} | all-to-all | bytes 786432 | tf_op jit(solution)/shard_map/all_to_all | solution.py:21
  166.9 15.4 %all_to_all.45 = f32[8,48,128]{2,1,0:T(8,128)S(1)} all-to-all(f32[8,48,128]{2,1,0:T(8,128)S(1)} %broadcast_in_dim.20), channel_id=1, replica_groups=mesh['y'=4,'x'=4,'z'=8,'core'=2] {'z'}, dimensions={0} | all-to-all | bytes 393216 | tf_op jit(solution)/shard_map/all_to_all | solution.py:21
  182.4 3.2 %collective-permute-start.6 = (f32[48,128]{0,1:T(8,128)S(1)}, f32[48,128]{0,1:T(8,128)S(1)}, u32[]{:S(2)}, u32[]{:S(2)}) collective-permute-start(f32[48,128]{0,1:T(8,128)S(1)} %copy.83), channel_id=1, source_target_pairs={{0,1},{1,0},{2,3},{3,2},{4,5},{5,4},{6,7},{7,6},{8,9},{9,8},{10,11... | collective-permute-start | bytes 73736 | tf_op jit(solution)/shard_map/ppermute | solution.py:17
  185.6 0.9 collective-permute-done.6
  187.2 11.7 %cholesky.55 = f32[128,128]{1,0:T(8,128)S(1)} custom-call(f32[128,128]{1,0:T(8,128)S(1)} %fusion.8), custom_call_target="Cholesky" | custom-call | tf_op jit(solution)/shard_map/jit(cholesky)/cholesky | solution.py:71
  199.7 2.3 %convolution_multiply_fusion = f32[128,128]{1,0:T(8,128)} fusion(f32[128,128]{1,0:T(8,128)S(1)} %cholesky.44, f32[128,128]{1,0:T(8,128)S(1)} %cholesky.55, pred[]{:T(512)} %compare_reduce_fusion, pred[]{:T(512)} %compare_reduce_fusion.1), kind=kOutput, calls=%fused_computation.2 | convolution fusion | flops 25280512 | bytes 196610 | tf_op jit(solution)/shard_map/dot_general | solution.py:78
  202.6 9.8 %custom-call.7 = f32[1,128,128]{1,2,0:T(8,128)S(1)} custom-call(f32[1,128,128]{2,1,0:T(8,128)S(1)} %select_bitcast_fusion), custom_call_target="InvertDiagBlocksLowerTriangular" | custom-call | tf_op jit(solution)/shard_map/triangular_solve/custom-call.0 | solution.py:73
  212.7 0.9 convolution_multiply_fusion.1
  (74 shorter events, 10.2 us)
Async XLA Ops:
  0.6 1.0 copy-start
  7.6 4.9 %collective-permute-start = (f32[1024,128]{1,0:T(8,128)S(1)}, f32[1024,128]{1,0:T(8,128)S(1)}, u32[]{:S(2)}, u32[]{:S(2)}) collective-permute-start(f32[1024,128]{1,0:T(8,128)S(1)} %slice_select_fusion), channel_id=1, source_target_pairs={{0,1},{1,0},{2,3},{3,2},{4,5},{5,4},{6,7},{7,6},{8,9},{9,8},{10,11... | collective-permute-start | bytes 1572872 | tf_op jit(solution)/shard_map/ppermute | solution.py:17
  52.8 5.1 %collective-permute-start.1 = (f32[1024,128]{1,0:T(8,128)S(1)}, f32[1024,128]{1,0:T(8,128)S(1)}, u32[]{:S(2)}, u32[]{:S(2)}) collective-permute-start(f32[1024,128]{1,0:T(8,128)S(1)} %bitcast.56), channel_id=1, source_target_pairs={{0,1},{1,0},{2,3},{3,2},{4,5},{5,4},{6,7},{7,6},{8,9},{9,8},{10,11... | collective-permute-start | bytes 1572872 | tf_op jit(solution)/shard_map/ppermute | solution.py:17
  96.6 3.3 %collective-permute-start.3 = (f32[48,128]{0,1:T(8,128)S(1)}, f32[48,128]{0,1:T(8,128)S(1)}, u32[]{:S(2)}, u32[]{:S(2)}) collective-permute-start(f32[48,128]{0,1:T(8,128)S(1)} %broadcast_select_fusion.9), channel_id=1, source_target_pairs={{0,1},{1,0},{2,3},{3,2},{4,5},{5,4},{6,7},{7,6},{8,9},{9,8},{10,11... | collective-permute-start | bytes 73736 | tf_op jit(solution)/shard_map/ppermute | solution.py:17
  100.8 15.7 %all-to-all-start.5 = ((f32[8,48,128]{2,1,0:T(8,128)}), f32[8,48,128]{2,1,0:T(8,128)S(1)}, u32[]{:S(2)}, u32[]{:S(2)}) async-start(f32[8,48,128]{2,1,0:T(8,128)} %broadcast_in_dim.18), calls=%async_computation.5 | async-start | bytes 393216 | tf_op jit(solution)/shard_map/all_to_all | solution.py:21
  116.6 2.2 %collective-permute-start.4 = (f32[48,128]{0,1:T(8,128)S(1)}, f32[48,128]{0,1:T(8,128)S(1)}, u32[]{:S(2)}, u32[]{:S(2)}) collective-permute-start(f32[48,128]{0,1:T(8,128)S(1)} %copy.74), channel_id=1, source_target_pairs={{0,1},{1,0},{2,3},{3,2},{4,5},{5,4},{6,7},{7,6},{8,9},{9,8},{10,11... | collective-permute-start | bytes 73736 | tf_op jit(solution)/shard_map/ppermute | solution.py:17
  118.6 2.0 collective-permute-start.2
  121.6 30.1 %all-to-all-start.4 = ((f32[8,128,128]{1,2,0:T(8,128)}), f32[8,128,128]{1,2,0:T(8,128)S(1)}, u32[]{:S(2)}, u32[]{:S(2)}) async-start(f32[8,128,128]{1,2,0:T(8,128)} %copy.67), calls=%async_computation.4 | async-start | bytes 1048576 | tf_op jit(solution)/shard_map/all_to_all | solution.py:21
  153.0 1.4 collective-permute-start.5
  182.4 4.1 %collective-permute-start.6 = (f32[48,128]{0,1:T(8,128)S(1)}, f32[48,128]{0,1:T(8,128)S(1)}, u32[]{:S(2)}, u32[]{:S(2)}) collective-permute-start(f32[48,128]{0,1:T(8,128)S(1)} %copy.83), channel_id=1, source_target_pairs={{0,1},{1,0},{2,3},{3,2},{4,5},{5,4},{6,7},{7,6},{8,9},{9,8},{10,11... | collective-permute-start | bytes 73736 | tf_op jit(solution)/shard_map/ppermute | solution.py:17

commit v2 on v1

v2 whole, which is shorter than its diff:
```python
import functools
import math

import jax
import jax.numpy as jnp
from jax import lax
from jax.experimental import pallas as pl
from jax.experimental.pallas import tpu as pltpu
from jax.sharding import Mesh
from jax.sharding import PartitionSpec as P

HIGHEST = lax.Precision.HIGHEST
CONTRACT = (((0,), (0,)), ((), ()))
TRANSPOSED = (((1,), (1,)), ((), ()))
ROW = ("y", "x")
SWAP = [(0, 1), (1, 0)]
TILE = 8
PANEL = 16
STEP = 2
VMEM = 48 * 1024 * 1024


def swap(value):
    return lax.ppermute(value, "core", SWAP)


def exchange(value, axes):
    return lax.all_to_all(value, axes, 0, 0, tiled=False)


def gathered(value, axes):
    count = lax.axis_size(axes)
    return exchange(jnp.broadcast_to(value, (count,) + value.shape), axes)


def dot(a, b, dims=(((1,), (0,)), ((), ())), precision=None):
    return lax.dot_general(a, b, dims, precision=precision, preferred_element_type=jnp.float32)


def split(value, count):
    parts = []
    for _ in range(count):
        parts.append(value.astype(jnp.bfloat16))
        value = value - parts[-1].astype(jnp.float32)
    return parts


def params():
    return pltpu.CompilerParams(vmem_limit_bytes=VMEM)


def project_kernel(count, half_ref, slab_ref, right_ref, out_ref, parts_ref):
    wide = right_ref.shape[1]

    @pl.when(pl.program_id(0) == 0)
    def _():
        for place, part in enumerate(split(right_ref[...], count)):
            parts_ref[:, place * wide : (place + 1) * wide] = part

    block = slab_ref[...].reshape(-1, slab_ref.shape[-1])
    parts = split(block, count)
    pair = parts_ref[:, : 2 * wide]
    first = dot(parts[0], pair)
    if count == 2:
        small = first[:, wide:] + dot(parts[1], parts_ref[:, :wide])
    else:
        second = dot(parts[1], pair)
        third = dot(parts[0], parts_ref[:, 2 * wide :]) + dot(parts[2], parts_ref[:, :wide])
        small = (first[:, wide:] + second[:, :wide]) + (second[:, wide:] + third)
    out_ref[...] = (first[:, :wide] + small).reshape(out_ref.shape)


def project(slab, right, half, count):
    zs, _, height, depth = slab.shape
    wide = right.shape[1]
    return pl.pallas_call(
        functools.partial(project_kernel, count),
        grid_spec=pltpu.PrefetchScalarGridSpec(
            num_scalar_prefetch=1,
            grid=(zs // STEP,),
            in_specs=[
                pl.BlockSpec((STEP, 1, height, depth), lambda i, half: (i, half[0], 0, 0)),
                pl.BlockSpec((depth, wide), lambda i, half: (0, 0)),
            ],
            out_specs=pl.BlockSpec((STEP, height, wide), lambda i, half: (i, 0, 0)),
            scratch_shapes=[pltpu.VMEM((depth, count * wide), jnp.bfloat16)],
        ),
        out_shape=jax.ShapeDtypeStruct((zs, height, wide), jnp.float32),
        compiler_params=params(),
        cost_estimate=pl.CostEstimate(
            flops=2 * zs * height * depth * wide * (4 if count == 2 else 8),
            bytes_accessed=4 * zs * height * depth,
            transcendentals=0,
        ),
        name="project%d" % count,
    )(half, slab, right)


def pull_kernel(more, half_ref, slab_ref, left_ref, *refs):
    out_ref, total_ref = refs[-2:]
    step = pl.program_id(0)
    wide = left_ref.shape[-1]
    block = slab_ref[...].reshape(-1, slab_ref.shape[-1])
    high, low = split(block, 2)
    left = jnp.concatenate(split(left_ref[...].reshape(-1, wide), 2), axis=1)
    left = jnp.transpose(left.astype(jnp.float32)).astype(jnp.bfloat16)
    both = dot(left, high)
    value = both[:wide] + (both[wide:] + dot(left[:wide], low))

    @pl.when(step == 0)
    def _():
        total_ref[...] = value

    @pl.when(step > 0)
    def _():
        total_ref[...] += value

    @pl.when(step == pl.num_programs(0) - 1)
    def _():
        result = jnp.transpose(total_ref[...])
        out_ref[...] = result + refs[0][...] if more else result


def pull(slab, left, half, before=None):
    zs, _, height, depth = slab.shape
    wide = left.shape[-1]
    flat = pl.BlockSpec((depth, wide), lambda i, half: (0, 0))
    more = before is not None
    return pl.pallas_call(
        functools.partial(pull_kernel, more),
        grid_spec=pltpu.PrefetchScalarGridSpec(
            num_scalar_prefetch=1,
            grid=(zs // STEP,),
            in_specs=[
                pl.BlockSpec((STEP, 1, height, depth), lambda i, half: (i, half[0], 0, 0)),
                pl.BlockSpec((STEP, height, wide), lambda i, half: (i, 0, 0)),
            ]
            + [flat] * more,
            out_specs=flat,
            scratch_shapes=[pltpu.VMEM((wide, depth), jnp.float32)],
        ),
        out_shape=jax.ShapeDtypeStruct((depth, wide), jnp.float32),
        compiler_params=params(),
        cost_estimate=pl.CostEstimate(
            flops=2 * zs * height * depth * wide * 4,
            bytes_accessed=4 * zs * height * depth,
            transcendentals=0,
        ),
        name="pull",
    )(half, slab, left, *([before] if more else []))


def spread(row):
    return jnp.broadcast_to(row, (TILE, row.shape[1]))


def eliminate(gram, floor):
    n = gram.shape[0]
    count, per = n // TILE, PANEL // TILE
    sub = lax.broadcasted_iota(jnp.int32, (TILE, n), 0)
    lane = lax.broadcasted_iota(jnp.int32, (TILE, n), 1)
    left = [gram[TILE * i : TILE * (i + 1)] for i in range(count)]
    right = [(lane == sub + TILE * i).astype(jnp.float32) for i in range(count)]
    scale = [None] * count
    for start in range(0, count, per):
        tiles = range(start, min(start + 2 * per, count))
        base = start * TILE
        column = {
            (t, q): jnp.broadcast_to(left[q][:, base + t : base + t + 1], (TILE, n))
            for t in range(PANEL)
            for q in tiles
            if start + t // TILE <= q
        }
        pivots = []
        for s in range(PANEL):
            here, at = start + s // TILE, s % TILE
            pivot = jnp.maximum(spread(column[s, here][at : at + 1]), floor)
            over = 1.0 / pivot
            pivots.append(pivot)
            entry = {
                t: spread(column[s, start + t // TILE][t % TILE : t % TILE + 1])
                if start + t // TILE > here
                else spread(column[t, here][at : at + 1])
                for t in range(s + 1, PANEL)
            }
            left_row, right_row = spread(left[here][at : at + 1]), spread(right[here][at : at + 1])
            for q in tiles:
                if q < here:
                    continue
                ratio = column[s, q] * over
                if q == here:
                    ratio = jnp.where(sub > at, ratio, 0.0)
                for t in range(s + 1, PANEL):
                    if (t, q) in column:
                        column[t, q] = column[t, q] - ratio * entry[t]
                left[q] = left[q] - ratio * left_row
                right[q] = right[q] - ratio * right_row
        for i in range(per):
            own = [pivots[i * TILE + s][s : s + 1] for s in range(TILE)]
            scale[start + i] = lax.rsqrt(jnp.concatenate(own, axis=0))
        rest = start + 2 * per
        if rest < count:
            panel = range(start, start + per)
            u = jnp.concatenate([left[i] * scale[i] for i in panel], axis=0)
            v = jnp.concatenate([right[i] * scale[i] for i in panel], axis=0)
            change = dot(u, jnp.concatenate([u, v], axis=1), CONTRACT, HIGHEST)
            for q in range(rest, count):
                rows = change[TILE * q : TILE * (q + 1)]
                left[q] = left[q] - rows[:, :n]
                right[q] = right[q] - rows[:, n:]
    upper = [jnp.where(lane >= sub + TILE * i, left[i] * scale[i], 0.0) for i in range(count)]
    lower = [right[i] * scale[i] for i in range(count)]
    return jnp.concatenate(upper, axis=0), jnp.concatenate(lower, axis=0)


def store_packed(core, gram, own_ref, other_ref):
    half = gram.shape[0] // 2
    last = gram[half:, half:]
    tail = jnp.concatenate([last[: half // 2], last[half // 2 :]], axis=1)
    packed = jnp.concatenate([gram[:half], tail], axis=0)
    middle = packed.shape[0] // 2
    first, second = packed[:middle], packed[middle:]
    own_ref[...] = jnp.where(core == 0, first, second)
    other_ref[...] = jnp.where(core == 0, second, first)


def load_packed(core, own, other):
    packed = jnp.concatenate(
        [jnp.where(core == 0, own, other), jnp.where(core == 0, other, own)], axis=0
    )
    half = packed.shape[1] // 2
    top, tail = packed[:half], packed[half:]
    last = jnp.concatenate([tail[:, :half], tail[:, half:]], axis=0)
    bottom = jnp.concatenate([jnp.transpose(top[:, half:]), last], axis=1)
    return jnp.concatenate([top, bottom], axis=0)


def floor_of(gram):
    return 1e-9 * jnp.max(gram)


def small_call(kernel, shapes, name, flops, core, *operands):
    memory = pl.BlockSpec(memory_space=pltpu.VMEM)
    return pl.pallas_call(
        kernel,
        in_specs=[pl.BlockSpec(memory_space=pltpu.SMEM)] + [memory] * len(operands),
        out_specs=[memory] * len(shapes),
        out_shape=[jax.ShapeDtypeStruct(shape, jnp.float32) for shape in shapes],
        compiler_params=params(),
        cost_estimate=pl.CostEstimate(
            flops=flops,
            bytes_accessed=4 * sum(operand.size for operand in operands),
            transcendentals=0,
        ),
        name=name,
    )(core, *operands)


def gram_kernel(core_ref, value_ref, own_ref, other_ref):
    value = value_ref[...]
    store_packed(core_ref[0], dot(value, value, CONTRACT, HIGHEST), own_ref, other_ref)


def factor_kernel(core_ref, own_ref, other_ref, upper_ref, lower_ref):
    gram = load_packed(core_ref[0], own_ref[...], other_ref[...])
    upper_ref[...], lower_ref[...] = eliminate(gram, floor_of(gram))


def middle_kernel(core_ref, parts_ref, lower_ref, inner_ref, own_ref, other_ref):
    sketch = parts_ref[0]
    for place in range(1, parts_ref.shape[0]):
        sketch += parts_ref[place]
    inner = dot(sketch, lower_ref[...], TRANSPOSED, HIGHEST)
    inner_ref[...] = inner
    store_packed(core_ref[0], dot(inner, inner, CONTRACT, HIGHEST), own_ref, other_ref)


def last_kernel(
    root_rows, core_ref, own_ref, other_ref, inner_ref, before_ref, basis_ref, factor_ref
):
    gram = load_packed(core_ref[0], own_ref[...], other_ref[...])
    upper, lower = eliminate(gram, floor_of(gram))
    basis_ref[...] = dot(inner_ref[...], lower, TRANSPOSED, HIGHEST) * root_rows
    factor_ref[...] = dot(upper, before_ref[...], precision=HIGHEST) / root_rows


def summed(own, other, stages):
    value = own + swap(other)
    for axes in stages:
        value = jnp.sum(gathered(value, axes), axis=0)
    return value, swap(value)


def local(slab, test_matrix):
    rows, columns = slab.shape
    wide = test_matrix.shape[1]
    zs = lax.axis_size("z")
    row_count = lax.axis_size(ROW)
    row_total = rows * row_count
    root_rows = math.sqrt(row_total)
    core = lax.axis_index("core").astype(jnp.int32).reshape(1)
    far = 1 - core
    slab = slab.reshape(zs, 2, -1, columns)
    square = (wide, wide)
    packed = [(3 * wide // 8, wide)] * 2

    sent = swap(project(slab, test_matrix, far, 2))
    part = project(slab, test_matrix, core, 2) + sent
    own = gathered(jnp.sum(exchange(part, "z"), axis=0), "z")

    other = swap(own)
    part = pull(slab, other, far, pull(slab, own, core))
    piece = jnp.sum(exchange(part.reshape(row_count, -1, wide), ROW), axis=0) / row_total
    pulled = gathered(piece, ROW).reshape(-1, wide)

    halves = small_call(gram_kernel, packed, "gram", 12 * columns * wide**2, core, pulled)
    halves = summed(*halves, ("z",))
    before, lower = small_call(factor_kernel, [square] * 2, "factor", 6 * 10**9, core, *halves)

    sent = swap(project(slab, pulled, far, 3))
    part = project(slab, pulled, core, 3) + sent
    parts = exchange(part, "z")

    inner, *halves = small_call(
        middle_kernel, [(rows // (2 * zs), wide)] + packed, "middle", 10**8, core, parts, lower
    )
    halves = summed(*halves, (ROW, "z"))
    basis, factor = small_call(
        functools.partial(last_kernel, root_rows),
        [inner.shape, square],
        "last",
        6 * 10**9,
        core,
        *halves,
        inner,
        before,
    )
    return basis, factor


def solution(mesh):
    sizes = dict(mesh.shape)
    chips = mesh.devices.reshape(4, sizes["row"] // 4, sizes["col"] // 2, 2)
    fine = Mesh(chips, ("y", "x", "z", "core"))
    col = ("z", "core")
    in_specs = (P(ROW, col), P(col, None))
    out_specs = (P(ROW + col, None), P())
    return jax.shard_map(local, mesh=fine, in_specs=in_specs, out_specs=out_specs, check_vma=False)
```

time: 214 us -> 178 us (0.83)
  other arithmetic: 48.3 us -> 1.05 us
  Pallas kernels: 0 us -> 36 us
  matrix products: 28.3 us -> 0 us
  waiting for transfers between devices: 7.19 us -> 21.5 us
  starting transfers between devices: 24 us -> 17.4 us
  local copies, waits for them, and re-layouts: 6.26 us -> 1.85 us
    another operation x10 -> x0, other arithmetic: 45.8 us -> none  [the longest x6 24.9 us: factor(): lower = jnp.linalg.cholesky(gram)]
    pallas_call x0 -> x10, Pallas kernels: none -> 36 us  [the longest x4 18 us: project(): pl.pallas_call(functools.partial(project_kernel, count), grid_spec=pltpu....]
    dot_general x8 -> x0, matrix products: 27.7 us -> none  [the longest x5 20.4 us: matmul(): jnp.dot(a, b, precision=precision, preferred_element_type=jnp.float32)]
    all_to_all x2, waiting for transfers between devices: 0.01 us -> 17.7 us  [exchange(): return lax.all_to_all(value, axes, 0, 0, tiled=False)]
    ppermute x7, waiting for transfers between devices: 7.18 us -> 3.73 us  [swap(): return lax.ppermute(value, 'core', SWAP)]
    all_to_all x2, starting transfers between devices: 10.2 us -> 6.88 us  [exchange(): return lax.all_to_all(value, axes, 0, 0, tiled=False)]
    ppermute x7, starting transfers between devices: 13.8 us -> 10.6 us  [swap(): return lax.ppermute(value, 'core', SWAP)]
  transfers between devices with their start and end apart: 9 -> 9, of which waited for: 6 -> 6; matrix products, arithmetic and copies ran while one was open for 18% -> 1% of each run, Pallas kernels for 0% -> 10%
where the time goes in v2:
time: 178 us; the launch traced here: 177 us
  blocking collectives  98.7 us (55%)
  Pallas kernels  36 us (20%)
  waiting for transfers between devices  21.5 us (12%)
  starting transfers between devices  17.4 us (10%)
  local copies, waits for them, and re-layouts  1.85 us (1%)
    all_to_all x6, blocking collectives, exchange(): return lax.all_to_all(value, axes, 0, 0, tiled=False)  98.7 us
    pallas_call x4, Pallas kernels, project(): pl.pallas_call(functools.partial(project_kernel, count), grid_spec=pltpu....  18 us
    all_to_all x2, waiting for transfers between devices, exchange(): return lax.all_to_all(value, axes, 0, 0, tiled=False)  17.7 us
    ppermute x7, starting transfers between devices, swap(): return lax.ppermute(value, 'core', SWAP)  10.6 us
    pallas_call x4, Pallas kernels, small_call(): pl.pallas_call(kernel, in_specs=[pl.BlockSpec(memory_space=pltpu.SMEM)] +...  9.66 us
    pallas_call x2, Pallas kernels, pull(): pl.pallas_call(functools.partial(pull_kernel, more), grid_spec=pltpu.Pref...  8.32 us
    all_to_all x2, starting transfers between devices, exchange(): return lax.all_to_all(value, axes, 0, 0, tiled=False)  6.88 us
    ppermute x7, waiting for transfers between devices, swap(): return lax.ppermute(value, 'core', SWAP)  3.73 us
  transfers between devices with their start and end apart: 9, of which 6 were waited for; matrix products, arithmetic and copies ran while one was open for 1% of the time, Pallas kernels for 10%

profile of v2, /device:TPU:1, one launch (start us, length us, event | category | flops | bytes accessed | tf_op | source)
XLA Modules:
  0.0 177.2 jit_solution(10710856927149123753)
XLA Ops:
  0.6 1.0 copy-done
  1.7 4.1 %project2.3 = f32[8,128,128]{2,1,0:T(8,128)S(1)} custom-call(s32[1]{0:T(128)S(6)} %sub.3.half_ref, f32[8,2,128,1024]{3,2,1,0:T(8,128)} %bitcast.8, f32[1024,128]{1,0:T(8,128)S(1)} %copy-done), custom_call_target="tpu_custom_call" | custom-call | flops 1073741824 | bytes 4194304 | tf_op jit(solution)/shard_map/project2/pallas_call | solution.py:76
  5.7 3.3 %collective-permute-start = (f32[8,128,128]{2,1,0:T(8,128)S(1)}, f32[8,128,128]{2,1,0:T(8,128)S(1)}, u32[]{:S(2)}, u32[]{:S(2)}) collective-permute-start(f32[8,128,128]{2,1,0:T(8,128)S(1)} %project2.3), channel_id=1, source_target_pairs={{0,1},{1,0},{2,3},{3,2},{4,5},{5,4},{6,7},{7,6},{8,9},{9,8},{10,11... | collective-permute-start | bytes 1572872 | tf_op jit(solution)/shard_map/ppermute | solution.py:24
  9.1 4.0 %project2.2 = f32[8,128,128]{2,1,0:T(8,128)S(1)} custom-call(s32[1]{0:T(128)} %bitcast.half_ref.core_ref, f32[8,2,128,1024]{3,2,1,0:T(8,128)} %bitcast.9, f32[1024,128]{1,0:T(8,128)S(1)} %copy-done.1), custom_call_target="tpu_custom_call" | custom-call | flops 1073741824 | bytes 4194304 | tf_op jit(solution)/shard_map/project2/pallas_call | solution.py:76
  13.1 24.2 %all_to_all.40 = f32[8,128,128]{2,1,0:T(8,128)S(1)} all-to-all(f32[8,128,128]{2,1,0:T(8,128)S(1)} %add.12), channel_id=1, replica_groups=mesh['y'=4,'x'=4,'z'=8,'core'=2] {'z'}, dimensions={0} | all-to-all | bytes 1048576 | tf_op jit(solution)/shard_map/all_to_all | solution.py:28
  37.5 20.3 %all_to_all.41.left_ref = f32[8,128,128]{2,1,0:T(8,128)S(1)} all-to-all(f32[8,128,128]{2,1,0:T(8,128)S(1)} %broadcast_in_dim.15), channel_id=1, replica_groups=mesh['y'=4,'x'=4,'z'=8,'core'=2] {'z'}, dimensions={0} | all-to-all | bytes 1048576 | tf_op jit(solution)/shard_map/all_to_all | solution.py:28
  57.7 0.6 collective-permute-start.1
  58.3 4.1 %pull.2.refs_0_ = f32[1024,128]{1,0:T(8,128)S(1)} custom-call(s32[1]{0:T(128)} %bitcast.half_ref.core_ref, f32[8,2,128,1024]{3,2,1,0:T(8,128)} %bitcast.10, f32[8,128,128]{2,1,0:T(8,128)S(1)} %all_to_all.41.left_ref), custom_call_target="tpu_custom_call" | custom-call | flops 1073741824 | bytes 4194304 | tf_op jit(solution)/shard_map/pull/pallas_call | solution.py:129
  62.5 4.2 %pull.3 = f32[1024,128]{1,0:T(8,128)S(1)} custom-call(s32[1]{0:T(128)S(6)} %sub.3.half_ref, f32[8,2,128,1024]{3,2,1,0:T(8,128)} %bitcast.11, f32[8,128,128]{2,1,0:T(8,128)S(1)} %collective-permute-done.1.left_ref, f32[1024,128]{1,0:T(8,128)S(1)} %pull.2.refs_0_), custom_call_target="tpu_custom_call" | custom-call | flops 1073741824 | bytes 4194304 | tf_op jit(solution)/shard_map/pull/pallas_call | solution.py:129
  66.7 17.6 %all_to_all.42 = f32[16,64,128]{2,1,0:T(8,128)S(1)} all-to-all(f32[16,64,128]{2,1,0:T(8,128)S(1)} %bitcast.7), channel_id=1, replica_groups=mesh['y'=4,'x'=4,'z'=8,'core'=2] {'y','x'}, dimensions={0} | all-to-all | bytes 1048576 | tf_op jit(solution)/shard_map/all_to_all | solution.py:28
  84.4 13.4 %all_to_all.43 = f32[16,64,128]{2,1,0:T(8,128)S(1)} all-to-all(f32[16,64,128]{2,1,0:T(8,128)S(1)} %broadcast_in_dim.16), channel_id=1, replica_groups=mesh['y'=4,'x'=4,'z'=8,'core'=2] {'y','x'}, dimensions={0} | all-to-all | bytes 1048576 | tf_op jit(solution)/shard_map/all_to_all | solution.py:28
  97.8 4.9 %project3.3 = f32[8,128,128]{2,1,0:T(8,128)S(1)} custom-call(s32[1]{0:T(128)S(6)} %sub.3.half_ref, f32[8,2,128,1024]{3,2,1,0:T(8,128)} %bitcast.12, f32[1024,128]{1,0:T(8,128)S(1)} %bitcast.4), custom_call_target="tpu_custom_call" | custom-call | flops 2147483648 | bytes 4194304 | tf_op jit(solution)/shard_map/project3/pallas_call | solution.py:76
  102.8 2.2 %collective-permute-start.2 = (f32[8,128,128]{2,1,0:T(8,128)S(1)}, f32[8,128,128]{2,1,0:T(8,128)S(1)}, u32[]{:S(2)}, u32[]{:S(2)}) collective-permute-start(f32[8,128,128]{2,1,0:T(8,128)S(1)} %project3.3), channel_id=1, source_target_pairs={{0,1},{1,0},{2,3},{3,2},{4,5},{5,4},{6,7},{7,6},{8,9},{9,8},{10,11... | collective-permute-start | bytes 1572872 | tf_op jit(solution)/shard_map/ppermute | solution.py:24
  105.0 0.7 gram.1
  105.8 1.2 collective-permute-done.3
  107.0 0.7 broadcast_in_dim.17
  107.7 3.4 %all-to-all-start.5 = ((f32[8,48,128]{2,1,0:T(8,128)}), f32[8,48,128]{2,1,0:T(8,128)S(1)}, u32[]{:S(2)}, u32[]{:S(2)}) async-start(f32[8,48,128]{2,1,0:T(8,128)} %broadcast_in_dim.17), calls=%async_computation.5 | async-start | bytes 393216 | tf_op jit(solution)/shard_map/all_to_all | solution.py:28
  111.1 5.0 %project3.2 = f32[8,128,128]{2,1,0:T(8,128)S(1)} custom-call(s32[1]{0:T(128)} %bitcast.half_ref.core_ref, f32[8,2,128,1024]{3,2,1,0:T(8,128)} %bitcast.13, f32[1024,128]{1,0:T(8,128)S(1)} %bitcast.6), custom_call_target="tpu_custom_call" | custom-call | flops 2147483648 | bytes 4194304 | tf_op jit(solution)/shard_map/project3/pallas_call | solution.py:76
  116.1 0.9 add.13
  116.9 5.0 %all-to-all-done.5 = f32[8,48,128]{2,1,0:T(8,128)S(1)} async-done(((f32[8,48,128]{2,1,0:T(8,128)}), f32[8,48,128]{2,1,0:T(8,128)S(1)}, u32[]{:S(2)}, u32[]{:S(2)}) %all-to-all-start.5) | async-done | bytes 196640 | tf_op jit(solution)/shard_map/all_to_all | solution.py:28
  121.9 3.5 %all-to-all-start.4 = ((f32[8,128,128]{2,1,0:T(8,128)}), f32[8,128,128]{2,1,0:T(8,128)S(1)}, u32[]{:S(2)}, u32[]{:S(2)}) async-start(f32[8,128,128]{2,1,0:T(8,128)} %add.13), calls=%async_computation.4 | async-start | bytes 1048576 | tf_op jit(solution)/shard_map/all_to_all | solution.py:28
  126.0 0.8 collective-permute-done.4.other_ref
  126.9 3.7 %factor.1 = (f32[128,128]{1,0:T(8,128)S(1)}, f32[128,128]{1,0:T(8,128)S(1)}) custom-call(s32[1]{0:T(128)} %bitcast.half_ref.core_ref, f32[48,128]{1,0:T(8,128)S(1)} %reduce_sum.47.own_ref, f32[48,128]{1,0:T(8,128)S(1)} %collective-permute-done.4.other_ref), custom_call_target="tpu_custom_call" | custom-call | flops 6000000000 | bytes 49152 | tf_op jit(solution)/shard_map/factor/pallas_call | solution.py:244
  130.6 12.7 %all-to-all-done.4.parts_ref = f32[8,128,128]{2,1,0:T(8,128)S(1)} async-done(((f32[8,128,128]{2,1,0:T(8,128)}), f32[8,128,128]{2,1,0:T(8,128)S(1)}, u32[]{:S(2)}, u32[]{:S(2)}) %all-to-all-start.4) | async-done | bytes 524320 | tf_op jit(solution)/shard_map/all_to_all | solution.py:28
  143.3 0.6 middle.1
  143.9 0.7 collective-permute-start.5
  144.7 0.8 collective-permute-done.5
  145.6 12.2 %all_to_all.44 = f32[16,48,128]{2,1,0:T(8,128)S(1)} all-to-all(f32[16,48,128]{2,1,0:T(8,128)S(1)} %broadcast_in_dim.18), channel_id=1, replica_groups=mesh['y'=4,'x'=4,'z'=8,'core'=2] {'y','x'}, dimensions={0} | all-to-all | bytes 786432 | tf_op jit(solution)/shard_map/all_to_all | solution.py:28
  157.8 10.9 %all_to_all.45 = f32[8,48,128]{2,1,0:T(8,128)S(1)} all-to-all(f32[8,48,128]{2,1,0:T(8,128)S(1)} %broadcast_in_dim.19), channel_id=1, replica_groups=mesh['y'=4,'x'=4,'z'=8,'core'=2] {'z'}, dimensions={0} | all-to-all | bytes 393216 | tf_op jit(solution)/shard_map/all_to_all | solution.py:28
  168.7 3.1 %collective-permute-start.6 = (f32[48,128]{1,0:T(8,128)S(1)}, f32[48,128]{1,0:T(8,128)S(1)}, u32[]{:S(2)}, u32[]{:S(2)}) collective-permute-start(f32[48,128]{1,0:T(8,128)S(1)} %reduce_sum.49.own_ref), channel_id=1, source_target_pairs={{0,1},{1,0},{2,3},{3,2},{4,5},{5,4},{6,7},{7,6},{8,9},{9,8},{10,11... | collective-permute-start | bytes 73736 | tf_op jit(solution)/shard_map/ppermute | solution.py:24
  171.8 0.8 collective-permute-done.6.other_ref
  172.6 4.6 %last.1 = (f32[128,128]{1,0:T(8,128)}, f32[128,128]{1,0:T(8,128)}) custom-call(s32[1]{0:T(128)} %bitcast.half_ref.core_ref, f32[48,128]{1,0:T(8,128)S(1)} %reduce_sum.49.own_ref, f32[48,128]{1,0:T(8,128)S(1)} %collective-permute-done.6.other_ref, f32[128,128]{1,0:T(8,128)S(1)} %get-tuple-element.14.inner_ref, f32[128,128]{1,0:T(8,128)S(1)} %get-tuple-element.15.before_ref), custom_call_target="tpu_custom_call" | custom-call | flops 6000000000 | bytes 180224 | tf_op jit(solution)/shard_map/last/pallas_call | solution.py:244
  (21 shorter events, 1.0 us)
Async XLA Ops:
  0.6 1.0 copy-start
  1.7 7.4 %copy-start.1 = (f32[1024,128]{1,0:T(8,128)S(1)}, f32[1024,128]{1,0:T(8,128)}, u32[]{:S(2)}) copy-start(f32[1024,128]{1,0:T(8,128)} %right_ref.3) | copy-start | bytes 1572868
  5.7 7.3 %collective-permute-start = (f32[8,128,128]{2,1,0:T(8,128)S(1)}, f32[8,128,128]{2,1,0:T(8,128)S(1)}, u32[]{:S(2)}, u32[]{:S(2)}) collective-permute-start(f32[8,128,128]{2,1,0:T(8,128)S(1)} %project2.3), channel_id=1, source_target_pairs={{0,1},{1,0},{2,3},{3,2},{4,5},{5,4},{6,7},{7,6},{8,9},{9,8},{10,11... | collective-permute-start | bytes 1572872 | tf_op jit(solution)/shard_map/ppermute | solution.py:24
  57.7 4.7 %collective-permute-start.1 = (f32[8,128,128]{2,1,0:T(8,128)S(1)}, f32[8,128,128]{2,1,0:T(8,128)S(1)}, u32[]{:S(2)}, u32[]{:S(2)}) collective-permute-start(f32[8,128,128]{2,1,0:T(8,128)S(1)} %all_to_all.41.left_ref), channel_id=1, source_target_pairs={{0,1},{1,0},{2,3},{3,2},{4,5},{5,4},{6,7},{7,6},{8,9},{9,8},{10,11... | collective-permute-start | bytes 1572872 | tf_op jit(solution)/shard_map/ppermute | solution.py:24
  102.8 13.3 %collective-permute-start.2 = (f32[8,128,128]{2,1,0:T(8,128)S(1)}, f32[8,128,128]{2,1,0:T(8,128)S(1)}, u32[]{:S(2)}, u32[]{:S(2)}) collective-permute-start(f32[8,128,128]{2,1,0:T(8,128)S(1)} %project3.3), channel_id=1, source_target_pairs={{0,1},{1,0},{2,3},{3,2},{4,5},{5,4},{6,7},{7,6},{8,9},{9,8},{10,11... | collective-permute-start | bytes 1572872 | tf_op jit(solution)/shard_map/ppermute | solution.py:24
  105.7 1.3 collective-permute-start.3
  107.7 14.3 %all-to-all-start.5 = ((f32[8,48,128]{2,1,0:T(8,128)}), f32[8,48,128]{2,1,0:T(8,128)S(1)}, u32[]{:S(2)}, u32[]{:S(2)}) async-start(f32[8,48,128]{2,1,0:T(8,128)} %broadcast_in_dim.17), calls=%async_computation.5 | async-start | bytes 393216 | tf_op jit(solution)/shard_map/all_to_all | solution.py:28
  121.9 21.4 %all-to-all-start.4 = ((f32[8,128,128]{2,1,0:T(8,128)}), f32[8,128,128]{2,1,0:T(8,128)S(1)}, u32[]{:S(2)}, u32[]{:S(2)}) async-start(f32[8,128,128]{2,1,0:T(8,128)} %add.13), calls=%async_computation.4 | async-start | bytes 1048576 | tf_op jit(solution)/shard_map/all_to_all | solution.py:28
  125.4 1.4 collective-permute-start.4
  143.9 1.6 collective-permute-start.5
  168.7 3.9 %collective-permute-start.6 = (f32[48,128]{1,0:T(8,128)S(1)}, f32[48,128]{1,0:T(8,128)S(1)}, u32[]{:S(2)}, u32[]{:S(2)}) collective-permute-start(f32[48,128]{1,0:T(8,128)S(1)} %reduce_sum.49.own_ref), channel_id=1, source_target_pairs={{0,1},{1,0},{2,3},{3,2},{4,5},{5,4},{6,7},{7,6},{8,9},{9,8},{10,11... | collective-permute-start | bytes 73736 | tf_op jit(solution)/shard_map/ppermute | solution.py:24

commit v3 on v2

--- a/solution.py
+++ b/solution.py
@@ -17,7 +17,10 @@
 TILE = 8
 PANEL = 16
 STEP = 2
-VMEM = 48 * 1024 * 1024
+PULL = 8
+COUNT = 3
+VMEM = 12 * 1024 * 1024
+LOAD_VMEM = 46 * 1024 * 1024
 
 
 def swap(value):
@@ -45,109 +48,128 @@
     return parts
 
 
-def params():
-    return pltpu.CompilerParams(vmem_limit_bytes=VMEM)
-
-
-def project_kernel(count, half_ref, slab_ref, right_ref, out_ref, parts_ref):
-    wide = right_ref.shape[1]
-
-    @pl.when(pl.program_id(0) == 0)
-    def _():
-        for place, part in enumerate(split(right_ref[...], count)):
-            parts_ref[:, place * wide : (place + 1) * wide] = part
-
-    block = slab_ref[...].reshape(-1, slab_ref.shape[-1])
-    parts = split(block, count)
-    pair = parts_ref[:, : 2 * wide]
-    first = dot(parts[0], pair)
-    if count == 2:
-        small = first[:, wide:] + dot(parts[1], parts_ref[:, :wide])
-    else:
-        second = dot(parts[1], pair)
-        third = dot(parts[0], parts_ref[:, 2 * wide :]) + dot(parts[2], parts_ref[:, :wide])
-        small = (first[:, wide:] + second[:, :wide]) + (second[:, wide:] + third)
-    out_ref[...] = (first[:, :wide] + small).reshape(out_ref.shape)
-
-
-def project(slab, right, half, count):
+def params(limit=VMEM):
+    return pltpu.CompilerParams(vmem_limit_bytes=limit)
+
+
+def rows_of(ref, place, height):
+    return ref[place : place + height].reshape(-1, ref.shape[-1])
+
+
+def load_kernel(half_ref, slab_ref, right_ref, out_ref, *refs):
+    part_refs, (pair_ref, block_ref, right_buffer, sems) = refs[:COUNT], refs[COUNT:]
+    half, zs, wide = half_ref[0], block_ref.shape[0], out_ref.shape[-1]
+    right_copy = pltpu.make_async_copy(right_ref, right_buffer, sems.at[zs])
+    right_copy.start()
+    copies = [
+        pltpu.make_async_copy(slab_ref.at[place, half], block_ref.at[place], sems.at[place])
+        for place in range(zs)
+    ]
+    for copy in copies:
+        copy.start()
+    right_copy.wait()
+    high, low = split(right_buffer[...], 2)
+    pair_ref[:, :wide] = high
+    pair_ref[:, wide:] = low
+    for place in range(0, zs, STEP):
+        for copy in copies[place : place + STEP]:
+            copy.wait()
+        parts = split(rows_of(block_ref, place, STEP), COUNT)
+        for part, ref in zip(parts, part_refs):
+            ref[place : place + STEP] = part.reshape(STEP, -1, ref.shape[-1])
+        first = dot(parts[0], pair_ref[...])
+        value = first[:, :wide] + (first[:, wide:] + dot(parts[1], pair_ref[:, :wide]))
+        out_ref[place : place + STEP] = value.reshape(STEP, -1, wide)
+
+
+def load(slab, right, half):
     zs, _, height, depth = slab.shape
     wide = right.shape[1]
+    memory = pl.BlockSpec(memory_space=pltpu.VMEM)
+    anywhere = pl.BlockSpec(memory_space=pl.ANY)
+    part = jax.ShapeDtypeStruct((zs, height, depth), jnp.bfloat16)
+    product, *parts = pl.pallas_call(
+        load_kernel,
+        in_specs=[pl.BlockSpec(memory_space=pltpu.SMEM), anywhere, anywhere],
+        out_specs=[memory] * (1 + COUNT),
+        scratch_shapes=[
+            pltpu.VMEM((depth, 2 * wide), jnp.bfloat16),
+            pltpu.VMEM((zs, height, depth), jnp.float32),
+            pltpu.VMEM((depth, wide), jnp.float32),
+            pltpu.SemaphoreType.DMA((zs + 1,)),
+        ],
+        out_shape=[jax.ShapeDtypeStruct((zs, height, wide), jnp.float32)] + [part] * COUNT,
+        compiler_params=params(LOAD_VMEM),
+        cost_estimate=cost(zs * height, depth, wide, 4),
+        name="load",
+    )(half, slab, right)
+    return product, parts
+
+
+def cost(height, depth, wide, times):
+    return pl.CostEstimate(
+        flops=2 * height * depth * wide * times,
+        bytes_accessed=4 * height * depth,
+        transcendentals=0,
+    )
+
+
+def project_kernel(right_ref, high_ref, middle_ref, low_ref, out_ref):
+    wide = right_ref.shape[1]
+    parts = split(right_ref[...], COUNT)
+    pair = jnp.concatenate(parts[:2], axis=1)
+    for place in range(0, out_ref.shape[0], STEP):
+        high, middle = rows_of(high_ref, place, STEP), rows_of(middle_ref, place, STEP)
+        first, second = dot(high, pair), dot(middle, pair)
+        third = dot(high, parts[2]) + dot(rows_of(low_ref, place, STEP), parts[0])
+        small = (first[:, wide:] + second[:, :wide]) + (second[:, wide:] + third)
+        out_ref[place : place + STEP] = (first[:, :wide] + small).reshape(STEP, -1, wide)
+
+
+def project(right, parts):
+    zs, height, depth = parts[0].shape
+    wide = right.shape[1]
+    memory = pl.BlockSpec(memory_space=pltpu.VMEM)
     return pl.pallas_call(
-        functools.partial(project_kernel, count),
-        grid_spec=pltpu.PrefetchScalarGridSpec(
-            num_scalar_prefetch=1,
-            grid=(zs // STEP,),
-            in_specs=[
-                pl.BlockSpec((STEP, 1, height, depth), lambda i, half: (i, half[0], 0, 0)),
-                pl.BlockSpec((depth, wide), lambda i, half: (0, 0)),
-            ],
-            out_specs=pl.BlockSpec((STEP, height, wide), lambda i, half: (i, 0, 0)),
-            scratch_shapes=[pltpu.VMEM((depth, count * wide), jnp.bfloat16)],
-        ),
+        project_kernel,
+        in_specs=[memory] * (1 + COUNT),
+        out_specs=memory,
         out_shape=jax.ShapeDtypeStruct((zs, height, wide), jnp.float32),
         compiler_params=params(),
-        cost_estimate=pl.CostEstimate(
-            flops=2 * zs * height * depth * wide * (4 if count == 2 else 8),
-            bytes_accessed=4 * zs * height * depth,
-            transcendentals=0,
-        ),
-        name="project%d" % count,
-    )(half, slab, right)
-
-
-def pull_kernel(more, half_ref, slab_ref, left_ref, *refs):
-    out_ref, total_ref = refs[-2:]
-    step = pl.program_id(0)
-    wide = left_ref.shape[-1]
-    block = slab_ref[...].reshape(-1, slab_ref.shape[-1])
-    high, low = split(block, 2)
-    left = jnp.concatenate(split(left_ref[...].reshape(-1, wide), 2), axis=1)
-    left = jnp.transpose(left.astype(jnp.float32)).astype(jnp.bfloat16)
-    both = dot(left, high)
-    value = both[:wide] + (both[wide:] + dot(left[:wide], low))
-
-    @pl.when(step == 0)
-    def _():
-        total_ref[...] = value
-
-    @pl.when(step > 0)
-    def _():
-        total_ref[...] += value
-
-    @pl.when(step == pl.num_programs(0) - 1)
-    def _():
-        result = jnp.transpose(total_ref[...])
-        out_ref[...] = result + refs[0][...] if more else result
-
-
-def pull(slab, left, half, before=None):
-    zs, _, height, depth = slab.shape
+        cost_estimate=cost(zs * height, depth, wide, 8),
+        name="project",
+    )(right, *parts)
+
+
+def pull_kernel(more, left_ref, high_ref, low_ref, *refs):
+    out_ref = refs[-1]
+    zs, wide = left_ref.shape[0], left_ref.shape[-1]
+    total = None
+    for place in range(0, zs, PULL):
+        left = jnp.transpose(rows_of(left_ref, place, PULL))
+        high, low = split(left, 2)
+        block = rows_of(high_ref, place, PULL)
+        both = dot(jnp.concatenate([high, low], axis=0), block)
+        value = both[:wide] + (both[wide:] + dot(high, rows_of(low_ref, place, PULL)))
+        total = value if total is None else total + value
+    result = jnp.transpose(total)
+    out_ref[...] = result + refs[0][...] if more else result
+
+
+def pull(left, parts, before=None):
+    zs, height, depth = parts[0].shape
     wide = left.shape[-1]
-    flat = pl.BlockSpec((depth, wide), lambda i, half: (0, 0))
+    memory = pl.BlockSpec(memory_space=pltpu.VMEM)
     more = before is not None
     return pl.pallas_call(
         functools.partial(pull_kernel, more),
-        grid_spec=pltpu.PrefetchScalarGridSpec(
-            num_scalar_prefetch=1,
-            grid=(zs // STEP,),
-            in_specs=[
-                pl.BlockSpec((STEP, 1, height, depth), lambda i, half: (i, half[0], 0, 0)),
-                pl.BlockSpec((STEP, height, wide), lambda i, half: (i, 0, 0)),
-            ]
-            + [flat] * more,
-            out_specs=flat,
-            scratch_shapes=[pltpu.VMEM((wide, depth), jnp.float32)],
-        ),
+        in_specs=[memory] * (3 + more),
+        out_specs=memory,
         out_shape=jax.ShapeDtypeStruct((depth, wide), jnp.float32),
         compiler_params=params(),
-        cost_estimate=pl.CostEstimate(
-            flops=2 * zs * height * depth * wide * 4,
-            bytes_accessed=4 * zs * height * depth,
-            transcendentals=0,
-        ),
+        cost_estimate=cost(zs * height, depth, wide, 4),
         name="pull",
-    )(half, slab, left, *([before] if more else []))
+    )(left, *parts[:2], *([before] if more else []))
 
 
 def spread(row):
@@ -304,12 +326,14 @@
     square = (wide, wide)
     packed = [(3 * wide // 8, wide)] * 2
 
-    sent = swap(project(slab, test_matrix, far, 2))
-    part = project(slab, test_matrix, core, 2) + sent
+    product, far_parts = load(slab, test_matrix, far)
+    sent = swap(product)
+    product, parts = load(slab, test_matrix, core)
+    part = product + sent
     own = gathered(jnp.sum(exchange(part, "z"), axis=0), "z")
 
     other = swap(own)
-    part = pull(slab, other, far, pull(slab, own, core))
+    part = pull(other, far_parts, pull(own, parts))
     piece = jnp.sum(exchange(part.reshape(row_count, -1, wide), ROW), axis=0) / row_total
     pulled = gathered(piece, ROW).reshape(-1, wide)
 
@@ -317,12 +341,12 @@
     halves = summed(*halves, ("z",))
     before, lower = small_call(factor_kernel, [square] * 2, "factor", 6 * 10**9, core, *halves)
 
-    sent = swap(project(slab, pulled, far, 3))
-    part = project(slab, pulled, core, 3) + sent
-    parts = exchange(part, "z")
+    sent = swap(project(pulled, far_parts))
+    part = project(pulled, parts) + sent
+    pieces = exchange(part, "z")
 
     inner, *halves = small_call(
-        middle_kernel, [(rows // (2 * zs), wide)] + packed, "middle", 10**8, core, parts, lower
+        middle_kernel, [(rows // (2 * zs), wide)] + packed, "middle", 10**8, core, pieces, lower
     )
     halves = summed(*halves, (ROW, "z"))
     basis, factor = small_call(

time: 178 us -> 178 us (level)
  local copies, waits for them, and re-layouts: 1.85 us -> 17.8 us
  Pallas kernels: 36 us -> 22.9 us
  blocking collectives: 98.7 us -> 93.3 us
  starting transfers between devices: 17.4 us -> 21.1 us
  waiting for transfers between devices: 21.5 us -> 19.1 us
    unnamed x4 -> x30, local copies, waits for them, and re-layouts: 1.04 us -> 17 us
    pallas_call x6, Pallas kernels: 26.3 us -> 13.3 us  [the longest x2 6.32 us: load(): pl.pallas_call(load_kernel, in_specs=[pl.BlockSpec(memory_space=pltpu.SME...]
    all_to_all x6, blocking collectives: 98.7 us -> 93.3 us  [exchange(): return lax.all_to_all(value, axes, 0, 0, tiled=False)]
    ppermute x7, starting transfers between devices: 10.6 us -> 14 us  [swap(): return lax.ppermute(value, 'core', SWAP)]
    all_to_all x2, waiting for transfers between devices: 17.7 us -> 15.4 us  [exchange(): return lax.all_to_all(value, axes, 0, 0, tiled=False)]
  transfers between devices with their start and end apart: 9 -> 9, of which waited for: 6 -> 6; matrix products, arithmetic and copies ran while one was open for 1% -> 1% of each run, Pallas kernels for 10% -> 6%
where the time goes in v3:
time: 178 us; the launch traced here: 177 us
  blocking collectives  93.3 us (52%)
  Pallas kernels  22.9 us (13%)
  starting transfers between devices  21.1 us (12%)
  waiting for transfers between devices  19.1 us (11%)
  local copies, waits for them, and re-layouts  17.8 us (10%)
  other arithmetic  2.09 us (1%)
    all_to_all x6, blocking collectives, exchange(): return lax.all_to_all(value, axes, 0, 0, tiled=False)  93.3 us
    unnamed x30, local copies, waits for them, and re-layouts  17 us
    all_to_all x2, waiting for transfers between devices, exchange(): return lax.all_to_all(value, axes, 0, 0, tiled=False)  15.4 us
    ppermute x7, starting transfers between devices, swap(): return lax.ppermute(value, 'core', SWAP)  14 us
    pallas_call x4, Pallas kernels, small_call(): pl.pallas_call(kernel, in_specs=[pl.BlockSpec(memory_space=pltpu.SMEM)] +...  9.66 us
    all_to_all x2, starting transfers between devices, exchange(): return lax.all_to_all(value, axes, 0, 0, tiled=False)  7.06 us
    pallas_call x2, Pallas kernels, load(): pl.pallas_call(load_kernel, in_specs=[pl.BlockSpec(memory_space=pltpu.SME...  6.32 us
    pallas_call x2, Pallas kernels, project(): pl.pallas_call(project_kernel, in_specs=[memory] * (1 + COUNT), out_specs...  4.71 us
  transfers between devices with their start and end apart: 9, of which 6 were waited for; matrix products, arithmetic and copies ran while one was open for 1% of the time, Pallas kernels for 6%

profile of v3, /device:TPU:1, one launch (start us, length us, event | category | flops | bytes accessed | tf_op | source)
XLA Modules:
  0.0 177.2 jit_solution(7088086388835682476)
XLA Ops:
  1.7 3.2 %load.3 = (f32[8,128,128]{2,1,0:T(8,128)S(1)}, bf16[8,128,1024]{2,1,0:T(8,128)(2,1)S(1)}, bf16[8,128,1024]{2,1,0:T(8,128)(2,1)S(1)}, bf16[8,128,1024]{2,1,0:T(8,128)(2,1)S(1)}) custom-call(s32[1]{0:T(128)S(6)} %sub.3.half_ref, f32[8,2,128,1024]{3,2,1,0:T(8,128)} %bitcast.8, f32[1024,128]{1,0:T(8,128)S(1)} %copy-done), custom_call_target="tpu_custom_call" | custom-call | flops 1073741824 | bytes 4194304 | tf_op jit(solution)/shard_map/load/pallas_call | solution.py:91
  4.9 1.3 copy-done.5
  6.3 1.4 copy-done.13
  7.6 3.2 %collective-permute-start = (f32[8,128,128]{2,1,0:T(8,128)S(1)}, f32[8,128,128]{2,1,0:T(8,128)S(1)}, u32[]{:S(2)}, u32[]{:S(2)}) collective-permute-start(f32[8,128,128]{2,1,0:T(8,128)S(1)} %get-tuple-element.18), channel_id=1, source_target_pairs={{0,1},{1,0},{2,3},{3,2},{4,5},{5,4},{6,7},{7,6},{8,9},{9,8},{10,11... | collective-permute-start | bytes 1572872 | tf_op jit(solution)/shard_map/ppermute | solution.py:27
  10.9 3.1 %load.2 = (f32[8,128,128]{2,1,0:T(8,128)S(1)}, bf16[8,128,1024]{2,1,0:T(8,128)(2,1)S(1)}, bf16[8,128,1024]{2,1,0:T(8,128)(2,1)S(1)}, bf16[8,128,1024]{2,1,0:T(8,128)(2,1)S(1)}) custom-call(s32[1]{0:T(128)} %bitcast.half_ref.core_ref, f32[8,2,128,1024]{3,2,1,0:T(8,128)} %bitcast.9, f32[1024,128]{1,0:T(8,128)S(1)} %copy-done.1), custom_call_target="tpu_custom_call" | custom-call | flops 1073741824 | bytes 4194304 | tf_op jit(solution)/shard_map/load/pallas_call | solution.py:91
  14.0 1.3 copy-done.2
  15.3 1.3 copy-done.11
  16.7 22.1 %all_to_all.40 = f32[8,128,128]{2,1,0:T(8,128)S(1)} all-to-all(f32[8,128,128]{2,1,0:T(8,128)S(1)} %add.12), channel_id=1, replica_groups=mesh['y'=4,'x'=4,'z'=8,'core'=2] {'z'}, dimensions={0} | all-to-all | bytes 1048576 | tf_op jit(solution)/shard_map/all_to_all | solution.py:31
  38.9 17.0 %all_to_all.41.left_ref = f32[8,128,128]{2,1,0:T(8,128)S(1)} all-to-all(f32[8,128,128]{2,1,0:T(8,128)S(1)} %broadcast_in_dim.15), channel_id=1, replica_groups=mesh['y'=4,'x'=4,'z'=8,'core'=2] {'z'}, dimensions={0} | all-to-all | bytes 1048576 | tf_op jit(solution)/shard_map/all_to_all | solution.py:31
  55.9 4.0 %collective-permute-start.1 = (f32[8,128,128]{2,1,0:T(8,128)S(1)}, f32[8,128,128]{2,1,0:T(8,128)S(1)}, u32[]{:S(2)}, u32[]{:S(2)}) collective-permute-start(f32[8,128,128]{2,1,0:T(8,128)S(1)} %all_to_all.41.left_ref), channel_id=1, source_target_pairs={{0,1},{1,0},{2,3},{3,2},{4,5},{5,4},{6,7},{7,6},{8,9},{9,8},{10,11... | collective-permute-start | bytes 1572872 | tf_op jit(solution)/shard_map/ppermute | solution.py:27
  59.9 1.6 copy-done.3
  64.9 17.6 %all_to_all.42 = f32[16,64,128]{2,1,0:T(8,128)S(1)} all-to-all(f32[16,64,128]{2,1,0:T(8,128)S(1)} %bitcast.4), channel_id=1, replica_groups=mesh['y'=4,'x'=4,'z'=8,'core'=2] {'y','x'}, dimensions={0} | all-to-all | bytes 1048576 | tf_op jit(solution)/shard_map/all_to_all | solution.py:31
  82.6 13.4 %all_to_all.43 = f32[16,64,128]{2,1,0:T(8,128)S(1)} all-to-all(f32[16,64,128]{2,1,0:T(8,128)S(1)} %broadcast_in_dim.16), channel_id=1, replica_groups=mesh['y'=4,'x'=4,'z'=8,'core'=2] {'y','x'}, dimensions={0} | all-to-all | bytes 1048576 | tf_op jit(solution)/shard_map/all_to_all | solution.py:31
  96.0 1.6 copy-done.7
  97.6 1.6 copy-done.10
  99.2 1.6 copy-done.14
  100.8 2.4 %project.3 = f32[8,128,128]{2,1,0:T(8,128)S(1)} custom-call(f32[1024,128]{1,0:T(8,128)S(1)} %bitcast.5, bf16[8,128,1024]{2,1,0:T(8,128)(2,1)S(1)} %copy-done.7, bf16[8,128,1024]{2,1,0:T(8,128)(2,1)S(1)} %copy-done.10, bf16[8,128,1024]{2,1,0:T(8,128)(2,1)S(1)} %copy-done.14), custom_call_target="tpu_custom_call" | custom-call | flops 2147483648 | bytes 4194304 | tf_op jit(solution)/shard_map/project/pallas_call | solution.py:133
  103.2 2.2 %collective-permute-start.2 = (f32[8,128,128]{2,1,0:T(8,128)S(1)}, f32[8,128,128]{2,1,0:T(8,128)}, u32[]{:S(2)}, u32[]{:S(2)}) collective-permute-start(f32[8,128,128]{2,1,0:T(8,128)S(1)} %project.3), channel_id=1, source_target_pairs={{0,1},{1,0},{2,3},{3,2},{4,5},{5,4},{6,7},{7,6},{8,9},{9,8},{10,11... | collective-permute-start | bytes 1572872 | tf_op jit(solution)/shard_map/ppermute | solution.py:27
  106.2 1.2 collective-permute-done.3
  108.0 3.6 %all-to-all-start.5 = ((f32[8,48,128]{2,1,0:T(8,128)}), f32[8,48,128]{2,1,0:T(8,128)S(1)}, u32[]{:S(2)}, u32[]{:S(2)}) async-start(f32[8,48,128]{2,1,0:T(8,128)} %broadcast_in_dim.17), calls=%async_computation.5 | async-start | bytes 393216 | tf_op jit(solution)/shard_map/all_to_all | solution.py:31
  111.6 1.6 copy-done.4
  113.2 1.6 copy-done.12
  114.8 2.4 %project.2 = f32[8,128,128]{2,1,0:T(8,128)S(1)} custom-call(f32[1024,128]{1,0:T(8,128)S(1)} %bitcast.7, bf16[8,128,1024]{2,1,0:T(8,128)(2,1)S(1)} %get-tuple-element.21.high_ref, bf16[8,128,1024]{2,1,0:T(8,128)(2,1)S(1)} %copy-done.4, bf16[8,128,1024]{2,1,0:T(8,128)(2,1)S(1)} %copy-done.12), custom_call_target="tpu_custom_call" | custom-call | flops 2147483648 | bytes 4194304 | tf_op jit(solution)/shard_map/project/pallas_call | solution.py:133
  117.2 1.9 %add.13 = f32[8,128,128]{2,1,0:T(8,128)} add(f32[8,128,128]{2,1,0:T(8,128)S(1)} %project.2, f32[8,128,128]{2,1,0:T(8,128)} %collective-permute-done.2) | non-fusion elementwise | flops 131072 | bytes 1572864 | tf_op jit(solution)/shard_map/add | solution.py:345
  119.1 2.9 %all-to-all-done.5 = f32[8,48,128]{2,1,0:T(8,128)S(1)} async-done(((f32[8,48,128]{2,1,0:T(8,128)}), f32[8,48,128]{2,1,0:T(8,128)S(1)}, u32[]{:S(2)}, u32[]{:S(2)}) %all-to-all-start.5) | async-done | bytes 196640 | tf_op jit(solution)/shard_map/all_to_all | solution.py:31
  122.0 3.5 %all-to-all-start.4 = ((f32[8,128,128]{2,1,0:T(8,128)}), f32[8,128,128]{2,1,0:T(8,128)S(1)}, u32[]{:S(2)}, u32[]{:S(2)}) async-start(f32[8,128,128]{2,1,0:T(8,128)} %add.13), calls=%async_computation.4 | async-start | bytes 1048576 | tf_op jit(solution)/shard_map/all_to_all | solution.py:31
  127.2 3.7 %factor.1 = (f32[128,128]{1,0:T(8,128)S(1)}, f32[128,128]{1,0:T(8,128)S(1)}) custom-call(s32[1]{0:T(128)} %bitcast.half_ref.core_ref, f32[48,128]{1,0:T(8,128)S(1)} %reduce_sum.47.own_ref, f32[48,128]{1,0:T(8,128)S(1)} %collective-permute-done.4.other_ref), custom_call_target="tpu_custom_call" | custom-call | flops 6000000000 | bytes 49152 | tf_op jit(solution)/shard_map/factor/pallas_call | solution.py:266
  130.9 12.5 %all-to-all-done.4.parts_ref = f32[8,128,128]{2,1,0:T(8,128)S(1)} async-done(((f32[8,128,128]{2,1,0:T(8,128)}), f32[8,128,128]{2,1,0:T(8,128)S(1)}, u32[]{:S(2)}, u32[]{:S(2)}) %all-to-all-start.4) | async-done | bytes 524320 | tf_op jit(solution)/shard_map/all_to_all | solution.py:31
  145.5 12.2 %all_to_all.44 = f32[16,48,128]{2,1,0:T(8,128)S(1)} all-to-all(f32[16,48,128]{2,1,0:T(8,128)S(1)} %broadcast_in_dim.18), channel_id=1, replica_groups=mesh['y'=4,'x'=4,'z'=8,'core'=2] {'y','x'}, dimensions={0} | all-to-all | bytes 786432 | tf_op jit(solution)/shard_map/all_to_all | solution.py:31
  157.8 10.9 %all_to_all.45 = f32[8,48,128]{2,1,0:T(8,128)S(1)} all-to-all(f32[8,48,128]{2,1,0:T(8,128)S(1)} %broadcast_in_dim.19), channel_id=1, replica_groups=mesh['y'=4,'x'=4,'z'=8,'core'=2] {'z'}, dimensions={0} | all-to-all | bytes 393216 | tf_op jit(solution)/shard_map/all_to_all | solution.py:31
  168.7 3.1 %collective-permute-start.6 = (f32[48,128]{1,0:T(8,128)S(1)}, f32[48,128]{1,0:T(8,128)S(1)}, u32[]{:S(2)}, u32[]{:S(2)}) collective-permute-start(f32[48,128]{1,0:T(8,128)S(1)} %reduce_sum.49.own_ref), channel_id=1, source_target_pairs={{0,1},{1,0},{2,3},{3,2},{4,5},{5,4},{6,7},{7,6},{8,9},{9,8},{10,11... | collective-permute-start | bytes 73736 | tf_op jit(solution)/shard_map/ppermute | solution.py:27
  172.6 4.6 %last.1 = (f32[128,128]{1,0:T(8,128)}, f32[128,128]{1,0:T(8,128)}) custom-call(s32[1]{0:T(128)} %bitcast.half_ref.core_ref, f32[48,128]{1,0:T(8,128)S(1)} %reduce_sum.49.own_ref, f32[48,128]{1,0:T(8,128)S(1)} %collective-permute-done.6.other_ref, f32[128,128]{1,0:T(8,128)S(1)} %get-tuple-element.30.inner_ref, f32[128,128]{1,0:T(8,128)S(1)} %get-tuple-element.31.before_ref), custom_call_target="tpu_custom_call" | custom-call | flops 6000000000 | bytes 180224 | tf_op jit(solution)/shard_map/last/pallas_call | solution.py:266
  (47 shorter events, 10.8 us)
Async XLA Ops:
  0.6 1.0 copy-start
  1.7 9.2 %copy-start.1 = (f32[1024,128]{1,0:T(8,128)S(1)}, f32[1024,128]{1,0:T(8,128)}, u32[]{:S(2)}) copy-start(f32[1024,128]{1,0:T(8,128)} %right_ref.3) | copy-start | bytes 1572868
  4.9 1.4 copy-start.5
  6.3 1.4 copy-start.13
  7.6 6.4 %copy-start.8 = (bf16[8,128,1024]{2,1,0:T(8,128)(2,1)}, bf16[8,128,1024]{2,1,0:T(8,128)(2,1)S(1)}, u32[]{:S(2)}) copy-start(bf16[8,128,1024]{2,1,0:T(8,128)(2,1)S(1)} %get-tuple-element.20.low_ref.middle_ref) | copy-start | bytes 6291460
  7.6 9.0 %collective-permute-start = (f32[8,128,128]{2,1,0:T(8,128)S(1)}, f32[8,128,128]{2,1,0:T(8,128)S(1)}, u32[]{:S(2)}, u32[]{:S(2)}) collective-permute-start(f32[8,128,128]{2,1,0:T(8,128)S(1)} %get-tuple-element.18), channel_id=1, source_target_pairs={{0,1},{1,0},{2,3},{3,2},{4,5},{5,4},{6,7},{7,6},{8,9},{9,8},{10,11... | collective-permute-start | bytes 1572872 | tf_op jit(solution)/shard_map/ppermute | solution.py:27
  14.0 1.3 copy-start.2
  15.3 1.3 copy-start.11
  55.9 6.7 %collective-permute-start.1 = (f32[8,128,128]{2,1,0:T(8,128)S(1)}, f32[8,128,128]{2,1,0:T(8,128)S(1)}, u32[]{:S(2)}, u32[]{:S(2)}) collective-permute-start(f32[8,128,128]{2,1,0:T(8,128)S(1)} %all_to_all.41.left_ref), channel_id=1, source_target_pairs={{0,1},{1,0},{2,3},{3,2},{4,5},{5,4},{6,7},{7,6},{8,9},{9,8},{10,11... | collective-permute-start | bytes 1572872 | tf_op jit(solution)/shard_map/ppermute | solution.py:27
  59.9 1.6 copy-start.3
  61.5 1.6 copy-start.6
  61.5 2.2 %copy-start.9 = (bf16[8,128,1024]{2,1,0:T(8,128)(2,1)S(1)}, bf16[8,128,1024]{2,1,0:T(8,128)(2,1)}, u32[]{:S(2)}) copy-start(bf16[8,128,1024]{2,1,0:T(8,128)(2,1)} %copy-done.8) | copy-start | bytes 6291460
  96.0 1.6 copy-start.7
  97.6 1.6 copy-start.10
  99.2 1.6 copy-start.14
  103.2 14.0 %collective-permute-start.2 = (f32[8,128,128]{2,1,0:T(8,128)S(1)}, f32[8,128,128]{2,1,0:T(8,128)}, u32[]{:S(2)}, u32[]{:S(2)}) collective-permute-start(f32[8,128,128]{2,1,0:T(8,128)S(1)} %project.3), channel_id=1, source_target_pairs={{0,1},{1,0},{2,3},{3,2},{4,5},{5,4},{6,7},{7,6},{8,9},{9,8},{10,11... | collective-permute-start | bytes 1572872 | tf_op jit(solution)/shard_map/ppermute | solution.py:27
  106.1 1.3 collective-permute-start.3
  108.0 14.0 %all-to-all-start.5 = ((f32[8,48,128]{2,1,0:T(8,128)}), f32[8,48,128]{2,1,0:T(8,128)S(1)}, u32[]{:S(2)}, u32[]{:S(2)}) async-start(f32[8,48,128]{2,1,0:T(8,128)} %broadcast_in_dim.17), calls=%async_computation.5 | async-start | bytes 393216 | tf_op jit(solution)/shard_map/all_to_all | solution.py:31
  111.6 1.6 copy-start.4
  113.2 1.6 copy-start.12
  122.0 21.4 %all-to-all-start.4 = ((f32[8,128,128]{2,1,0:T(8,128)}), f32[8,128,128]{2,1,0:T(8,128)S(1)}, u32[]{:S(2)}, u32[]{:S(2)}) async-start(f32[8,128,128]{2,1,0:T(8,128)} %add.13), calls=%async_computation.4 | async-start | bytes 1048576 | tf_op jit(solution)/shard_map/all_to_all | solution.py:31
  125.5 1.7 collective-permute-start.4
  144.1 1.4 collective-permute-start.5
  168.7 3.9 %collective-permute-start.6 = (f32[48,128]{1,0:T(8,128)S(1)}, f32[48,128]{1,0:T(8,128)S(1)}, u32[]{:S(2)}, u32[]{:S(2)}) collective-permute-start(f32[48,128]{1,0:T(8,128)S(1)} %reduce_sum.49.own_ref), channel_id=1, source_target_pairs={{0,1},{1,0},{2,3},{3,2},{4,5},{5,4},{6,7},{7,6},{8,9},{9,8},{10,11... | collective-permute-start | bytes 73736 | tf_op jit(solution)/shard_map/ppermute | solution.py:27

commit v4 on v3

--- a/solution.py
+++ b/solution.py
@@ -20,7 +20,6 @@
 PULL = 8
 COUNT = 3
 VMEM = 12 * 1024 * 1024
-LOAD_VMEM = 46 * 1024 * 1024
 
 
 def swap(value):
@@ -29,11 +28,6 @@
 
 def exchange(value, axes):
     return lax.all_to_all(value, axes, 0, 0, tiled=False)
-
-
-def gathered(value, axes):
-    count = lax.axis_size(axes)
-    return exchange(jnp.broadcast_to(value, (count,) + value.shape), axes)
 
 
 def dot(a, b, dims=(((1,), (0,)), ((), ())), precision=None):
@@ -48,8 +42,11 @@
     return parts
 
 
-def params(limit=VMEM):
-    return pltpu.CompilerParams(vmem_limit_bytes=limit)
+keep = pltpu.with_memory_space_constraint
+
+
+def params():
+    return pltpu.CompilerParams(vmem_limit_bytes=VMEM)
 
 
 def rows_of(ref, place, height):
@@ -86,8 +83,8 @@
     zs, _, height, depth = slab.shape
     wide = right.shape[1]
     memory = pl.BlockSpec(memory_space=pltpu.VMEM)
-    anywhere = pl.BlockSpec(memory_space=pl.ANY)
-    part = jax.ShapeDtypeStruct((zs, height, depth), jnp.bfloat16)
+    anywhere = pl.BlockSpec(memory_space=pltpu.HBM)
+    part = pltpu.VMEM((zs, height, depth), jnp.bfloat16)
     product, *parts = pl.pallas_call(
         load_kernel,
         in_specs=[pl.BlockSpec(memory_space=pltpu.SMEM), anywhere, anywhere],
@@ -99,10 +96,10 @@
             pltpu.SemaphoreType.DMA((zs + 1,)),
         ],
         out_shape=[jax.ShapeDtypeStruct((zs, height, wide), jnp.float32)] + [part] * COUNT,
-        compiler_params=params(LOAD_VMEM),
+        compiler_params=params(),
         cost_estimate=cost(zs * height, depth, wide, 4),
         name="load",
-    )(half, slab, right)
+    )(half, keep(slab, pltpu.HBM), keep(right, pltpu.HBM))
     return product, parts
 
 
@@ -138,7 +135,7 @@
         compiler_params=params(),
         cost_estimate=cost(zs * height, depth, wide, 8),
         name="project",
-    )(right, *parts)
+    )(right, *[keep(part, pltpu.VMEM) for part in parts])
 
 
 def pull_kernel(more, left_ref, high_ref, low_ref, *refs):
@@ -169,7 +166,7 @@
         compiler_params=params(),
         cost_estimate=cost(zs * height, depth, wide, 4),
         name="pull",
-    )(left, *parts[:2], *([before] if more else []))
+    )(left, *[keep(part, pltpu.VMEM) for part in parts[:2]], *([before] if more else []))
 
 
 def spread(row):
@@ -283,16 +280,62 @@
     store_packed(core_ref[0], dot(value, value, CONTRACT, HIGHEST), own_ref, other_ref)
 
 
-def factor_kernel(core_ref, own_ref, other_ref, upper_ref, lower_ref):
-    gram = load_packed(core_ref[0], own_ref[...], other_ref[...])
-    upper_ref[...], lower_ref[...] = eliminate(gram, floor_of(gram))
-
-
-def middle_kernel(core_ref, parts_ref, lower_ref, inner_ref, own_ref, other_ref):
-    sketch = parts_ref[0]
-    for place in range(1, parts_ref.shape[0]):
-        sketch += parts_ref[place]
-    inner = dot(sketch, lower_ref[...], TRANSPOSED, HIGHEST)
+def add_kernel(first_ref, second_ref, out_ref):
+    out_ref[...] = first_ref[...] + second_ref[...]
+
+
+def total_kernel(scale, pieces_ref, out_ref):
+    value = pieces_ref[0]
+    for place in range(1, pieces_ref.shape[0]):
+        value += pieces_ref[place]
+    out_ref[...] = jnp.broadcast_to((value * scale)[None], out_ref.shape)
+
+
+def plain_call(kernel, shape, name, *operands):
+    memory = pl.BlockSpec(memory_space=pltpu.VMEM)
+    return pl.pallas_call(
+        kernel,
+        in_specs=[memory] * len(operands),
+        out_specs=memory,
+        out_shape=jax.ShapeDtypeStruct(shape, jnp.float32),
+        compiler_params=params(),
+        name=name,
+    )(*operands)
+
+
+def tail_kernel(start, pieces_ref, out_ref):
+    value = pieces_ref[0, start:]
+    for place in range(1, pieces_ref.shape[0]):
+        value += pieces_ref[place, start:]
+    out_ref[...] = value
+
+
+def pair_kernel(own_ref, other_ref, out_ref):
+    out_ref[...] = jnp.broadcast_to((own_ref[...] + other_ref[...])[None], out_ref.shape)
+
+
+def total(pieces, count, scale=1.0):
+    shape = (count,) + pieces.shape[1:]
+    return plain_call(functools.partial(total_kernel, scale), shape, "total", pieces)
+
+
+def join_kernel(product_ref, sent_ref, own_ref, other_ref, out_ref):
+    height = product_ref.shape[1]
+    out_ref[:, :height] = product_ref[...] + sent_ref[...]
+    gram = own_ref[...] + other_ref[...]
+    out_ref[:, height:] = jnp.broadcast_to(gram[None], (out_ref.shape[0],) + gram.shape)
+
+
+def middle_kernel(
+    core_ref, pieces_ref, pulled_own_ref, pulled_other_ref, inner_ref, before_ref, own_ref, other_ref
+):
+    gram = load_packed(core_ref[0], pulled_own_ref[...], pulled_other_ref[...])
+    before_ref[...], lower = eliminate(gram, floor_of(gram))
+    height = inner_ref.shape[0]
+    sketch = pieces_ref[0, :height]
+    for place in range(1, pieces_ref.shape[0]):
+        sketch += pieces_ref[place, :height]
+    inner = dot(sketch, lower, TRANSPOSED, HIGHEST)
     inner_ref[...] = inner
     store_packed(core_ref[0], dot(inner, inner, CONTRACT, HIGHEST), own_ref, other_ref)
 
@@ -304,13 +347,6 @@
     upper, lower = eliminate(gram, floor_of(gram))
     basis_ref[...] = dot(inner_ref[...], lower, TRANSPOSED, HIGHEST) * root_rows
     factor_ref[...] = dot(upper, before_ref[...], precision=HIGHEST) / root_rows
-
-
-def summed(own, other, stages):
-    value = own + swap(other)
-    for axes in stages:
-        value = jnp.sum(gathered(value, axes), axis=0)
-    return value, swap(value)
 
 
 def local(slab, test_matrix):
@@ -329,33 +365,46 @@
     product, far_parts = load(slab, test_matrix, far)
     sent = swap(product)
     product, parts = load(slab, test_matrix, core)
-    part = product + sent
-    own = gathered(jnp.sum(exchange(part, "z"), axis=0), "z")
+    part = plain_call(add_kernel, product.shape, "add", product, sent)
+    own = exchange(total(exchange(part, "z"), zs), "z")
 
     other = swap(own)
     part = pull(other, far_parts, pull(own, parts))
-    piece = jnp.sum(exchange(part.reshape(row_count, -1, wide), ROW), axis=0) / row_total
-    pulled = gathered(piece, ROW).reshape(-1, wide)
-
-    halves = small_call(gram_kernel, packed, "gram", 12 * columns * wide**2, core, pulled)
-    halves = summed(*halves, ("z",))
-    before, lower = small_call(factor_kernel, [square] * 2, "factor", 6 * 10**9, core, *halves)
-
+    pieces = total(exchange(part.reshape(row_count, -1, wide), ROW), row_count, 1.0 / row_total)
+    pulled = exchange(pieces, ROW).reshape(-1, wide)
+
+    own, other = small_call(gram_kernel, packed, "gram", 12 * columns * wide**2, core, pulled)
+    other = swap(other)
     sent = swap(project(pulled, far_parts))
-    part = project(pulled, parts) + sent
-    pieces = exchange(part, "z")
-
-    inner, *halves = small_call(
-        middle_kernel, [(rows // (2 * zs), wide)] + packed, "middle", 10**8, core, pieces, lower
+    product = project(pulled, parts)
+    height = product.shape[1]
+    shape = (zs, height + own.shape[0], wide)
+    joined = plain_call(join_kernel, shape, "join", product, sent, own, other)
+    pieces = exchange(joined, "z")
+    own = plain_call(functools.partial(tail_kernel, height), own.shape, "tail", pieces)
+
+    inner, before, *halves = small_call(
+        middle_kernel,
+        [(height, wide), square] + packed,
+        "middle",
+        6 * 10**9,
+        core,
+        pieces,
+        own,
+        swap(own),
     )
-    halves = summed(*halves, (ROW, "z"))
+    own, other = halves
+    copies = plain_call(pair_kernel, (row_count,) + own.shape, "pair", own, swap(other))
+    copies = total(exchange(copies, ROW), zs)
+    own = total(exchange(copies, "z"), 1)[0]
     basis, factor = small_call(
         functools.partial(last_kernel, root_rows),
         [inner.shape, square],
         "last",
         6 * 10**9,
         core,
-        *halves,
+        own,
+        swap(own),
         inner,
         before,
     )

time: 178 us -> 161 us (0.904)
  blocking collectives: 93.3 us -> 123 us
  local copies, waits for them, and re-layouts: 17.8 us -> 0 us
  waiting for transfers between devices: 19.1 us -> 2.96 us
  starting transfers between devices: 21.1 us -> 10.8 us
  other arithmetic: 2.09 us -> 0 us
    all_to_all x6 -> x7, blocking collectives: 93.3 us -> 123 us  [exchange(): return lax.all_to_all(value, axes, 0, 0, tiled=False)]
    unnamed x30 -> x0, local copies, waits for them, and re-layouts: 17 us -> none
    all_to_all x2 -> x0, waiting for transfers between devices: 15.4 us -> none  [exchange(): return lax.all_to_all(value, axes, 0, 0, tiled=False)]
    all_to_all x2 -> x0, starting transfers between devices: 7.06 us -> none  [exchange(): return lax.all_to_all(value, axes, 0, 0, tiled=False)]
    ppermute x7, starting transfers between devices: 14 us -> 10.8 us  [swap(): return lax.ppermute(value, 'core', SWAP)]
    add x4 -> x0, other arithmetic: 1.96 us -> none  [the longest x1 1.89 us: local(): part = project(pulled, parts) + sent]
    pallas_call x4 -> x3, Pallas kernels: 9.66 us -> 9.61 us  [small_call(): pl.pallas_call(kernel, in_specs=[pl.BlockSpec(memory_space=pltpu.SMEM)] +...]
  transfers between devices with their start and end apart: 9 -> 7, of which waited for: 6 -> 4; matrix products, arithmetic and copies ran while one was open for 1% -> 0% of each run, Pallas kernels for 6% -> 5%
where the time goes in v4:
time: 161 us
  blocking collectives  123 us (76%)
  Pallas kernels  23.5 us (15%)
  starting transfers between devices  10.8 us (7%)
  waiting for transfers between devices  2.96 us (2%)
    all_to_all x7, blocking collectives, exchange(): return lax.all_to_all(value, axes, 0, 0, tiled=False)  123 us
    ppermute x7, starting transfers between devices, swap(): return lax.ppermute(value, 'core', SWAP)  10.8 us
    pallas_call x3, Pallas kernels, small_call(): pl.pallas_call(kernel, in_specs=[pl.BlockSpec(memory_space=pltpu.SMEM)] +...  9.61 us
    pallas_call x2, Pallas kernels, load(): pl.pallas_call(load_kernel, in_specs=[pl.BlockSpec(memory_space=pltpu.SME...  6.58 us
    pallas_call x2, Pallas kernels, project(): pl.pallas_call(project_kernel, in_specs=[memory] * (1 + COUNT), out_specs...  4.71 us
  transfers between devices with their start and end apart: 7, of which 4 were waited for; matrix products, arithmetic and copies ran while one was open for 0% of the time, Pallas kernels for 5%

profile of v4, /device:TPU:1, one launch (start us, length us, event | category | flops | bytes accessed | tf_op | source)
XLA Modules:
  0.0 160.7 jit_solution(3966321340751326079)
XLA Ops:
  0.6 3.3 %load.3 = (f32[8,128,128]{2,1,0:T(8,128)S(1)}, bf16[8,128,1024]{2,1,0:T(8,128)(2,1)S(1)}, bf16[8,128,1024]{2,1,0:T(8,128)(2,1)S(1)}, bf16[8,128,1024]{2,1,0:T(8,128)(2,1)S(1)}) custom-call(s32[1]{0:T(128)S(6)} %sub.3.half_ref, f32[8,2,128,1024]{3,2,1,0:T(8,128)} %bitcast.11, f32[1024,128]{1,0:T(8,128)} %right_ref.3), custom_call_target="tpu_custom_call" | custom-call | flops 1073741824 | bytes 4194304 | tf_op jit(solution)/shard_map/load/pallas_call | solution.py:88
  3.9 3.3 %collective-permute-start = (f32[8,128,128]{2,1,0:T(8,128)S(1)}, f32[8,128,128]{2,1,0:T(8,128)S(1)}, u32[]{:S(2)}, u32[]{:S(2)}) collective-permute-start(f32[8,128,128]{2,1,0:T(8,128)S(1)} %get-tuple-element.17), channel_id=1, source_target_pairs={{0,1},{1,0},{2,3},{3,2},{4,5},{5,4},{6,7},{7,6},{8,9},{9,8},{10,11... | collective-permute-start | bytes 1572872 | tf_op jit(solution)/shard_map/ppermute | solution.py:26
  7.3 3.3 %load.2 = (f32[8,128,128]{2,1,0:T(8,128)S(1)}, bf16[8,128,1024]{2,1,0:T(8,128)(2,1)S(1)}, bf16[8,128,1024]{2,1,0:T(8,128)(2,1)S(1)}, bf16[8,128,1024]{2,1,0:T(8,128)(2,1)S(1)}) custom-call(s32[1]{0:T(128)} %bitcast.half_ref.core_ref, f32[8,2,128,1024]{3,2,1,0:T(8,128)} %bitcast.12, f32[1024,128]{1,0:T(8,128)} %right_ref.3), custom_call_target="tpu_custom_call" | custom-call | flops 1073741824 | bytes 4194304 | tf_op jit(solution)/shard_map/load/pallas_call | solution.py:88
  10.6 0.0 collective-permute-done.second_ref
  10.6 0.1 add.1
  10.6 24.2 %all_to_all.35.pieces_ref = f32[8,128,128]{2,1,0:T(8,128)S(1)} all-to-all(f32[8,128,128]{2,1,0:T(8,128)S(1)} %add.1), channel_id=1, replica_groups=mesh['y'=4,'x'=4,'z'=8,'core'=2] {'z'}, dimensions={0} | all-to-all | bytes 1048576 | tf_op jit(solution)/shard_map/all_to_all | solution.py:30
  34.9 20.3 %all_to_all.36.left_ref = f32[8,128,128]{2,1,0:T(8,128)S(1)} all-to-all(f32[8,128,128]{2,1,0:T(8,128)S(1)} %total.4), channel_id=1, replica_groups=mesh['y'=4,'x'=4,'z'=8,'core'=2] {'z'}, dimensions={0} | all-to-all | bytes 1048576 | tf_op jit(solution)/shard_map/all_to_all | solution.py:30
  55.2 0.6 collective-permute-start.1
  55.8 1.1 pull.2.refs_0_
  56.9 0.4 collective-permute-done.1.left_ref
  57.3 1.1 pull.3
  58.4 17.3 %all_to_all.37.pieces_ref = f32[16,64,128]{2,1,0:T(8,128)S(1)} all-to-all(f32[16,64,128]{2,1,0:T(8,128)S(1)} %bitcast.5), channel_id=1, replica_groups=mesh['y'=4,'x'=4,'z'=8,'core'=2] {'y','x'}, dimensions={0} | all-to-all | bytes 1048576 | tf_op jit(solution)/shard_map/all_to_all | solution.py:30
  75.7 0.1 total.5
  75.8 13.4 %all_to_all.38 = f32[16,64,128]{2,1,0:T(8,128)S(1)} all-to-all(f32[16,64,128]{2,1,0:T(8,128)S(1)} %total.5), channel_id=1, replica_groups=mesh['y'=4,'x'=4,'z'=8,'core'=2] {'y','x'}, dimensions={0} | all-to-all | bytes 1048576 | tf_op jit(solution)/shard_map/all_to_all | solution.py:30
  89.2 2.4 %project.3 = f32[8,128,128]{2,1,0:T(8,128)S(1)} custom-call(f32[1024,128]{1,0:T(8,128)S(1)} %bitcast.6, bf16[8,128,1024]{2,1,0:T(8,128)(2,1)S(1)} %get-tuple-element.18.high_ref, bf16[8,128,1024]{2,1,0:T(8,128)(2,1)S(1)} %get-tuple-element.19.low_ref.middle_ref, bf16[8,128,1024]{2,1,0:T(8,128)(2,1)S(1)} %get-tuple-element.23.low_ref), custom_call_target="tpu_custom_call" | custom-call | flops 2147483648 | bytes 4194304 | tf_op jit(solution)/shard_map/project/pallas_call | solution.py:130
  91.6 2.4 %collective-permute-start.2 = (f32[8,128,128]{2,1,0:T(8,128)S(1)}, f32[8,128,128]{2,1,0:T(8,128)S(1)}, u32[]{:S(2)}, u32[]{:S(2)}) collective-permute-start(f32[8,128,128]{2,1,0:T(8,128)S(1)} %project.3), channel_id=1, source_target_pairs={{0,1},{1,0},{2,3},{3,2},{4,5},{5,4},{6,7},{7,6},{8,9},{9,8},{10,11... | collective-permute-start | bytes 1572872 | tf_op jit(solution)/shard_map/ppermute | solution.py:26
  94.0 0.7 gram.1
  94.7 0.3 collective-permute-start.3
  94.9 2.4 %project.2.product_ref = f32[8,128,128]{2,1,0:T(8,128)S(1)} custom-call(f32[1024,128]{1,0:T(8,128)S(1)} %bitcast.8, bf16[8,128,1024]{2,1,0:T(8,128)(2,1)S(1)} %get-tuple-element.20.high_ref, bf16[8,128,1024]{2,1,0:T(8,128)(2,1)S(1)} %get-tuple-element.21.low_ref.middle_ref, bf16[8,128,1024]{2,1,0:T(8,128)(2,1)S(1)} %get-tuple-element.22.low_ref), custom_call_target="tpu_custom_call" | custom-call | flops 2147483648 | bytes 4194304 | tf_op jit(solution)/shard_map/project/pallas_call | solution.py:130
  97.3 0.0 collective-permute-done.3.other_ref
  97.3 0.1 join.1
  97.4 24.4 %all_to_all.39.pieces_ref = f32[8,176,128]{2,1,0:T(8,128)S(1)} all-to-all(f32[8,176,128]{2,1,0:T(8,128)S(1)} %join.1), channel_id=1, replica_groups=mesh['y'=4,'x'=4,'z'=8,'core'=2] {'z'}, dimensions={0} | all-to-all | bytes 1441792 | tf_op jit(solution)/shard_map/all_to_all | solution.py:30
  121.9 0.7 collective-permute-start.4
  122.6 0.8 collective-permute-done.4.pulled_other_ref
  123.4 4.3 %middle.1 = (f32[128,128]{1,0:T(8,128)S(1)}, f32[128,128]{1,0:T(8,128)S(1)}, f32[48,128]{1,0:T(8,128)S(1)}, f32[48,128]{1,0:T(8,128)S(1)}) custom-call(s32[1]{0:T(128)} %bitcast.half_ref.core_ref, f32[8,176,128]{2,1,0:T(8,128)S(1)} %all_to_all.39.pieces_ref, f32[48,128]{1,0:T(8,128)S(1)} %tail.1.pulled_own_ref, ...), custom_call_target="tpu_custom_call" | custom-call | flops 6000000000 | bytes 770048 | tf_op jit(solution)/shard_map/middle/pallas_call | solution.py:263
  127.7 0.4 collective-permute-start.5
  128.1 0.8 collective-permute-done.5.other_ref
  129.0 12.2 %all_to_all.40.pieces_ref = f32[16,48,128]{2,1,0:T(8,128)S(1)} all-to-all(f32[16,48,128]{2,1,0:T(8,128)S(1)} %pair.1), channel_id=1, replica_groups=mesh['y'=4,'x'=4,'z'=8,'core'=2] {'y','x'}, dimensions={0} | all-to-all | bytes 786432 | tf_op jit(solution)/shard_map/all_to_all | solution.py:30
  141.3 10.9 %all_to_all.41.pieces_ref = f32[8,48,128]{2,1,0:T(8,128)S(1)} all-to-all(f32[8,48,128]{2,1,0:T(8,128)S(1)} %total.6), channel_id=1, replica_groups=mesh['y'=4,'x'=4,'z'=8,'core'=2] {'z'}, dimensions={0} | all-to-all | bytes 393216 | tf_op jit(solution)/shard_map/all_to_all | solution.py:30
  152.2 3.1 %collective-permute-start.6 = (f32[48,128]{1,0:T(8,128)S(1)}, f32[48,128]{1,0:T(8,128)S(1)}, u32[]{:S(2)}, u32[]{:S(2)}) collective-permute-start(f32[48,128]{1,0:T(8,128)S(1)} %bitcast.9), channel_id=1, source_target_pairs={{0,1},{1,0},{2,3},{3,2},{4,5},{5,4},{6,7},{7,6},{8,9},{9,8},{10,11... | collective-permute-start | bytes 73736 | tf_op jit(solution)/shard_map/ppermute | solution.py:26
  155.2 0.8 collective-permute-done.6.other_ref
  156.1 4.6 %last.1 = (f32[128,128]{1,0:T(8,128)}, f32[128,128]{1,0:T(8,128)}) custom-call(s32[1]{0:T(128)} %bitcast.half_ref.core_ref, f32[48,128]{1,0:T(8,128)S(1)} %bitcast.10, f32[48,128]{1,0:T(8,128)S(1)} %collective-permute-done.6.other_ref, f32[128,128]{1,0:T(8,128)S(1)} %get-tuple-element.28.inner_ref, f32[128,128]{1,0:T(8,128)S(1)} %get-tuple-element.29.before_ref), custom_call_target="tpu_custom_call" | custom-call | flops 6000000000 | bytes 180224 | tf_op jit(solution)/shard_map/last/pallas_call | solution.py:263
  (6 shorter events, 0.1 us)
Async XLA Ops:
  3.9 6.6 %collective-permute-start = (f32[8,128,128]{2,1,0:T(8,128)S(1)}, f32[8,128,128]{2,1,0:T(8,128)S(1)}, u32[]{:S(2)}, u32[]{:S(2)}) collective-permute-start(f32[8,128,128]{2,1,0:T(8,128)S(1)} %get-tuple-element.17), channel_id=1, source_target_pairs={{0,1},{1,0},{2,3},{3,2},{4,5},{5,4},{6,7},{7,6},{8,9},{9,8},{10,11... | collective-permute-start | bytes 1572872 | tf_op jit(solution)/shard_map/ppermute | solution.py:26
  55.2 2.1 %collective-permute-start.1 = (f32[8,128,128]{2,1,0:T(8,128)S(1)}, f32[8,128,128]{2,1,0:T(8,128)S(1)}, u32[]{:S(2)}, u32[]{:S(2)}) collective-permute-start(f32[8,128,128]{2,1,0:T(8,128)S(1)} %all_to_all.36.left_ref), channel_id=1, source_target_pairs={{0,1},{1,0},{2,3},{3,2},{4,5},{5,4},{6,7},{7,6},{8,9},{9,8},{10,11... | collective-permute-start | bytes 1572872 | tf_op jit(solution)/shard_map/ppermute | solution.py:26
  91.6 5.8 %collective-permute-start.2 = (f32[8,128,128]{2,1,0:T(8,128)S(1)}, f32[8,128,128]{2,1,0:T(8,128)S(1)}, u32[]{:S(2)}, u32[]{:S(2)}) collective-permute-start(f32[8,128,128]{2,1,0:T(8,128)S(1)} %project.3), channel_id=1, source_target_pairs={{0,1},{1,0},{2,3},{3,2},{4,5},{5,4},{6,7},{7,6},{8,9},{9,8},{10,11... | collective-permute-start | bytes 1572872 | tf_op jit(solution)/shard_map/ppermute | solution.py:26
  94.7 2.6 %collective-permute-start.3 = (f32[48,128]{1,0:T(8,128)S(1)}, f32[48,128]{1,0:T(8,128)S(1)}, u32[]{:S(2)}, u32[]{:S(2)}) collective-permute-start(f32[48,128]{1,0:T(8,128)S(1)} %get-tuple-element.25), channel_id=1, source_target_pairs={{0,1},{1,0},{2,3},{3,2},{4,5},{5,4},{6,7},{7,6},{8,9},{9,8},{10,11... | collective-permute-start | bytes 73736 | tf_op jit(solution)/shard_map/ppermute | solution.py:26
  121.9 1.6 collective-permute-start.4
  127.7 1.3 collective-permute-start.5
  152.2 3.9 %collective-permute-start.6 = (f32[48,128]{1,0:T(8,128)S(1)}, f32[48,128]{1,0:T(8,128)S(1)}, u32[]{:S(2)}, u32[]{:S(2)}) collective-permute-start(f32[48,128]{1,0:T(8,128)S(1)} %bitcast.9), channel_id=1, source_target_pairs={{0,1},{1,0},{2,3},{3,2},{4,5},{5,4},{6,7},{7,6},{8,9},{9,8},{10,11... | collective-permute-start | bytes 73736 | tf_op jit(solution)/shard_map/ppermute | solution.py:26

commit v5 on v4

--- a/solution.py
+++ b/solution.py
@@ -123,19 +123,19 @@
         out_ref[place : place + STEP] = (first[:, :wide] + small).reshape(STEP, -1, wide)
 
 
-def project(right, parts):
+def project(right, parts, after=()):
     zs, height, depth = parts[0].shape
     wide = right.shape[1]
     memory = pl.BlockSpec(memory_space=pltpu.VMEM)
     return pl.pallas_call(
-        project_kernel,
-        in_specs=[memory] * (1 + COUNT),
+        without(project_kernel, 1 + COUNT, len(after)),
+        in_specs=[memory] * (1 + COUNT) + [pl.BlockSpec(memory_space=pl.ANY)] * len(after),
         out_specs=memory,
         out_shape=jax.ShapeDtypeStruct((zs, height, wide), jnp.float32),
         compiler_params=params(),
         cost_estimate=cost(zs * height, depth, wide, 8),
         name="project",
-    )(right, *[keep(part, pltpu.VMEM) for part in parts])
+    )(right, *[keep(part, pltpu.VMEM) for part in parts], *after)
 
 
 def pull_kernel(more, left_ref, high_ref, low_ref, *refs):
@@ -232,52 +232,83 @@
     return jnp.concatenate(upper, axis=0), jnp.concatenate(lower, axis=0)
 
 
-def store_packed(core, gram, own_ref, other_ref):
-    half = gram.shape[0] // 2
-    last = gram[half:, half:]
-    tail = jnp.concatenate([last[: half // 2], last[half // 2 :]], axis=1)
-    packed = jnp.concatenate([gram[:half], tail], axis=0)
+def pack(gram):
+    n = gram.shape[0]
+    q = n // 4
+    middle = jnp.concatenate([gram[q : 2 * q, q:], gram[3 * q :, 3 * q :]], axis=1)
+    low = gram[2 * q : 3 * q, 2 * q :]
+    tail = jnp.concatenate([low[: q // 2], low[q // 2 :]], axis=1)
+    return jnp.concatenate([gram[:q], middle, tail], axis=0)
+
+
+def unpack(packed):
+    n = packed.shape[1]
+    q = n // 4
+    middle, tail = packed[q : 2 * q], packed[2 * q :]
+    low = jnp.concatenate([tail[:, : 2 * q], tail[:, 2 * q :]], axis=0)
+    second = jnp.concatenate([jnp.zeros((q, q), jnp.float32), middle[:, : 3 * q]], axis=1)
+    third = jnp.concatenate([jnp.zeros((q, 2 * q), jnp.float32), low], axis=1)
+    fourth = jnp.concatenate([jnp.zeros((q, 3 * q), jnp.float32), middle[:, 3 * q :]], axis=1)
+    upper = jnp.concatenate([packed[:q], second, third, fourth], axis=0)
+    row = lax.broadcasted_iota(jnp.int32, (n, n), 0)
+    column = lax.broadcasted_iota(jnp.int32, (n, n), 1)
+    return jnp.where(row <= column, upper, jnp.transpose(upper))
+
+
+def store_halves(core, gram, own_ref, other_ref):
+    packed = pack(gram)
     middle = packed.shape[0] // 2
     first, second = packed[:middle], packed[middle:]
     own_ref[...] = jnp.where(core == 0, first, second)
     other_ref[...] = jnp.where(core == 0, second, first)
 
 
-def load_packed(core, own, other):
-    packed = jnp.concatenate(
-        [jnp.where(core == 0, own, other), jnp.where(core == 0, other, own)], axis=0
-    )
-    half = packed.shape[1] // 2
-    top, tail = packed[:half], packed[half:]
-    last = jnp.concatenate([tail[:, :half], tail[:, half:]], axis=0)
-    bottom = jnp.concatenate([jnp.transpose(top[:, half:]), last], axis=1)
-    return jnp.concatenate([top, bottom], axis=0)
+def load_halves(core, own, other):
+    first = jnp.where(core == 0, own, other)
+    second = jnp.where(core == 0, other, own)
+    return unpack(jnp.concatenate([first, second], axis=0))
 
 
 def floor_of(gram):
     return 1e-9 * jnp.max(gram)
 
 
-def small_call(kernel, shapes, name, flops, core, *operands):
+def without(kernel, place, count):
+    def call(*refs):
+        kernel(*refs[:place], *refs[place + count :])
+
+    return call
+
+
+def small_call(kernel, shapes, name, cycles, operands, scalars=(), after=()):
     memory = pl.BlockSpec(memory_space=pltpu.VMEM)
     return pl.pallas_call(
-        kernel,
-        in_specs=[pl.BlockSpec(memory_space=pltpu.SMEM)] + [memory] * len(operands),
+        without(kernel, len(scalars) + len(operands), len(after)),
+        in_specs=[pl.BlockSpec(memory_space=pltpu.SMEM)] * len(scalars)
+        + [memory] * len(operands)
+        + [pl.BlockSpec(memory_space=pl.ANY)] * len(after),
         out_specs=[memory] * len(shapes),
         out_shape=[jax.ShapeDtypeStruct(shape, jnp.float32) for shape in shapes],
         compiler_params=params(),
         cost_estimate=pl.CostEstimate(
-            flops=flops,
-            bytes_accessed=4 * sum(operand.size for operand in operands),
-            transcendentals=0,
+            flops=cycles * 10**6, bytes_accessed=4 * shapes[0][-1], transcendentals=0
         ),
         name=name,
-    )(core, *operands)
-
-
-def gram_kernel(core_ref, value_ref, own_ref, other_ref):
+    )(*scalars, *operands, *after)
+
+
+def plain_call(kernel, shape, name, *operands, after=()):
+    return small_call(kernel, [shape], name, 100, operands, after=after)[0]
+
+
+def gram_kernel(value_ref, out_ref):
     value = value_ref[...]
-    store_packed(core_ref[0], dot(value, value, CONTRACT, HIGHEST), own_ref, other_ref)
+    out_ref[...] = pack(dot(value, value, CONTRACT, HIGHEST))
+
+
+def factor_kernel(first_ref, second_ref, upper_ref, lower_ref):
+    gram = unpack(first_ref[...] + second_ref[...])
+    upper_ref[...], lower_ref[...] = eliminate(gram, floor_of(gram))
 
 
 def add_kernel(first_ref, second_ref, out_ref):
@@ -291,23 +322,8 @@
     out_ref[...] = jnp.broadcast_to((value * scale)[None], out_ref.shape)
 
 
-def plain_call(kernel, shape, name, *operands):
-    memory = pl.BlockSpec(memory_space=pltpu.VMEM)
-    return pl.pallas_call(
-        kernel,
-        in_specs=[memory] * len(operands),
-        out_specs=memory,
-        out_shape=jax.ShapeDtypeStruct(shape, jnp.float32),
-        compiler_params=params(),
-        name=name,
-    )(*operands)
-
-
-def tail_kernel(start, pieces_ref, out_ref):
-    value = pieces_ref[0, start:]
-    for place in range(1, pieces_ref.shape[0]):
-        value += pieces_ref[place, start:]
-    out_ref[...] = value
+def add(first, second, after=()):
+    return plain_call(add_kernel, first.shape, "add", first, second, after=after)
 
 
 def pair_kernel(own_ref, other_ref, out_ref):
@@ -319,31 +335,19 @@
     return plain_call(functools.partial(total_kernel, scale), shape, "total", pieces)
 
 
-def join_kernel(product_ref, sent_ref, own_ref, other_ref, out_ref):
-    height = product_ref.shape[1]
-    out_ref[:, :height] = product_ref[...] + sent_ref[...]
-    gram = own_ref[...] + other_ref[...]
-    out_ref[:, height:] = jnp.broadcast_to(gram[None], (out_ref.shape[0],) + gram.shape)
-
-
-def middle_kernel(
-    core_ref, pieces_ref, pulled_own_ref, pulled_other_ref, inner_ref, before_ref, own_ref, other_ref
-):
-    gram = load_packed(core_ref[0], pulled_own_ref[...], pulled_other_ref[...])
-    before_ref[...], lower = eliminate(gram, floor_of(gram))
-    height = inner_ref.shape[0]
-    sketch = pieces_ref[0, :height]
+def middle_kernel(core_ref, pieces_ref, lower_ref, inner_ref, own_ref, other_ref):
+    sketch = pieces_ref[0]
     for place in range(1, pieces_ref.shape[0]):
-        sketch += pieces_ref[place, :height]
-    inner = dot(sketch, lower, TRANSPOSED, HIGHEST)
+        sketch += pieces_ref[place]
+    inner = dot(sketch, lower_ref[...], TRANSPOSED, HIGHEST)
     inner_ref[...] = inner
-    store_packed(core_ref[0], dot(inner, inner, CONTRACT, HIGHEST), own_ref, other_ref)
+    store_halves(core_ref[0], dot(inner, inner, CONTRACT, HIGHEST), own_ref, other_ref)
 
 
 def last_kernel(
     root_rows, core_ref, own_ref, other_ref, inner_ref, before_ref, basis_ref, factor_ref
 ):
-    gram = load_packed(core_ref[0], own_ref[...], other_ref[...])
+    gram = load_halves(core_ref[0], own_ref[...], other_ref[...])
     upper, lower = eliminate(gram, floor_of(gram))
     basis_ref[...] = dot(inner_ref[...], lower, TRANSPOSED, HIGHEST) * root_rows
     factor_ref[...] = dot(upper, before_ref[...], precision=HIGHEST) / root_rows
@@ -360,12 +364,13 @@
     far = 1 - core
     slab = slab.reshape(zs, 2, -1, columns)
     square = (wide, wide)
-    packed = [(3 * wide // 8, wide)] * 2
+    packed = (5 * wide // 8, wide)
+    halves = [(5 * wide // 16, wide)] * 2
 
     product, far_parts = load(slab, test_matrix, far)
     sent = swap(product)
     product, parts = load(slab, test_matrix, core)
-    part = plain_call(add_kernel, product.shape, "add", product, sent)
+    part = add(product, sent)
     own = exchange(total(exchange(part, "z"), zs), "z")
 
     other = swap(own)
@@ -373,27 +378,22 @@
     pieces = total(exchange(part.reshape(row_count, -1, wide), ROW), row_count, 1.0 / row_total)
     pulled = exchange(pieces, ROW).reshape(-1, wide)
 
-    own, other = small_call(gram_kernel, packed, "gram", 12 * columns * wide**2, core, pulled)
-    other = swap(other)
-    sent = swap(project(pulled, far_parts))
-    product = project(pulled, parts)
-    height = product.shape[1]
-    shape = (zs, height + own.shape[0], wide)
-    joined = plain_call(join_kernel, shape, "join", product, sent, own, other)
-    pieces = exchange(joined, "z")
-    own = plain_call(functools.partial(tail_kernel, height), own.shape, "tail", pieces)
-
-    inner, before, *halves = small_call(
-        middle_kernel,
-        [(height, wide), square] + packed,
-        "middle",
-        6 * 10**9,
-        core,
-        pieces,
-        own,
-        swap(own),
+    gram = small_call(gram_kernel, [packed], "gram", 700, [pulled])[0]
+    grams, distance = [gram], 1
+    while distance < zs:
+        partners = [(place, place ^ distance) for place in range(zs)]
+        grams.append(add(grams[-1], lax.ppermute(grams[-1], "z", partners)))
+        distance *= 2
+    pair = [grams[-1], swap(grams[-1])]
+    before, lower = small_call(factor_kernel, [square] * 2, "factor", 3600, pair)
+
+    sent = swap(project(pulled, far_parts, grams[:1]))
+    part = add(project(pulled, parts, grams[:1]), sent, grams[1:2])
+    pieces = exchange(part, "z")
+
+    inner, own, other = small_call(
+        middle_kernel, [part.shape[1:]] + halves, "middle", 650, [pieces, lower], [core]
     )
-    own, other = halves
     copies = plain_call(pair_kernel, (row_count,) + own.shape, "pair", own, swap(other))
     copies = total(exchange(copies, ROW), zs)
     own = total(exchange(copies, "z"), 1)[0]
@@ -401,12 +401,9 @@
         functools.partial(last_kernel, root_rows),
         [inner.shape, square],
         "last",
-        6 * 10**9,
-        core,
-        own,
-        swap(own),
-        inner,
-        before,
+        4600,
+        [own, swap(own), inner, before],
+        [core],
     )
     return basis, factor
 

time: 161 us -> 167 us (1.037)
  blocking collectives: 123 us -> 102 us
  starting transfers between devices: 10.8 us -> 26.6 us
  waiting for transfers between devices: 2.96 us -> 12.9 us
    all_to_all x7 -> x6, blocking collectives: 123 us -> 102 us  [exchange(): return lax.all_to_all(value, axes, 0, 0, tiled=False)]
    ppermute x0 -> x3, waiting for transfers between devices: none -> 9.98 us  [local(): grams.append(add(grams[-1], lax.ppermute(grams[-1], 'z', partners)))]
    ppermute x0 -> x3, starting transfers between devices: none -> 9.32 us  [local(): grams.append(add(grams[-1], lax.ppermute(grams[-1], 'z', partners)))]
    all_to_all x0 -> x1, starting transfers between devices: none -> 3.49 us  [exchange(): return lax.all_to_all(value, axes, 0, 0, tiled=False)]
    ppermute x7 -> x6, starting transfers between devices: 10.8 us -> 13.8 us  [swap(): return lax.ppermute(value, 'core', SWAP)]
    pallas_call x13 -> x16, Pallas kernels: 14.6 us -> 15.6 us  [the longest x14 10.8 us: small_call(): pl.pallas_call(without(kernel, len(scalars) + len(operands), len(after)),...]
  transfers between devices with their start and end apart: 7 -> 10, of which waited for: 4 -> 7; matrix products, arithmetic and copies ran while one was open for 0% -> 0% of each run, Pallas kernels for 5% -> 6%
where the time goes in v5:
time: 167 us; the launch traced here: 166 us
  blocking collectives  102 us (61%)
  starting transfers between devices  26.6 us (16%)
  Pallas kernels  24.4 us (15%)
  waiting for transfers between devices  12.9 us (8%)
    all_to_all x6, blocking collectives, exchange(): return lax.all_to_all(value, axes, 0, 0, tiled=False)  102 us
    ppermute x6, starting transfers between devices, swap(): return lax.ppermute(value, 'core', SWAP)  13.8 us
    pallas_call x14, Pallas kernels, small_call(): pl.pallas_call(without(kernel, len(scalars) + len(operands), len(after)),...  10.8 us
    ppermute x3, waiting for transfers between devices, local(): grams.append(add(grams[-1], lax.ppermute(grams[-1], 'z', partners)))  9.98 us
    ppermute x3, starting transfers between devices, local(): grams.append(add(grams[-1], lax.ppermute(grams[-1], 'z', partners)))  9.32 us
    pallas_call x2, Pallas kernels, load(): pl.pallas_call(load_kernel, in_specs=[pl.BlockSpec(memory_space=pltpu.SME...  6.52 us
    pallas_call x2, Pallas kernels, project(): pl.pallas_call(without(project_kernel, 1 + COUNT, len(after)), in_specs=[...  4.81 us
    all_to_all x1, starting transfers between devices, exchange(): return lax.all_to_all(value, axes, 0, 0, tiled=False)  3.49 us
  transfers between devices with their start and end apart: 10, of which 7 were waited for; matrix products, arithmetic and copies ran while one was open for 0% of the time, Pallas kernels for 6%

profile of v5, /device:TPU:1, one launch (start us, length us, event | category | flops | bytes accessed | tf_op | source)
XLA Modules:
  0.0 166.3 jit_solution(4046170989697922842)
XLA Ops:
  0.6 3.2 %load.3 = (f32[8,128,128]{2,1,0:T(8,128)S(1)}, bf16[8,128,1024]{2,1,0:T(8,128)(2,1)S(1)}, bf16[8,128,1024]{2,1,0:T(8,128)(2,1)S(1)}, bf16[8,128,1024]{2,1,0:T(8,128)(2,1)S(1)}) custom-call(s32[1]{0:T(128)S(6)} %sub.3.half_ref, f32[8,2,128,1024]{3,2,1,0:T(8,128)} %bitcast.11, f32[1024,128]{1,0:T(8,128)} %right_ref.3), custom_call_target="tpu_custom_call" | custom-call | flops 1073741824 | bytes 4194304 | tf_op jit(solution)/shard_map/load/pallas_call | solution.py:88
  3.9 3.3 %collective-permute-start = (f32[8,128,128]{2,1,0:T(8,128)S(1)}, f32[8,128,128]{2,1,0:T(8,128)S(1)}, u32[]{:S(2)}, u32[]{:S(2)}) collective-permute-start(f32[8,128,128]{2,1,0:T(8,128)S(1)} %get-tuple-element.16), channel_id=1, source_target_pairs={{0,1},{1,0},{2,3},{3,2},{4,5},{5,4},{6,7},{7,6},{8,9},{9,8},{10,11... | collective-permute-start | bytes 1572872 | tf_op jit(solution)/shard_map/ppermute | solution.py:26
  7.2 3.3 %load.2 = (f32[8,128,128]{2,1,0:T(8,128)S(1)}, bf16[8,128,1024]{2,1,0:T(8,128)(2,1)S(1)}, bf16[8,128,1024]{2,1,0:T(8,128)(2,1)S(1)}, bf16[8,128,1024]{2,1,0:T(8,128)(2,1)S(1)}) custom-call(s32[1]{0:T(128)} %bitcast.half_ref.refs_0_, f32[8,2,128,1024]{3,2,1,0:T(8,128)} %bitcast.12, f32[1024,128]{1,0:T(8,128)} %right_ref.3), custom_call_target="tpu_custom_call" | custom-call | flops 1073741824 | bytes 4194304 | tf_op jit(solution)/shard_map/load/pallas_call | solution.py:88
  10.6 24.2 %all_to_all.35.refs_0_ = f32[8,128,128]{2,1,0:T(8,128)S(1)} all-to-all(f32[8,128,128]{2,1,0:T(8,128)S(1)} %add.5), channel_id=1, replica_groups=mesh['y'=4,'x'=4,'z'=8,'core'=2] {'z'}, dimensions={0} | all-to-all | bytes 1048576 | tf_op jit(solution)/shard_map/all_to_all | solution.py:30
  34.9 20.3 %all_to_all.36.left_ref = f32[8,128,128]{2,1,0:T(8,128)S(1)} all-to-all(f32[8,128,128]{2,1,0:T(8,128)S(1)} %total.4), channel_id=1, replica_groups=mesh['y'=4,'x'=4,'z'=8,'core'=2] {'z'}, dimensions={0} | all-to-all | bytes 1048576 | tf_op jit(solution)/shard_map/all_to_all | solution.py:30
  55.1 0.6 collective-permute-start.1
  55.7 1.1 pull.2.refs_0_
  56.9 0.4 collective-permute-done.1.left_ref
  57.2 1.2 pull.3
  58.4 17.3 %all_to_all.37.refs_0_ = f32[16,64,128]{2,1,0:T(8,128)S(1)} all-to-all(f32[16,64,128]{2,1,0:T(8,128)S(1)} %bitcast.5), channel_id=1, replica_groups=mesh['y'=4,'x'=4,'z'=8,'core'=2] {'y','x'}, dimensions={0} | all-to-all | bytes 1048576 | tf_op jit(solution)/shard_map/all_to_all | solution.py:30
  75.7 13.4 %all_to_all.38 = f32[16,64,128]{2,1,0:T(8,128)S(1)} all-to-all(f32[16,64,128]{2,1,0:T(8,128)S(1)} %total.5), channel_id=1, replica_groups=mesh['y'=4,'x'=4,'z'=8,'core'=2] {'y','x'}, dimensions={0} | all-to-all | bytes 1048576 | tf_op jit(solution)/shard_map/all_to_all | solution.py:30
  89.2 0.7 gram.1.refs_4_.refs_0_
  89.9 2.4 %project.3 = f32[8,128,128]{2,1,0:T(8,128)S(1)} custom-call(f32[1024,128]{1,0:T(8,128)S(1)} %bitcast.7, bf16[8,128,1024]{2,1,0:T(8,128)(2,1)S(1)} %get-tuple-element.17.high_ref.refs_1_, bf16[8,128,1024]{2,1,0:T(8,128)(2,1)S(1)} %get-tuple-element.18.low_ref.refs_2_, bf16[8,128,1024]{2,1,0:T(8,128)(2,1)S(1)} %get-tuple-element.22.refs_3_, ...), custom_call_target="tpu_custom_call" | custom-call | flops 2147483648 | bytes 4194304 | tf_op jit(solution)/shard_map/project/pallas_call | solution.py:130
  92.3 2.4 %collective-permute-start.2 = (f32[8,128,128]{2,1,0:T(8,128)S(1)}, f32[8,128,128]{2,1,0:T(8,128)S(1)}, u32[]{:S(2)}, u32[]{:S(2)}) collective-permute-start(f32[8,128,128]{2,1,0:T(8,128)S(1)} %project.3), channel_id=1, source_target_pairs={{0,1},{1,0},{2,3},{3,2},{4,5},{5,4},{6,7},{7,6},{8,9},{9,8},{10,11... | collective-permute-start | bytes 1572872 | tf_op jit(solution)/shard_map/ppermute | solution.py:26
  95.0 2.4 %project.2.refs_0_ = f32[8,128,128]{2,1,0:T(8,128)S(1)} custom-call(f32[1024,128]{1,0:T(8,128)S(1)} %bitcast.8, bf16[8,128,1024]{2,1,0:T(8,128)(2,1)S(1)} %get-tuple-element.19.high_ref.refs_1_, bf16[8,128,1024]{2,1,0:T(8,128)(2,1)S(1)} %get-tuple-element.20.low_ref.refs_2_, bf16[8,128,1024]{2,1,0:T(8,128)(2,1)S(1)} %get-tuple-element.21.refs_3_, ...), custom_call_target="tpu_custom_call" | custom-call | flops 2147483648 | bytes 4194304 | tf_op jit(solution)/shard_map/project/pallas_call | solution.py:130
  97.6 0.8 add.7
  98.4 3.5 %all-to-all-start.4 = ((f32[8,128,128]{2,1,0:T(8,128)}), f32[8,128,128]{2,1,0:T(8,128)S(1)}, u32[]{:S(2)}, u32[]{:S(2)}) async-start(f32[8,128,128]{2,1,0:T(8,128)} %add.7), calls=%async_computation.4 | async-start | bytes 1048576 | tf_op jit(solution)/shard_map/all_to_all | solution.py:30
  101.9 2.3 %collective-permute-start.4 = (f32[80,128]{1,0:T(8,128)S(1)}, f32[80,128]{1,0:T(8,128)S(1)}, u32[]{:S(2)}, u32[]{:S(2)}) collective-permute-start(f32[80,128]{1,0:T(8,128)S(1)} %add.6.refs_2_.refs_0_), channel_id=1, source_target_pairs={{0,4},{2,6},{4,0},{6,2},{8,12},{10,14},{12,8},{14,10},{1,5},{3,7},... | collective-permute-start | bytes 122888 | tf_op jit(solution)/shard_map/ppermute | solution.py:385
  104.2 7.6 %collective-permute-done.4.refs_1_ = f32[80,128]{1,0:T(8,128)S(1)} collective-permute-done((f32[80,128]{1,0:T(8,128)S(1)}, f32[80,128]{1,0:T(8,128)S(1)}, u32[]{:S(2)}, u32[]{:S(2)}) %collective-permute-start.4) | collective-permute-done | bytes 40992 | tf_op jit(solution)/shard_map/ppermute | solution.py:385
  111.8 6.8 %collective-permute-start.5 = (f32[80,128]{1,0:T(8,128)S(1)}, f32[80,128]{1,0:T(8,128)S(1)}, u32[]{:S(2)}, u32[]{:S(2)}) collective-permute-start(f32[80,128]{1,0:T(8,128)S(1)} %add.8.refs_0_), channel_id=1, source_target_pairs={{0,8},{2,10},{4,12},{6,14},{8,0},{10,2},{12,4},{14,6},{1,9},{3,11}... | collective-permute-start | bytes 122888 | tf_op jit(solution)/shard_map/ppermute | solution.py:385
  118.6 2.2 %collective-permute-done.5.refs_1_ = f32[80,128]{1,0:T(8,128)S(1)} collective-permute-done((f32[80,128]{1,0:T(8,128)S(1)}, f32[80,128]{1,0:T(8,128)S(1)}, u32[]{:S(2)}, u32[]{:S(2)}) %collective-permute-start.5) | collective-permute-done | bytes 40992 | tf_op jit(solution)/shard_map/ppermute | solution.py:385
  120.8 4.1 %collective-permute-start.6 = (f32[80,128]{1,0:T(8,128)S(1)}, f32[80,128]{1,0:T(8,128)S(1)}, u32[]{:S(2)}, u32[]{:S(2)}) collective-permute-start(f32[80,128]{1,0:T(8,128)S(1)} %add.9.refs_0_), channel_id=1, source_target_pairs={{0,1},{1,0},{2,3},{3,2},{4,5},{5,4},{6,7},{7,6},{8,9},{9,8},{10,11... | collective-permute-start | bytes 122888 | tf_op jit(solution)/shard_map/ppermute | solution.py:26
  124.9 0.9 collective-permute-done.6.refs_1_
  125.7 3.7 %factor.1 = (f32[128,128]{1,0:T(8,128)S(1)}, f32[128,128]{1,0:T(8,128)S(1)}) custom-call(f32[80,128]{1,0:T(8,128)S(1)} %add.9.refs_0_, f32[80,128]{1,0:T(8,128)S(1)} %collective-permute-done.6.refs_1_), custom_call_target="tpu_custom_call" | custom-call | flops 3600000000 | bytes 512 | tf_op jit(solution)/shard_map/factor/pallas_call | solution.py:285
  129.4 0.7 middle.1
  130.1 0.4 collective-permute-start.7
  130.6 0.8 collective-permute-done.7.refs_1_
  131.4 11.5 %all_to_all.39.refs_0_ = f32[16,40,128]{2,1,0:T(8,128)S(1)} all-to-all(f32[16,40,128]{2,1,0:T(8,128)S(1)} %pair.1), channel_id=1, replica_groups=mesh['y'=4,'x'=4,'z'=8,'core'=2] {'y','x'}, dimensions={0} | all-to-all | bytes 655360 | tf_op jit(solution)/shard_map/all_to_all | solution.py:30
  143.0 14.9 %all_to_all.40.refs_0_ = f32[8,40,128]{2,1,0:T(8,128)S(1)} all-to-all(f32[8,40,128]{2,1,0:T(8,128)S(1)} %total.6), channel_id=1, replica_groups=mesh['y'=4,'x'=4,'z'=8,'core'=2] {'z'}, dimensions={0} | all-to-all | bytes 327680 | tf_op jit(solution)/shard_map/all_to_all | solution.py:30
  157.9 3.0 %collective-permute-start.8 = (f32[40,128]{1,0:T(8,128)S(1)}, f32[40,128]{1,0:T(8,128)S(1)}, u32[]{:S(2)}, u32[]{:S(2)}) collective-permute-start(f32[40,128]{1,0:T(8,128)S(1)} %bitcast.9), channel_id=1, source_target_pairs={{0,1},{1,0},{2,3},{3,2},{4,5},{5,4},{6,7},{7,6},{8,9},{9,8},{10,11... | collective-permute-start | bytes 61448 | tf_op jit(solution)/shard_map/ppermute | solution.py:26
  160.8 0.8 collective-permute-done.8.refs_2_
  161.7 4.6 %last.1 = (f32[128,128]{1,0:T(8,128)}, f32[128,128]{1,0:T(8,128)}) custom-call(s32[1]{0:T(128)} %bitcast.half_ref.refs_0_, f32[40,128]{1,0:T(8,128)S(1)} %bitcast.10, f32[40,128]{1,0:T(8,128)S(1)} %collective-permute-done.8.refs_2_, f32[128,128]{1,0:T(8,128)S(1)} %get-tuple-element.26.refs_3_, f32[128,128]{1,0:T(8,128)S(1)} %get-tuple-element.27.refs_4_), custom_call_target="tpu_custom_call" | custom-call | flops 4600000000 | bytes 512 | tf_op jit(solution)/shard_map/last/pallas_call | solution.py:285
  (14 shorter events, 0.7 us)
Async XLA Ops:
  3.9 6.6 %collective-permute-start = (f32[8,128,128]{2,1,0:T(8,128)S(1)}, f32[8,128,128]{2,1,0:T(8,128)S(1)}, u32[]{:S(2)}, u32[]{:S(2)}) collective-permute-start(f32[8,128,128]{2,1,0:T(8,128)S(1)} %get-tuple-element.16), channel_id=1, source_target_pairs={{0,1},{1,0},{2,3},{3,2},{4,5},{5,4},{6,7},{7,6},{8,9},{9,8},{10,11... | collective-permute-start | bytes 1572872 | tf_op jit(solution)/shard_map/ppermute | solution.py:26
  55.1 2.1 %collective-permute-start.1 = (f32[8,128,128]{2,1,0:T(8,128)S(1)}, f32[8,128,128]{2,1,0:T(8,128)S(1)}, u32[]{:S(2)}, u32[]{:S(2)}) collective-permute-start(f32[8,128,128]{2,1,0:T(8,128)S(1)} %all_to_all.36.left_ref), channel_id=1, source_target_pairs={{0,1},{1,0},{2,3},{3,2},{4,5},{5,4},{6,7},{7,6},{8,9},{9,8},{10,11... | collective-permute-start | bytes 1572872 | tf_op jit(solution)/shard_map/ppermute | solution.py:26
  92.3 5.3 %collective-permute-start.2 = (f32[8,128,128]{2,1,0:T(8,128)S(1)}, f32[8,128,128]{2,1,0:T(8,128)S(1)}, u32[]{:S(2)}, u32[]{:S(2)}) collective-permute-start(f32[8,128,128]{2,1,0:T(8,128)S(1)} %project.3), channel_id=1, source_target_pairs={{0,1},{1,0},{2,3},{3,2},{4,5},{5,4},{6,7},{7,6},{8,9},{9,8},{10,11... | collective-permute-start | bytes 1572872 | tf_op jit(solution)/shard_map/ppermute | solution.py:26
  94.7 2.9 %collective-permute-start.3 = (f32[80,128]{1,0:T(8,128)S(1)}, f32[80,128]{1,0:T(8,128)S(1)}, u32[]{:S(2)}, u32[]{:S(2)}) collective-permute-start(f32[80,128]{1,0:T(8,128)S(1)} %gram.1.refs_4_.refs_0_), channel_id=1, source_target_pairs={{0,2},{2,0},{4,6},{6,4},{8,10},{10,8},{12,14},{14,12},{1,3},{3,1},... | collective-permute-start | bytes 122888 | tf_op jit(solution)/shard_map/ppermute | solution.py:385
  98.4 31.0 %all-to-all-start.4 = ((f32[8,128,128]{2,1,0:T(8,128)}), f32[8,128,128]{2,1,0:T(8,128)S(1)}, u32[]{:S(2)}, u32[]{:S(2)}) async-start(f32[8,128,128]{2,1,0:T(8,128)} %add.7), calls=%async_computation.4 | async-start | bytes 1048576 | tf_op jit(solution)/shard_map/all_to_all | solution.py:30
  101.9 9.9 %collective-permute-start.4 = (f32[80,128]{1,0:T(8,128)S(1)}, f32[80,128]{1,0:T(8,128)S(1)}, u32[]{:S(2)}, u32[]{:S(2)}) collective-permute-start(f32[80,128]{1,0:T(8,128)S(1)} %add.6.refs_2_.refs_0_), channel_id=1, source_target_pairs={{0,4},{2,6},{4,0},{6,2},{8,12},{10,14},{12,8},{14,10},{1,5},{3,7},... | collective-permute-start | bytes 122888 | tf_op jit(solution)/shard_map/ppermute | solution.py:385
  111.8 9.0 %collective-permute-start.5 = (f32[80,128]{1,0:T(8,128)S(1)}, f32[80,128]{1,0:T(8,128)S(1)}, u32[]{:S(2)}, u32[]{:S(2)}) collective-permute-start(f32[80,128]{1,0:T(8,128)S(1)} %add.8.refs_0_), channel_id=1, source_target_pairs={{0,8},{2,10},{4,12},{6,14},{8,0},{10,2},{12,4},{14,6},{1,9},{3,11}... | collective-permute-start | bytes 122888 | tf_op jit(solution)/shard_map/ppermute | solution.py:385
  120.8 4.9 %collective-permute-start.6 = (f32[80,128]{1,0:T(8,128)S(1)}, f32[80,128]{1,0:T(8,128)S(1)}, u32[]{:S(2)}, u32[]{:S(2)}) collective-permute-start(f32[80,128]{1,0:T(8,128)S(1)} %add.9.refs_0_), channel_id=1, source_target_pairs={{0,1},{1,0},{2,3},{3,2},{4,5},{5,4},{6,7},{7,6},{8,9},{9,8},{10,11... | collective-permute-start | bytes 122888 | tf_op jit(solution)/shard_map/ppermute | solution.py:26
  130.1 1.3 collective-permute-start.7
  157.9 3.8 %collective-permute-start.8 = (f32[40,128]{1,0:T(8,128)S(1)}, f32[40,128]{1,0:T(8,128)S(1)}, u32[]{:S(2)}, u32[]{:S(2)}) collective-permute-start(f32[40,128]{1,0:T(8,128)S(1)} %bitcast.9), channel_id=1, source_target_pairs={{0,1},{1,0},{2,3},{3,2},{4,5},{5,4},{6,7},{7,6},{8,9},{9,8},{10,11... | collective-permute-start | bytes 61448 | tf_op jit(solution)/shard_map/ppermute | solution.py:26

commit v6 on v5

--- a/solution.py
+++ b/solution.py
@@ -53,8 +53,7 @@
     return ref[place : place + height].reshape(-1, ref.shape[-1])
 
 
-def load_kernel(half_ref, slab_ref, right_ref, out_ref, *refs):
-    part_refs, (pair_ref, block_ref, right_buffer, sems) = refs[:COUNT], refs[COUNT:]
+def multiply_kernel(half_ref, slab_ref, right_ref, out_ref, pair_ref, block_ref, right_buffer, sems):
     half, zs, wide = half_ref[0], block_ref.shape[0], out_ref.shape[-1]
     right_copy = pltpu.make_async_copy(right_ref, right_buffer, sems.at[zs])
     right_copy.start()
@@ -71,36 +70,90 @@
     for place in range(0, zs, STEP):
         for copy in copies[place : place + STEP]:
             copy.wait()
-        parts = split(rows_of(block_ref, place, STEP), COUNT)
-        for part, ref in zip(parts, part_refs):
-            ref[place : place + STEP] = part.reshape(STEP, -1, ref.shape[-1])
-        first = dot(parts[0], pair_ref[...])
-        value = first[:, :wide] + (first[:, wide:] + dot(parts[1], pair_ref[:, :wide]))
+        high, low = split(rows_of(block_ref, place, STEP), 2)
+        first = dot(high, pair_ref[...])
+        value = first[:, :wide] + (first[:, wide:] + dot(low, pair_ref[:, :wide]))
         out_ref[place : place + STEP] = value.reshape(STEP, -1, wide)
 
 
-def load(slab, right, half):
+def multiply(slab, right, half):
     zs, _, height, depth = slab.shape
     wide = right.shape[1]
-    memory = pl.BlockSpec(memory_space=pltpu.VMEM)
-    anywhere = pl.BlockSpec(memory_space=pltpu.HBM)
-    part = pltpu.VMEM((zs, height, depth), jnp.bfloat16)
-    product, *parts = pl.pallas_call(
-        load_kernel,
-        in_specs=[pl.BlockSpec(memory_space=pltpu.SMEM), anywhere, anywhere],
-        out_specs=[memory] * (1 + COUNT),
+    high_memory = pl.BlockSpec(memory_space=pltpu.HBM)
+    return pl.pallas_call(
+        multiply_kernel,
+        in_specs=[pl.BlockSpec(memory_space=pltpu.SMEM), high_memory, high_memory],
+        out_specs=pl.BlockSpec(memory_space=pltpu.VMEM),
         scratch_shapes=[
             pltpu.VMEM((depth, 2 * wide), jnp.bfloat16),
             pltpu.VMEM((zs, height, depth), jnp.float32),
             pltpu.VMEM((depth, wide), jnp.float32),
             pltpu.SemaphoreType.DMA((zs + 1,)),
         ],
-        out_shape=[jax.ShapeDtypeStruct((zs, height, wide), jnp.float32)] + [part] * COUNT,
+        out_shape=jax.ShapeDtypeStruct((zs, height, wide), jnp.float32),
         compiler_params=params(),
         cost_estimate=cost(zs * height, depth, wide, 4),
-        name="load",
+        name="multiply",
     )(half, keep(slab, pltpu.HBM), keep(right, pltpu.HBM))
-    return product, parts
+
+
+def parts_kernel(turn, core_ref, slab_ref, *refs):
+    block_ref, sems = refs[-2:]
+    part_refs = refs[-2 - 2 * COUNT : -2]
+    zs, core = block_ref.shape[0], core_ref[0]
+
+    @pl.when(core == turn)
+    def _():
+        copies = [
+            [
+                pltpu.make_async_copy(
+                    slab_ref.at[place, half], block_ref.at[place, half], sems.at[place, half]
+                )
+                for half in range(2)
+            ]
+            for place in range(zs)
+        ]
+        for pair in copies:
+            for copy in pair:
+                copy.start()
+        for place in range(zs):
+            for half, refs in ((turn, part_refs[:COUNT]), (1 - turn, part_refs[COUNT:])):
+                copies[place][half].wait()
+                for part, ref in zip(split(block_ref[place, half], COUNT), refs):
+                    ref[place] = part
+
+
+def parts_of(slab, core, turn, before=(), passed=None):
+    zs, _, height, depth = slab.shape
+    high_memory = pl.BlockSpec(memory_space=pltpu.HBM)
+    memory = pl.BlockSpec(memory_space=pltpu.VMEM)
+    count = 2 * COUNT
+    through = [] if passed is None else [passed]
+    shapes = [pltpu.VMEM((zs, height, depth), jnp.bfloat16)] * count
+    shapes += [jax.ShapeDtypeStruct(value.shape, value.dtype) for value in through]
+    place = 2 + len(through)
+    aliases = {2: count} if through else {}
+    aliases |= {place + i: i for i in range(len(before))}
+
+    def kernel(*refs):
+        outs = refs[place + len(before) :]
+        parts_kernel(turn, *refs[:2], *outs[:count], *outs[-2:])
+
+    return pl.pallas_call(
+        kernel,
+        in_specs=[pl.BlockSpec(memory_space=pltpu.SMEM), high_memory]
+        + [memory] * (len(through) + len(before)),
+        out_specs=[memory] * (count + len(through)),
+        scratch_shapes=[
+            pltpu.VMEM((zs, 2, height, depth), jnp.float32),
+            pltpu.SemaphoreType.DMA((zs, 2)),
+        ],
+        out_shape=shapes,
+        input_output_aliases=aliases,
+        compiler_params=params(),
+        cost_estimate=cost(2 * zs * height, depth, 128, 4),
+        name="parts",
+    )(core, keep(slab, pltpu.HBM), *through, *[keep(part, pltpu.VMEM) for part in before])
 
 
 def cost(height, depth, wide, times):
@@ -301,14 +354,9 @@
     return small_call(kernel, [shape], name, 100, operands, after=after)[0]
 
 
-def gram_kernel(value_ref, out_ref):
+def gram_kernel(core_ref, value_ref, own_ref, other_ref):
     value = value_ref[...]
-    out_ref[...] = pack(dot(value, value, CONTRACT, HIGHEST))
-
-
-def factor_kernel(first_ref, second_ref, upper_ref, lower_ref):
-    gram = unpack(first_ref[...] + second_ref[...])
-    upper_ref[...], lower_ref[...] = eliminate(gram, floor_of(gram))
+    store_halves(core_ref[0], dot(value, value, CONTRACT, HIGHEST), own_ref, other_ref)
 
 
 def add_kernel(first_ref, second_ref, out_ref):
@@ -335,11 +383,30 @@
     return plain_call(functools.partial(total_kernel, scale), shape, "total", pieces)
 
 
-def middle_kernel(core_ref, pieces_ref, lower_ref, inner_ref, own_ref, other_ref):
-    sketch = pieces_ref[0]
+def join_kernel(product_ref, sent_ref, own_ref, other_ref, out_ref):
+    height = product_ref.shape[1]
+    out_ref[:, :height] = product_ref[...] + sent_ref[...]
+    gram = own_ref[...] + other_ref[...]
+    out_ref[:, height:] = jnp.broadcast_to(gram[None], (out_ref.shape[0],) + gram.shape)
+
+
+def tail_kernel(start, pieces_ref, out_ref):
+    value = pieces_ref[0, start:]
     for place in range(1, pieces_ref.shape[0]):
-        sketch += pieces_ref[place]
-    inner = dot(sketch, lower_ref[...], TRANSPOSED, HIGHEST)
+        value += pieces_ref[place, start:]
+    out_ref[...] = value
+
+
+def middle_kernel(
+    core_ref, pieces_ref, pulled_own_ref, pulled_other_ref, inner_ref, before_ref, own_ref, other_ref
+):
+    gram = load_halves(core_ref[0], pulled_own_ref[...], pulled_other_ref[...])
+    before_ref[...], lower = eliminate(gram, floor_of(gram))
+    height = inner_ref.shape[0]
+    sketch = pieces_ref[0, :height]
+    for place in range(1, pieces_ref.shape[0]):
+        sketch += pieces_ref[place, :height]
+    inner = dot(sketch, lower, TRANSPOSED, HIGHEST)
     inner_ref[...] = inner
     store_halves(core_ref[0], dot(inner, inner, CONTRACT, HIGHEST), own_ref, other_ref)
 
@@ -364,35 +431,38 @@
     far = 1 - core
     slab = slab.reshape(zs, 2, -1, columns)
     square = (wide, wide)
-    packed = (5 * wide // 8, wide)
     halves = [(5 * wide // 16, wide)] * 2
 
-    product, far_parts = load(slab, test_matrix, far)
-    sent = swap(product)
-    product, parts = load(slab, test_matrix, core)
-    part = add(product, sent)
+    sent = swap(multiply(slab, test_matrix, far))
+    product = multiply(slab, test_matrix, core)
+    made = parts_of(slab, core, 1)
+    part = add(product, sent, made[:1])
     own = exchange(total(exchange(part, "z"), zs), "z")
 
+    *made, own = parts_of(slab, core, 0, made, own)
+    parts, far_parts = made[:COUNT], made[COUNT:]
     other = swap(own)
     part = pull(other, far_parts, pull(own, parts))
     pieces = total(exchange(part.reshape(row_count, -1, wide), ROW), row_count, 1.0 / row_total)
     pulled = exchange(pieces, ROW).reshape(-1, wide)
 
-    gram = small_call(gram_kernel, [packed], "gram", 700, [pulled])[0]
-    grams, distance = [gram], 1
-    while distance < zs:
-        partners = [(place, place ^ distance) for place in range(zs)]
-        grams.append(add(grams[-1], lax.ppermute(grams[-1], "z", partners)))
-        distance *= 2
-    pair = [grams[-1], swap(grams[-1])]
-    before, lower = small_call(factor_kernel, [square] * 2, "factor", 3600, pair)
-
-    sent = swap(project(pulled, far_parts, grams[:1]))
-    part = add(project(pulled, parts, grams[:1]), sent, grams[1:2])
-    pieces = exchange(part, "z")
-
-    inner, own, other = small_call(
-        middle_kernel, [part.shape[1:]] + halves, "middle", 650, [pieces, lower], [core]
+    own, other = small_call(gram_kernel, halves, "gram", 700, [pulled], [core])
+    other = swap(other)
+    sent = swap(project(pulled, far_parts))
+    product = project(pulled, parts)
+    height = product.shape[1]
+    shape = (zs, height + own.shape[0], wide)
+    joined = plain_call(join_kernel, shape, "join", product, sent, own, other)
+    pieces = exchange(joined, "z")
+    own = plain_call(functools.partial(tail_kernel, height), own.shape, "tail", pieces)
+
+    inner, before, own, other = small_call(
+        middle_kernel,
+        [(height, wide), square] + halves,
+        "middle",
+        4300,
+        [pieces, own, swap(own)],
+        [core],
     )
     copies = plain_call(pair_kernel, (row_count,) + own.shape, "pair", own, swap(other))
     copies = total(exchange(copies, ROW), zs)

time: 167 us -> 161 us (0.964)
  blocking collectives: 102 us -> 116 us
  starting transfers between devices: 26.6 us -> 14.1 us
  waiting for transfers between devices: 12.9 us -> 2.94 us
  Pallas kernels: 24.4 us -> 27.5 us
    all_to_all x6 -> x7, blocking collectives: 102 us -> 116 us  [exchange(): return lax.all_to_all(value, axes, 0, 0, tiled=False)]
    ppermute x3 -> x0, waiting for transfers between devices: 9.98 us -> none  [local(): grams.append(add(grams[-1], lax.ppermute(grams[-1], 'z', partners)))]
    ppermute x3 -> x0, starting transfers between devices: 9.32 us -> none  [local(): grams.append(add(grams[-1], lax.ppermute(grams[-1], 'z', partners)))]
    pallas_call x2 -> x4, Pallas kernels: 6.52 us -> 10.4 us  [the longest x2 6.4 us: multiply(): pl.pallas_call(multiply_kernel, in_specs=[pl.BlockSpec(memory_space=pltpu...]
    all_to_all x1 -> x0, starting transfers between devices: 3.49 us -> none  [exchange(): return lax.all_to_all(value, axes, 0, 0, tiled=False)]
    pallas_call x14 -> x11, Pallas kernels: 10.8 us -> 10 us  [small_call(): pl.pallas_call(without(kernel, len(scalars) + len(operands), len(after)),...]
    ppermute x6 -> x7, starting transfers between devices: 13.8 us -> 14.1 us  [swap(): return lax.ppermute(value, 'core', SWAP)]
  transfers between devices with their start and end apart: 10 -> 7, of which waited for: 7 -> 4; matrix products, arithmetic and copies ran while one was open for 0% -> 0% of each run, Pallas kernels for 6% -> 7%
where the time goes in v6:
time: 161 us
  blocking collectives  116 us (72%)
  Pallas kernels  27.5 us (17%)
  starting transfers between devices  14.1 us (9%)
  waiting for transfers between devices  2.94 us (2%)
    all_to_all x7, blocking collectives, exchange(): return lax.all_to_all(value, axes, 0, 0, tiled=False)  116 us
    ppermute x7, starting transfers between devices, swap(): return lax.ppermute(value, 'core', SWAP)  14.1 us
    pallas_call x11, Pallas kernels, small_call(): pl.pallas_call(without(kernel, len(scalars) + len(operands), len(after)),...  10 us
    pallas_call x2, Pallas kernels, multiply(): pl.pallas_call(multiply_kernel, in_specs=[pl.BlockSpec(memory_space=pltpu...  6.4 us
    pallas_call x2, Pallas kernels, project(): pl.pallas_call(without(project_kernel, 1 + COUNT, len(after)), in_specs=[...  4.79 us
    pallas_call x2, Pallas kernels, parts_of(): pl.pallas_call(kernel, in_specs=[pl.BlockSpec(memory_space=pltpu.SMEM), h...  3.97 us
  transfers between devices with their start and end apart: 7, of which 4 were waited for; matrix products, arithmetic and copies ran while one was open for 0% of the time, Pallas kernels for 7%

profile of v6, /device:TPU:1, one launch (start us, length us, event | category | flops | bytes accessed | tf_op | source)
XLA Modules:
  0.0 161.0 jit_solution(5301328408039541035)
XLA Ops:
  0.6 3.2 %multiply.3 = f32[8,128,128]{2,1,0:T(8,128)S(1)} custom-call(s32[1]{0:T(128)S(6)} %sub.3.half_ref, f32[8,2,128,1024]{3,2,1,0:T(8,128)} %bitcast.11, f32[1024,128]{1,0:T(8,128)} %right_ref.3), custom_call_target="tpu_custom_call" | custom-call | flops 1073741824 | bytes 4194304 | tf_op jit(solution)/shard_map/multiply/pallas_call | solution.py:83
  3.8 3.3 %collective-permute-start = (f32[8,128,128]{2,1,0:T(8,128)S(1)}, f32[8,128,128]{2,1,0:T(8,128)S(1)}, u32[]{:S(2)}, u32[]{:S(2)}) collective-permute-start(f32[8,128,128]{2,1,0:T(8,128)S(1)} %multiply.3), channel_id=1, source_target_pairs={{0,1},{1,0},{2,3},{3,2},{4,5},{5,4},{6,7},{7,6},{8,9},{9,8},{10,11... | collective-permute-start | bytes 1572872 | tf_op jit(solution)/shard_map/ppermute | solution.py:26
  7.2 3.2 %multiply.2.refs_0_ = f32[8,128,128]{2,1,0:T(8,128)S(1)} custom-call(s32[1]{0:T(128)} %bitcast.half_ref.refs_0_, f32[8,2,128,1024]{3,2,1,0:T(8,128)} %bitcast.12, f32[1024,128]{1,0:T(8,128)} %right_ref.3), custom_call_target="tpu_custom_call" | custom-call | flops 1073741824 | bytes 4194304 | tf_op jit(solution)/shard_map/multiply/pallas_call | solution.py:83
  10.4 3.8 %parts.2 = (bf16[8,128,1024]{2,1,0:T(8,128)(2,1)S(1)}, bf16[8,128,1024]{2,1,0:T(8,128)(2,1)S(1)}, bf16[8,128,1024]{2,1,0:T(8,128)(2,1)S(1)}, bf16[8,128,1024]{2,...) custom-call(s32[1]{0:T(128)} %bitcast.half_ref.refs_0_, ...), custom_call_target="tpu_custom_call" | custom-call | flops 2147483648 | bytes 8388608 | tf_op jit(solution)/shard_map/parts/pallas_call | solution.py:142
  14.2 0.1 add.1
  14.3 21.1 %all_to_all.35.refs_0_ = f32[8,128,128]{2,1,0:T(8,128)S(1)} all-to-all(f32[8,128,128]{2,1,0:T(8,128)S(1)} %add.1), channel_id=1, replica_groups=mesh['y'=4,'x'=4,'z'=8,'core'=2] {'z'}, dimensions={0} | all-to-all | bytes 1048576 | tf_op jit(solution)/shard_map/all_to_all | solution.py:30
  35.4 19.0 %all_to_all.36.refs_2_ = f32[8,128,128]{2,1,0:T(8,128)S(1)} all-to-all(f32[8,128,128]{2,1,0:T(8,128)S(1)} %total.4), channel_id=1, replica_groups=mesh['y'=4,'x'=4,'z'=8,'core'=2] {'z'}, dimensions={0} | all-to-all | bytes 1048576 | tf_op jit(solution)/shard_map/all_to_all | solution.py:30
  54.4 0.1 parts.3
  54.6 2.8 %collective-permute-start.1 = (f32[8,128,128]{2,1,0:T(8,128)S(1)}, f32[8,128,128]{2,1,0:T(8,128)S(1)}, u32[]{:S(2)}, u32[]{:S(2)}) collective-permute-start(f32[8,128,128]{2,1,0:T(8,128)S(1)} %get-tuple-element.27.left_ref), channel_id=1, source_target_pairs={{0,1},{1,0},{2,3},{3,2},{4,5},{5,4},{6,7},{7,6},{8,9},{9,8},{10,11... | collective-permute-start | bytes 1572872 | tf_op jit(solution)/shard_map/ppermute | solution.py:26
  57.4 1.1 pull.2.refs_0_
  58.5 0.4 collective-permute-done.1.left_ref
  58.9 1.1 pull.3
  60.1 17.3 %all_to_all.37.refs_0_ = f32[16,64,128]{2,1,0:T(8,128)S(1)} all-to-all(f32[16,64,128]{2,1,0:T(8,128)S(1)} %bitcast.5), channel_id=1, replica_groups=mesh['y'=4,'x'=4,'z'=8,'core'=2] {'y','x'}, dimensions={0} | all-to-all | bytes 1048576 | tf_op jit(solution)/shard_map/all_to_all | solution.py:30
  77.4 0.1 total.5
  77.4 13.4 %all_to_all.38 = f32[16,64,128]{2,1,0:T(8,128)S(1)} all-to-all(f32[16,64,128]{2,1,0:T(8,128)S(1)} %total.5), channel_id=1, replica_groups=mesh['y'=4,'x'=4,'z'=8,'core'=2] {'y','x'}, dimensions={0} | all-to-all | bytes 1048576 | tf_op jit(solution)/shard_map/all_to_all | solution.py:30
  90.9 2.4 %project.3 = f32[8,128,128]{2,1,0:T(8,128)S(1)} custom-call(f32[1024,128]{1,0:T(8,128)S(1)} %bitcast.6, bf16[8,128,1024]{2,1,0:T(8,128)(2,1)S(1)} %get-tuple-element.28.high_ref.refs_1_, bf16[8,128,1024]{2,1,0:T(8,128)(2,1)S(1)} %get-tuple-element.29.low_ref.refs_2_, bf16[8,128,1024]{2,1,0:T(8,128)(2,1)S(1)} %get-tuple-element.33.refs_3_), custom_call_target="tpu_custom_call" | custom-call | flops 2147483648 | bytes 4194304 | tf_op jit(solution)/shard_map/project/pallas_call | solution.py:183
  93.2 2.4 %collective-permute-start.2 = (f32[8,128,128]{2,1,0:T(8,128)S(1)}, f32[8,128,128]{2,1,0:T(8,128)S(1)}, u32[]{:S(2)}, u32[]{:S(2)}) collective-permute-start(f32[8,128,128]{2,1,0:T(8,128)S(1)} %project.3), channel_id=1, source_target_pairs={{0,1},{1,0},{2,3},{3,2},{4,5},{5,4},{6,7},{7,6},{8,9},{9,8},{10,11... | collective-permute-start | bytes 1572872 | tf_op jit(solution)/shard_map/ppermute | solution.py:26
  95.7 0.7 gram.1
  96.4 0.1 collective-permute-start.3
  96.5 2.4 %project.2.refs_0_ = f32[8,128,128]{2,1,0:T(8,128)S(1)} custom-call(f32[1024,128]{1,0:T(8,128)S(1)} %bitcast.8, bf16[8,128,1024]{2,1,0:T(8,128)(2,1)S(1)} %get-tuple-element.30.high_ref.refs_1_, bf16[8,128,1024]{2,1,0:T(8,128)(2,1)S(1)} %get-tuple-element.31.low_ref.refs_2_, bf16[8,128,1024]{2,1,0:T(8,128)(2,1)S(1)} %get-tuple-element.32.refs_3_), custom_call_target="tpu_custom_call" | custom-call | flops 2147483648 | bytes 4194304 | tf_op jit(solution)/shard_map/project/pallas_call | solution.py:183
  98.9 0.1 join.1
  99.0 22.6 %all_to_all.39.refs_0_.refs_1_ = f32[8,168,128]{2,1,0:T(8,128)S(1)} all-to-all(f32[8,168,128]{2,1,0:T(8,128)S(1)} %join.1), channel_id=1, replica_groups=mesh['y'=4,'x'=4,'z'=8,'core'=2] {'z'}, dimensions={0} | all-to-all | bytes 1376256 | tf_op jit(solution)/shard_map/all_to_all | solution.py:30
  121.6 2.2 %collective-permute-start.4 = (f32[40,128]{1,0:T(8,128)S(1)}, f32[40,128]{1,0:T(8,128)S(1)}, u32[]{:S(2)}, u32[]{:S(2)}) collective-permute-start(f32[40,128]{1,0:T(8,128)S(1)} %tail.1.refs_2_), channel_id=1, source_target_pairs={{0,1},{1,0},{2,3},{3,2},{4,5},{5,4},{6,7},{7,6},{8,9},{9,8},{10,11... | collective-permute-start | bytes 61448 | tf_op jit(solution)/shard_map/ppermute | solution.py:26
  123.8 0.8 collective-permute-done.4.refs_3_
  124.7 4.3 %middle.1 = (f32[128,128]{1,0:T(8,128)S(1)}, f32[128,128]{1,0:T(8,128)S(1)}, f32[40,128]{1,0:T(8,128)S(1)}, f32[40,128]{1,0:T(8,128)S(1)}) custom-call(s32[1]{0:T(128)} %bitcast.half_ref.refs_0_, f32[8,168,128]{2,1,0:T(8,128)S(1)} %all_to_all.39.refs_0_.refs_1_, f32[40,128]{1,0:T(8,128)S(1)} %tail.1.refs_2_, f32[40,128]{1,0:T(8,128)S(1)} %collective-permute-done.4.refs_3_), custom_call_target="tpu_custom_call" | custom-call | flops 4300000256 | bytes 512 | tf_op jit(solution)/shard_map/middle/pallas_call | solution.py:338
  129.0 0.7 collective-permute-start.5
  129.7 0.8 collective-permute-done.5.refs_1_
  130.5 11.5 %all_to_all.40.refs_0_ = f32[16,40,128]{2,1,0:T(8,128)S(1)} all-to-all(f32[16,40,128]{2,1,0:T(8,128)S(1)} %pair.1), channel_id=1, replica_groups=mesh['y'=4,'x'=4,'z'=8,'core'=2] {'y','x'}, dimensions={0} | all-to-all | bytes 655360 | tf_op jit(solution)/shard_map/all_to_all | solution.py:30
  142.1 10.8 %all_to_all.41.refs_0_ = f32[8,40,128]{2,1,0:T(8,128)S(1)} all-to-all(f32[8,40,128]{2,1,0:T(8,128)S(1)} %total.6), channel_id=1, replica_groups=mesh['y'=4,'x'=4,'z'=8,'core'=2] {'z'}, dimensions={0} | all-to-all | bytes 327680 | tf_op jit(solution)/shard_map/all_to_all | solution.py:30
  152.9 2.6 %collective-permute-start.6 = (f32[40,128]{1,0:T(8,128)S(1)}, f32[40,128]{1,0:T(8,128)S(1)}, u32[]{:S(2)}, u32[]{:S(2)}) collective-permute-start(f32[40,128]{1,0:T(8,128)S(1)} %bitcast.9), channel_id=1, source_target_pairs={{0,1},{1,0},{2,3},{3,2},{4,5},{5,4},{6,7},{7,6},{8,9},{9,8},{10,11... | collective-permute-start | bytes 61448 | tf_op jit(solution)/shard_map/ppermute | solution.py:26
  155.5 0.8 collective-permute-done.6.refs_2_
  156.3 4.6 %last.1 = (f32[128,128]{1,0:T(8,128)}, f32[128,128]{1,0:T(8,128)}) custom-call(s32[1]{0:T(128)} %bitcast.half_ref.refs_0_, f32[40,128]{1,0:T(8,128)S(1)} %bitcast.10, f32[40,128]{1,0:T(8,128)S(1)} %collective-permute-done.6.refs_2_, f32[128,128]{1,0:T(8,128)S(1)} %get-tuple-element.38.refs_3_, f32[128,128]{1,0:T(8,128)S(1)} %get-tuple-element.39.refs_4_), custom_call_target="tpu_custom_call" | custom-call | flops 4600000000 | bytes 512 | tf_op jit(solution)/shard_map/last/pallas_call | solution.py:338
  (8 shorter events, 0.1 us)
Async XLA Ops:
  3.8 10.4 %collective-permute-start = (f32[8,128,128]{2,1,0:T(8,128)S(1)}, f32[8,128,128]{2,1,0:T(8,128)S(1)}, u32[]{:S(2)}, u32[]{:S(2)}) collective-permute-start(f32[8,128,128]{2,1,0:T(8,128)S(1)} %multiply.3), channel_id=1, source_target_pairs={{0,1},{1,0},{2,3},{3,2},{4,5},{5,4},{6,7},{7,6},{8,9},{9,8},{10,11... | collective-permute-start | bytes 1572872 | tf_op jit(solution)/shard_map/ppermute | solution.py:26
  54.6 4.4 %collective-permute-start.1 = (f32[8,128,128]{2,1,0:T(8,128)S(1)}, f32[8,128,128]{2,1,0:T(8,128)S(1)}, u32[]{:S(2)}, u32[]{:S(2)}) collective-permute-start(f32[8,128,128]{2,1,0:T(8,128)S(1)} %get-tuple-element.27.left_ref), channel_id=1, source_target_pairs={{0,1},{1,0},{2,3},{3,2},{4,5},{5,4},{6,7},{7,6},{8,9},{9,8},{10,11... | collective-permute-start | bytes 1572872 | tf_op jit(solution)/shard_map/ppermute | solution.py:26
  93.2 5.7 %collective-permute-start.2 = (f32[8,128,128]{2,1,0:T(8,128)S(1)}, f32[8,128,128]{2,1,0:T(8,128)S(1)}, u32[]{:S(2)}, u32[]{:S(2)}) collective-permute-start(f32[8,128,128]{2,1,0:T(8,128)S(1)} %project.3), channel_id=1, source_target_pairs={{0,1},{1,0},{2,3},{3,2},{4,5},{5,4},{6,7},{7,6},{8,9},{9,8},{10,11... | collective-permute-start | bytes 1572872 | tf_op jit(solution)/shard_map/ppermute | solution.py:26
  96.4 2.5 %collective-permute-start.3 = (f32[40,128]{1,0:T(8,128)S(1)}, f32[40,128]{1,0:T(8,128)S(1)}, u32[]{:S(2)}, u32[]{:S(2)}) collective-permute-start(f32[40,128]{1,0:T(8,128)S(1)} %get-tuple-element.35), channel_id=1, source_target_pairs={{0,1},{1,0},{2,3},{3,2},{4,5},{5,4},{6,7},{7,6},{8,9},{9,8},{10,11... | collective-permute-start | bytes 61448 | tf_op jit(solution)/shard_map/ppermute | solution.py:26
  121.6 3.0 %collective-permute-start.4 = (f32[40,128]{1,0:T(8,128)S(1)}, f32[40,128]{1,0:T(8,128)S(1)}, u32[]{:S(2)}, u32[]{:S(2)}) collective-permute-start(f32[40,128]{1,0:T(8,128)S(1)} %tail.1.refs_2_), channel_id=1, source_target_pairs={{0,1},{1,0},{2,3},{3,2},{4,5},{5,4},{6,7},{7,6},{8,9},{9,8},{10,11... | collective-permute-start | bytes 61448 | tf_op jit(solution)/shard_map/ppermute | solution.py:26
  129.0 1.5 collective-permute-start.5
  152.9 3.5 %collective-permute-start.6 = (f32[40,128]{1,0:T(8,128)S(1)}, f32[40,128]{1,0:T(8,128)S(1)}, u32[]{:S(2)}, u32[]{:S(2)}) collective-permute-start(f32[40,128]{1,0:T(8,128)S(1)} %bitcast.9), channel_id=1, source_target_pairs={{0,1},{1,0},{2,3},{3,2},{4,5},{5,4},{6,7},{7,6},{8,9},{9,8},{10,11... | collective-permute-start | bytes 61448 | tf_op jit(solution)/shard_map/ppermute | solution.py:26

commit v7 on v6

--- a/solution.py
+++ b/solution.py
@@ -435,11 +435,11 @@
 
     sent = swap(multiply(slab, test_matrix, far))
     product = multiply(slab, test_matrix, core)
-    made = parts_of(slab, core, 1)
+    made = parts_of(slab, core, 0)
     part = add(product, sent, made[:1])
     own = exchange(total(exchange(part, "z"), zs), "z")
 
-    *made, own = parts_of(slab, core, 0, made, own)
+    *made, own = parts_of(slab, core, 1, made, own)
     parts, far_parts = made[:COUNT], made[COUNT:]
     other = swap(own)
     part = pull(other, far_parts, pull(own, parts))

time: 161 us -> 156 us (0.969)
  blocking collectives: 116 us -> 112 us
  starting transfers between devices: 14.1 us -> 11.9 us
    all_to_all x7, blocking collectives: 116 us -> 112 us  [exchange(): return lax.all_to_all(value, axes, 0, 0, tiled=False)]
    ppermute x7, starting transfers between devices: 14.1 us -> 11.9 us  [swap(): return lax.ppermute(value, 'core', SWAP)]
  transfers between devices with their start and end apart: 7 -> 7, of which waited for: 4 -> 4; matrix products, arithmetic and copies ran while one was open for 0% -> 0% of each run, Pallas kernels for 7% -> 5%
where the time goes in v7:
time: 156 us
  blocking collectives  112 us (72%)
  Pallas kernels  27.4 us (18%)
  starting transfers between devices  11.9 us (8%)
  waiting for transfers between devices  2.94 us (2%)
    all_to_all x7, blocking collectives, exchange(): return lax.all_to_all(value, axes, 0, 0, tiled=False)  112 us
    ppermute x7, starting transfers between devices, swap(): return lax.ppermute(value, 'core', SWAP)  11.9 us
    pallas_call x11, Pallas kernels, small_call(): pl.pallas_call(without(kernel, len(scalars) + len(operands), len(after)),...  10 us
    pallas_call x2, Pallas kernels, multiply(): pl.pallas_call(multiply_kernel, in_specs=[pl.BlockSpec(memory_space=pltpu...  6.4 us
    pallas_call x2, Pallas kernels, project(): pl.pallas_call(without(project_kernel, 1 + COUNT, len(after)), in_specs=[...  4.79 us
    pallas_call x2, Pallas kernels, parts_of(): pl.pallas_call(kernel, in_specs=[pl.BlockSpec(memory_space=pltpu.SMEM), h...  3.97 us
  transfers between devices with their start and end apart: 7, of which 4 were waited for; matrix products, arithmetic and copies ran while one was open for 0% of the time, Pallas kernels for 5%

profile of v7, /device:TPU:1, one launch (start us, length us, event | category | flops | bytes accessed | tf_op | source)
XLA Modules:
  0.0 155.6 jit_solution(14113772788682580570)
XLA Ops:
  0.6 3.2 %multiply.3 = f32[8,128,128]{2,1,0:T(8,128)S(1)} custom-call(s32[1]{0:T(128)S(6)} %sub.3.half_ref, f32[8,2,128,1024]{3,2,1,0:T(8,128)} %bitcast.11, f32[1024,128]{1,0:T(8,128)} %right_ref.3), custom_call_target="tpu_custom_call" | custom-call | flops 1073741824 | bytes 4194304 | tf_op jit(solution)/shard_map/multiply/pallas_call | solution.py:83
  3.8 3.3 %collective-permute-start = (f32[8,128,128]{2,1,0:T(8,128)S(1)}, f32[8,128,128]{2,1,0:T(8,128)S(1)}, u32[]{:S(2)}, u32[]{:S(2)}) collective-permute-start(f32[8,128,128]{2,1,0:T(8,128)S(1)} %multiply.3), channel_id=1, source_target_pairs={{0,1},{1,0},{2,3},{3,2},{4,5},{5,4},{6,7},{7,6},{8,9},{9,8},{10,11... | collective-permute-start | bytes 1572872 | tf_op jit(solution)/shard_map/ppermute | solution.py:26
  7.2 3.2 %multiply.2.refs_0_ = f32[8,128,128]{2,1,0:T(8,128)S(1)} custom-call(s32[1]{0:T(128)} %bitcast.half_ref.refs_0_, f32[8,2,128,1024]{3,2,1,0:T(8,128)} %bitcast.12, f32[1024,128]{1,0:T(8,128)} %right_ref.3), custom_call_target="tpu_custom_call" | custom-call | flops 1073741824 | bytes 4194304 | tf_op jit(solution)/shard_map/multiply/pallas_call | solution.py:83
  10.4 0.2 parts.2
  10.5 0.1 add.1
  10.6 19.2 %all_to_all.35.refs_0_ = f32[8,128,128]{2,1,0:T(8,128)S(1)} all-to-all(f32[8,128,128]{2,1,0:T(8,128)S(1)} %add.1), channel_id=1, replica_groups=mesh['y'=4,'x'=4,'z'=8,'core'=2] {'z'}, dimensions={0} | all-to-all | bytes 1048576 | tf_op jit(solution)/shard_map/all_to_all | solution.py:30
  29.9 16.6 %all_to_all.36.refs_2_ = f32[8,128,128]{2,1,0:T(8,128)S(1)} all-to-all(f32[8,128,128]{2,1,0:T(8,128)S(1)} %total.4), channel_id=1, replica_groups=mesh['y'=4,'x'=4,'z'=8,'core'=2] {'z'}, dimensions={0} | all-to-all | bytes 1048576 | tf_op jit(solution)/shard_map/all_to_all | solution.py:30
  46.4 3.8 %parts.3 = (bf16[8,128,1024]{2,1,0:T(8,128)(2,1)S(1)}, bf16[8,128,1024]{2,1,0:T(8,128)(2,1)S(1)}, bf16[8,128,1024]{2,1,0:T(8,128)(2,1)S(1)}, bf16[8,128,1024]{2,...) custom-call(s32[1]{0:T(128)} %bitcast.half_ref.refs_0_, ...), custom_call_target="tpu_custom_call", output_to_operand_aliasing={{6}: (2, {}), {0}: (3, {}), {1}: (4, {}), {2}: (5, {}), {3}... | custom-call | flops 2147483648 | bytes 8388608 | tf_op jit(solution)/shard_map/parts/pallas_call | solution.py:142
  50.3 2.1 %collective-permute-start.1 = (f32[8,128,128]{2,1,0:T(8,128)S(1)}, f32[8,128,128]{2,1,0:T(8,128)S(1)}, u32[]{:S(2)}, u32[]{:S(2)}) collective-permute-start(f32[8,128,128]{2,1,0:T(8,128)S(1)} %get-tuple-element.27.left_ref), channel_id=1, source_target_pairs={{0,1},{1,0},{2,3},{3,2},{4,5},{5,4},{6,7},{7,6},{8,9},{9,8},{10,11... | collective-permute-start | bytes 1572872 | tf_op jit(solution)/shard_map/ppermute | solution.py:26
  52.3 1.1 pull.2.refs_0_
  53.5 0.4 collective-permute-done.1.left_ref
  53.9 1.1 pull.3
  55.0 17.3 %all_to_all.37.refs_0_ = f32[16,64,128]{2,1,0:T(8,128)S(1)} all-to-all(f32[16,64,128]{2,1,0:T(8,128)S(1)} %bitcast.5), channel_id=1, replica_groups=mesh['y'=4,'x'=4,'z'=8,'core'=2] {'y','x'}, dimensions={0} | all-to-all | bytes 1048576 | tf_op jit(solution)/shard_map/all_to_all | solution.py:30
  72.3 0.1 total.5
  72.4 13.4 %all_to_all.38 = f32[16,64,128]{2,1,0:T(8,128)S(1)} all-to-all(f32[16,64,128]{2,1,0:T(8,128)S(1)} %total.5), channel_id=1, replica_groups=mesh['y'=4,'x'=4,'z'=8,'core'=2] {'y','x'}, dimensions={0} | all-to-all | bytes 1048576 | tf_op jit(solution)/shard_map/all_to_all | solution.py:30
  85.8 2.4 %project.3 = f32[8,128,128]{2,1,0:T(8,128)S(1)} custom-call(f32[1024,128]{1,0:T(8,128)S(1)} %bitcast.6, bf16[8,128,1024]{2,1,0:T(8,128)(2,1)S(1)} %get-tuple-element.28.high_ref.refs_1_, bf16[8,128,1024]{2,1,0:T(8,128)(2,1)S(1)} %get-tuple-element.29.low_ref.refs_2_, bf16[8,128,1024]{2,1,0:T(8,128)(2,1)S(1)} %get-tuple-element.33.refs_3_), custom_call_target="tpu_custom_call" | custom-call | flops 2147483648 | bytes 4194304 | tf_op jit(solution)/shard_map/project/pallas_call | solution.py:183
  88.2 2.4 %collective-permute-start.2 = (f32[8,128,128]{2,1,0:T(8,128)S(1)}, f32[8,128,128]{2,1,0:T(8,128)S(1)}, u32[]{:S(2)}, u32[]{:S(2)}) collective-permute-start(f32[8,128,128]{2,1,0:T(8,128)S(1)} %project.3), channel_id=1, source_target_pairs={{0,1},{1,0},{2,3},{3,2},{4,5},{5,4},{6,7},{7,6},{8,9},{9,8},{10,11... | collective-permute-start | bytes 1572872 | tf_op jit(solution)/shard_map/ppermute | solution.py:26
  90.6 0.7 gram.1
  91.3 0.1 collective-permute-start.3
  91.4 2.4 %project.2.refs_0_ = f32[8,128,128]{2,1,0:T(8,128)S(1)} custom-call(f32[1024,128]{1,0:T(8,128)S(1)} %bitcast.8, bf16[8,128,1024]{2,1,0:T(8,128)(2,1)S(1)} %get-tuple-element.30.high_ref.refs_1_, bf16[8,128,1024]{2,1,0:T(8,128)(2,1)S(1)} %get-tuple-element.31.low_ref.refs_2_, bf16[8,128,1024]{2,1,0:T(8,128)(2,1)S(1)} %get-tuple-element.32.refs_3_), custom_call_target="tpu_custom_call" | custom-call | flops 2147483648 | bytes 4194304 | tf_op jit(solution)/shard_map/project/pallas_call | solution.py:183
  93.8 0.1 join.1
  93.9 23.8 %all_to_all.39.refs_0_.refs_1_ = f32[8,168,128]{2,1,0:T(8,128)S(1)} all-to-all(f32[8,168,128]{2,1,0:T(8,128)S(1)} %join.1), channel_id=1, replica_groups=mesh['y'=4,'x'=4,'z'=8,'core'=2] {'z'}, dimensions={0} | all-to-all | bytes 1376256 | tf_op jit(solution)/shard_map/all_to_all | solution.py:30
  117.7 0.7 collective-permute-start.4
  118.4 0.8 collective-permute-done.4.refs_3_
  119.2 4.3 %middle.1 = (f32[128,128]{1,0:T(8,128)S(1)}, f32[128,128]{1,0:T(8,128)S(1)}, f32[40,128]{1,0:T(8,128)S(1)}, f32[40,128]{1,0:T(8,128)S(1)}) custom-call(s32[1]{0:T(128)} %bitcast.half_ref.refs_0_, f32[8,168,128]{2,1,0:T(8,128)S(1)} %all_to_all.39.refs_0_.refs_1_, f32[40,128]{1,0:T(8,128)S(1)} %tail.1.refs_2_, f32[40,128]{1,0:T(8,128)S(1)} %collective-permute-done.4.refs_3_), custom_call_target="tpu_custom_call" | custom-call | flops 4300000256 | bytes 512 | tf_op jit(solution)/shard_map/middle/pallas_call | solution.py:338
  123.6 0.7 collective-permute-start.5
  124.2 0.8 collective-permute-done.5.refs_1_
  125.1 11.5 %all_to_all.40.refs_0_ = f32[16,40,128]{2,1,0:T(8,128)S(1)} all-to-all(f32[16,40,128]{2,1,0:T(8,128)S(1)} %pair.1), channel_id=1, replica_groups=mesh['y'=4,'x'=4,'z'=8,'core'=2] {'y','x'}, dimensions={0} | all-to-all | bytes 655360 | tf_op jit(solution)/shard_map/all_to_all | solution.py:30
  136.7 10.8 %all_to_all.41.refs_0_ = f32[8,40,128]{2,1,0:T(8,128)S(1)} all-to-all(f32[8,40,128]{2,1,0:T(8,128)S(1)} %total.6), channel_id=1, replica_groups=mesh['y'=4,'x'=4,'z'=8,'core'=2] {'z'}, dimensions={0} | all-to-all | bytes 327680 | tf_op jit(solution)/shard_map/all_to_all | solution.py:30
  147.4 2.6 %collective-permute-start.6 = (f32[40,128]{1,0:T(8,128)S(1)}, f32[40,128]{1,0:T(8,128)S(1)}, u32[]{:S(2)}, u32[]{:S(2)}) collective-permute-start(f32[40,128]{1,0:T(8,128)S(1)} %bitcast.9), channel_id=1, source_target_pairs={{0,1},{1,0},{2,3},{3,2},{4,5},{5,4},{6,7},{7,6},{8,9},{9,8},{10,11... | collective-permute-start | bytes 61448 | tf_op jit(solution)/shard_map/ppermute | solution.py:26
  150.1 0.8 collective-permute-done.6.refs_2_
  150.9 4.6 %last.1 = (f32[128,128]{1,0:T(8,128)}, f32[128,128]{1,0:T(8,128)}) custom-call(s32[1]{0:T(128)} %bitcast.half_ref.refs_0_, f32[40,128]{1,0:T(8,128)S(1)} %bitcast.10, f32[40,128]{1,0:T(8,128)S(1)} %collective-permute-done.6.refs_2_, f32[128,128]{1,0:T(8,128)S(1)} %get-tuple-element.38.refs_3_, f32[128,128]{1,0:T(8,128)S(1)} %get-tuple-element.39.refs_4_), custom_call_target="tpu_custom_call" | custom-call | flops 4600000000 | bytes 512 | tf_op jit(solution)/shard_map/last/pallas_call | solution.py:338
  (8 shorter events, 0.1 us)
Async XLA Ops:
  3.8 6.7 %collective-permute-start = (f32[8,128,128]{2,1,0:T(8,128)S(1)}, f32[8,128,128]{2,1,0:T(8,128)S(1)}, u32[]{:S(2)}, u32[]{:S(2)}) collective-permute-start(f32[8,128,128]{2,1,0:T(8,128)S(1)} %multiply.3), channel_id=1, source_target_pairs={{0,1},{1,0},{2,3},{3,2},{4,5},{5,4},{6,7},{7,6},{8,9},{9,8},{10,11... | collective-permute-start | bytes 1572872 | tf_op jit(solution)/shard_map/ppermute | solution.py:26
  50.3 3.6 %collective-permute-start.1 = (f32[8,128,128]{2,1,0:T(8,128)S(1)}, f32[8,128,128]{2,1,0:T(8,128)S(1)}, u32[]{:S(2)}, u32[]{:S(2)}) collective-permute-start(f32[8,128,128]{2,1,0:T(8,128)S(1)} %get-tuple-element.27.left_ref), channel_id=1, source_target_pairs={{0,1},{1,0},{2,3},{3,2},{4,5},{5,4},{6,7},{7,6},{8,9},{9,8},{10,11... | collective-permute-start | bytes 1572872 | tf_op jit(solution)/shard_map/ppermute | solution.py:26
  88.2 5.7 %collective-permute-start.2 = (f32[8,128,128]{2,1,0:T(8,128)S(1)}, f32[8,128,128]{2,1,0:T(8,128)S(1)}, u32[]{:S(2)}, u32[]{:S(2)}) collective-permute-start(f32[8,128,128]{2,1,0:T(8,128)S(1)} %project.3), channel_id=1, source_target_pairs={{0,1},{1,0},{2,3},{3,2},{4,5},{5,4},{6,7},{7,6},{8,9},{9,8},{10,11... | collective-permute-start | bytes 1572872 | tf_op jit(solution)/shard_map/ppermute | solution.py:26
  91.3 2.5 %collective-permute-start.3 = (f32[40,128]{1,0:T(8,128)S(1)}, f32[40,128]{1,0:T(8,128)S(1)}, u32[]{:S(2)}, u32[]{:S(2)}) collective-permute-start(f32[40,128]{1,0:T(8,128)S(1)} %get-tuple-element.35), channel_id=1, source_target_pairs={{0,1},{1,0},{2,3},{3,2},{4,5},{5,4},{6,7},{7,6},{8,9},{9,8},{10,11... | collective-permute-start | bytes 61448 | tf_op jit(solution)/shard_map/ppermute | solution.py:26
  117.7 1.5 collective-permute-start.4
  123.6 1.5 collective-permute-start.5
  147.4 3.5 %collective-permute-start.6 = (f32[40,128]{1,0:T(8,128)S(1)}, f32[40,128]{1,0:T(8,128)S(1)}, u32[]{:S(2)}, u32[]{:S(2)}) collective-permute-start(f32[40,128]{1,0:T(8,128)S(1)} %bitcast.9), channel_id=1, source_target_pairs={{0,1},{1,0},{2,3},{3,2},{4,5},{5,4},{6,7},{7,6},{8,9},{9,8},{10,11... | collective-permute-start | bytes 61448 | tf_op jit(solution)/shard_map/ppermute | solution.py:26

commit v8 on v7

--- a/solution.py
+++ b/solution.py
@@ -18,7 +18,7 @@
 PANEL = 16
 STEP = 2
 PULL = 8
-COUNT = 3
+PARTS = 5
 VMEM = 12 * 1024 * 1024
 
 
@@ -97,39 +97,40 @@
     )(half, keep(slab, pltpu.HBM), keep(right, pltpu.HBM))
 
 
-def parts_kernel(turn, core_ref, slab_ref, *refs):
-    block_ref, sems = refs[-2:]
-    part_refs = refs[-2 - 2 * COUNT : -2]
-    zs, core = block_ref.shape[0], core_ref[0]
-
-    @pl.when(core == turn)
-    def _():
-        copies = [
-            [
-                pltpu.make_async_copy(
-                    slab_ref.at[place, half], block_ref.at[place, half], sems.at[place, half]
-                )
-                for half in range(2)
-            ]
-            for place in range(zs)
+def parts_kernel(turn, slab_ref, part_refs, block_ref, sems):
+    zs, _, height, _ = block_ref.shape
+    copies = [
+        [
+            pltpu.make_async_copy(
+                slab_ref.at[place, half], block_ref.at[place, half], sems.at[place, half]
+            )
+            for half in range(2)
         ]
-        for pair in copies:
-            for copy in pair:
-                copy.start()
-        for place in range(zs):
-            for half, refs in ((turn, part_refs[:COUNT]), (1 - turn, part_refs[COUNT:])):
-                copies[place][half].wait()
-                for part, ref in zip(split(block_ref[place, half], COUNT), refs):
-                    ref[place] = part
+        for place in range(zs)
+    ]
+    for pair in copies:
+        for copy in pair:
+            copy.start()
+    for place in range(zs):
+        for half in range(2):
+            refs = part_refs[PARTS * (half != turn) :][:PARTS]
+            copies[place][half].wait()
+            block = block_ref[place, half]
+            for part, ref in zip(split(block, 2), refs[:2]):
+                ref[place] = part
+            for part, ref in zip(split(jnp.transpose(block), 3), refs[2:]):
+                ref[:, place * height : (place + 1) * height] = part
 
 
 def parts_of(slab, core, turn, before=(), passed=None):
     zs, _, height, depth = slab.shape
     high_memory = pl.BlockSpec(memory_space=pltpu.HBM)
     memory = pl.BlockSpec(memory_space=pltpu.VMEM)
-    count = 2 * COUNT
+    count = 2 * PARTS
     through = [] if passed is None else [passed]
-    shapes = [pltpu.VMEM((zs, height, depth), jnp.bfloat16)] * count
+    shapes = [pltpu.VMEM((zs, height, depth), jnp.bfloat16)] * 2
+    shapes += [pltpu.VMEM((depth, zs * height), jnp.bfloat16)] * 3
+    shapes = shapes * 2
     shapes += [jax.ShapeDtypeStruct(value.shape, value.dtype) for value in through]
     place = 2 + len(through)
     aliases = {2: count} if through else {}
@@ -137,7 +138,10 @@
 
     def kernel(*refs):
         outs = refs[place + len(before) :]
-        parts_kernel(turn, *refs[:2], *outs[:count], *outs[-2:])
+
+        @pl.when(refs[0][0] == turn)
+        def _():
+            parts_kernel(turn, refs[1], outs[:count], *outs[-2:])
 
     return pl.pallas_call(
         kernel,
@@ -165,30 +169,32 @@
 
 
 def project_kernel(right_ref, high_ref, middle_ref, low_ref, out_ref):
-    wide = right_ref.shape[1]
-    parts = split(right_ref[...], COUNT)
-    pair = jnp.concatenate(parts[:2], axis=1)
+    wide, height = right_ref.shape[1], out_ref.shape[1]
+    parts = split(jnp.transpose(right_ref[...]), 3)
+    stack = jnp.concatenate(parts, axis=0)
     for place in range(0, out_ref.shape[0], STEP):
-        high, middle = rows_of(high_ref, place, STEP), rows_of(middle_ref, place, STEP)
-        first, second = dot(high, pair), dot(middle, pair)
-        third = dot(high, parts[2]) + dot(rows_of(low_ref, place, STEP), parts[0])
-        small = (first[:, wide:] + second[:, :wide]) + (second[:, wide:] + third)
-        out_ref[place : place + STEP] = (first[:, :wide] + small).reshape(STEP, -1, wide)
-
-
-def project(right, parts, after=()):
-    zs, height, depth = parts[0].shape
+        run = slice(place * height, (place + STEP) * height)
+        first = dot(stack, high_ref[:, run])
+        second = dot(stack[: 2 * wide], middle_ref[:, run])
+        third = first[2 * wide :] + dot(parts[0], low_ref[:, run])
+        small = (first[wide : 2 * wide] + second[:wide]) + (second[wide:] + third)
+        value = jnp.transpose(first[:wide] + small)
+        out_ref[place : place + STEP] = value.reshape(STEP, height, wide)
+
+
+def project(right, parts, zs):
+    depth, height = parts[0].shape
     wide = right.shape[1]
     memory = pl.BlockSpec(memory_space=pltpu.VMEM)
     return pl.pallas_call(
-        without(project_kernel, 1 + COUNT, len(after)),
-        in_specs=[memory] * (1 + COUNT) + [pl.BlockSpec(memory_space=pl.ANY)] * len(after),
+        project_kernel,
+        in_specs=[memory] * 4,
         out_specs=memory,
-        out_shape=jax.ShapeDtypeStruct((zs, height, wide), jnp.float32),
+        out_shape=jax.ShapeDtypeStruct((zs, height // zs, wide), jnp.float32),
         compiler_params=params(),
-        cost_estimate=cost(zs * height, depth, wide, 8),
+        cost_estimate=cost(height, depth, wide, 8),
         name="project",
-    )(right, *[keep(part, pltpu.VMEM) for part in parts], *after)
+    )(right, *[keep(part, pltpu.VMEM) for part in parts])
 
 
 def pull_kernel(more, left_ref, high_ref, low_ref, *refs):
@@ -219,7 +225,7 @@
         compiler_params=params(),
         cost_estimate=cost(zs * height, depth, wide, 4),
         name="pull",
-    )(left, *[keep(part, pltpu.VMEM) for part in parts[:2]], *([before] if more else []))
+    )(left, *[keep(part, pltpu.VMEM) for part in parts], *([before] if more else []))
 
 
 def spread(row):
@@ -440,16 +446,16 @@
     own = exchange(total(exchange(part, "z"), zs), "z")
 
     *made, own = parts_of(slab, core, 1, made, own)
-    parts, far_parts = made[:COUNT], made[COUNT:]
+    parts, far_parts = made[:PARTS], made[PARTS:]
     other = swap(own)
-    part = pull(other, far_parts, pull(own, parts))
+    part = pull(other, far_parts[:2], pull(own, parts[:2]))
     pieces = total(exchange(part.reshape(row_count, -1, wide), ROW), row_count, 1.0 / row_total)
     pulled = exchange(pieces, ROW).reshape(-1, wide)
 
     own, other = small_call(gram_kernel, halves, "gram", 700, [pulled], [core])
     other = swap(other)
-    sent = swap(project(pulled, far_parts))
-    product = project(pulled, parts)
+    sent = swap(project(pulled, far_parts[2:], zs))
+    product = project(pulled, parts[2:], zs)
     height = product.shape[1]
     shape = (zs, height + own.shape[0], wide)
     joined = plain_call(join_kernel, shape, "join", product, sent, own, other)

time: 156 us -> 155 us (level)
  blocking collectives: 112 us -> 110 us
    all_to_all x7, blocking collectives: 112 us -> 110 us  [exchange(): return lax.all_to_all(value, axes, 0, 0, tiled=False)]
    pallas_call x2, Pallas kernels: 3.97 us -> 5.93 us  [parts_of(): pl.pallas_call(kernel, in_specs=[pl.BlockSpec(memory_space=pltpu.SMEM), h...]
where the time goes in v8:
time: 155 us; the launch traced here: 154 us
  blocking collectives  110 us (71%)
  Pallas kernels  28.5 us (18%)
  starting transfers between devices  12.4 us (8%)
  waiting for transfers between devices  2.94 us (2%)
    all_to_all x7, blocking collectives, exchange(): return lax.all_to_all(value, axes, 0, 0, tiled=False)  110 us
    ppermute x7, starting transfers between devices, swap(): return lax.ppermute(value, 'core', SWAP)  12.4 us
    pallas_call x11, Pallas kernels, small_call(): pl.pallas_call(without(kernel, len(scalars) + len(operands), len(after)),...  10 us
    pallas_call x2, Pallas kernels, multiply(): pl.pallas_call(multiply_kernel, in_specs=[pl.BlockSpec(memory_space=pltpu...  6.4 us
    pallas_call x2, Pallas kernels, parts_of(): pl.pallas_call(kernel, in_specs=[pl.BlockSpec(memory_space=pltpu.SMEM), h...  5.93 us
    pallas_call x2, Pallas kernels, project(): pl.pallas_call(project_kernel, in_specs=[memory] * 4, out_specs=memory, o...  3.91 us
  transfers between devices with their start and end apart: 7, of which 4 were waited for; matrix products, arithmetic and copies ran while one was open for 0% of the time, Pallas kernels for 5%

profile of v8, /device:TPU:1, one launch (start us, length us, event | category | flops | bytes accessed | tf_op | source)
XLA Modules:
  0.0 154.4 jit_solution(8242872713926471919)
XLA Ops:
  0.6 3.2 %multiply.3 = f32[8,128,128]{2,1,0:T(8,128)S(1)} custom-call(s32[1]{0:T(128)S(6)} %sub.3.half_ref, f32[8,2,128,1024]{3,2,1,0:T(8,128)} %bitcast.11, f32[1024,128]{1,0:T(8,128)} %right_ref.3), custom_call_target="tpu_custom_call" | custom-call | flops 1073741824 | bytes 4194304 | tf_op jit(solution)/shard_map/multiply/pallas_call | solution.py:83
  3.8 3.3 %collective-permute-start = (f32[8,128,128]{2,1,0:T(8,128)S(1)}, f32[8,128,128]{2,1,0:T(8,128)S(1)}, u32[]{:S(2)}, u32[]{:S(2)}) collective-permute-start(f32[8,128,128]{2,1,0:T(8,128)S(1)} %multiply.3), channel_id=1, source_target_pairs={{0,1},{1,0},{2,3},{3,2},{4,5},{5,4},{6,7},{7,6},{8,9},{9,8},{10,11... | collective-permute-start | bytes 1572872 | tf_op jit(solution)/shard_map/ppermute | solution.py:26
  7.2 3.2 %multiply.2.refs_0_ = f32[8,128,128]{2,1,0:T(8,128)S(1)} custom-call(s32[1]{0:T(128)} %bitcast.half_ref.refs_0_, f32[8,2,128,1024]{3,2,1,0:T(8,128)} %bitcast.12, f32[1024,128]{1,0:T(8,128)} %right_ref.3), custom_call_target="tpu_custom_call" | custom-call | flops 1073741824 | bytes 4194304 | tf_op jit(solution)/shard_map/multiply/pallas_call | solution.py:83
  10.4 0.2 parts.2
  10.5 0.1 add.1
  10.6 18.5 %all_to_all.35.refs_0_ = f32[8,128,128]{2,1,0:T(8,128)S(1)} all-to-all(f32[8,128,128]{2,1,0:T(8,128)S(1)} %add.1), channel_id=1, replica_groups=mesh['y'=4,'x'=4,'z'=8,'core'=2] {'z'}, dimensions={0} | all-to-all | bytes 1048576 | tf_op jit(solution)/shard_map/all_to_all | solution.py:30
  29.1 14.5 %all_to_all.36.refs_2_ = f32[8,128,128]{2,1,0:T(8,128)S(1)} all-to-all(f32[8,128,128]{2,1,0:T(8,128)S(1)} %total.4), channel_id=1, replica_groups=mesh['y'=4,'x'=4,'z'=8,'core'=2] {'z'}, dimensions={0} | all-to-all | bytes 1048576 | tf_op jit(solution)/shard_map/all_to_all | solution.py:30
  43.7 5.8 %parts.3 = (bf16[8,128,1024]{2,1,0:T(8,128)(2,1)S(1)}, bf16[8,128,1024]{2,1,0:T(8,128)(2,1)S(1)}, bf16[1024,1024]{1,0:T(8,128)(2,1)S(1)}, bf16[1024,1024]{1,0:T(...) custom-call(s32[1]{0:T(128)} %bitcast.half_ref.refs_0_, ...), custom_call_target="tpu_custom_call", output_to_operand_aliasing={{10}: (2, {}), {0}: (3, {}), {1}: (4, {}), {2}: (5, {}), {3... | custom-call | flops 2147483648 | bytes 8388608 | tf_op jit(solution)/shard_map/parts/pallas_call | solution.py:146
  49.5 2.6 %collective-permute-start.1 = (f32[8,128,128]{2,1,0:T(8,128)S(1)}, f32[8,128,128]{2,1,0:T(8,128)S(1)}, u32[]{:S(2)}, u32[]{:S(2)}) collective-permute-start(f32[8,128,128]{2,1,0:T(8,128)S(1)} %get-tuple-element.39.left_ref), channel_id=1, source_target_pairs={{0,1},{1,0},{2,3},{3,2},{4,5},{5,4},{6,7},{7,6},{8,9},{9,8},{10,11... | collective-permute-start | bytes 1572872 | tf_op jit(solution)/shard_map/ppermute | solution.py:26
  52.1 1.1 pull.2.refs_0_
  53.2 0.4 collective-permute-done.1.left_ref
  53.6 1.1 pull.3
  54.7 17.3 %all_to_all.37.refs_0_ = f32[16,64,128]{2,1,0:T(8,128)S(1)} all-to-all(f32[16,64,128]{2,1,0:T(8,128)S(1)} %bitcast.5), channel_id=1, replica_groups=mesh['y'=4,'x'=4,'z'=8,'core'=2] {'y','x'}, dimensions={0} | all-to-all | bytes 1048576 | tf_op jit(solution)/shard_map/all_to_all | solution.py:30
  72.0 0.1 total.5
  72.1 13.4 %all_to_all.38 = f32[16,64,128]{2,1,0:T(8,128)S(1)} all-to-all(f32[16,64,128]{2,1,0:T(8,128)S(1)} %total.5), channel_id=1, replica_groups=mesh['y'=4,'x'=4,'z'=8,'core'=2] {'y','x'}, dimensions={0} | all-to-all | bytes 1048576 | tf_op jit(solution)/shard_map/all_to_all | solution.py:30
  85.5 2.0 %project.3 = f32[8,128,128]{2,1,0:T(8,128)S(1)} custom-call(f32[1024,128]{1,0:T(8,128)S(1)} %bitcast.6, bf16[1024,1024]{1,0:T(8,128)(2,1)S(1)} %get-tuple-element.47.high_ref, bf16[1024,1024]{1,0:T(8,128)(2,1)S(1)} %get-tuple-element.48.middle_ref, bf16[1024,1024]{1,0:T(8,128)(2,1)S(1)} %get-tuple-element.49.low_ref), custom_call_target="tpu_custom_call" | custom-call | flops 2147483648 | bytes 4194304 | tf_op jit(solution)/shard_map/project/pallas_call | solution.py:189
  87.4 2.4 %collective-permute-start.2 = (f32[8,128,128]{2,1,0:T(8,128)S(1)}, f32[8,128,128]{2,1,0:T(8,128)S(1)}, u32[]{:S(2)}, u32[]{:S(2)}) collective-permute-start(f32[8,128,128]{2,1,0:T(8,128)S(1)} %project.3), channel_id=1, source_target_pairs={{0,1},{1,0},{2,3},{3,2},{4,5},{5,4},{6,7},{7,6},{8,9},{9,8},{10,11... | collective-permute-start | bytes 1572872 | tf_op jit(solution)/shard_map/ppermute | solution.py:26
  89.9 0.7 gram.1
  90.6 0.1 collective-permute-start.3
  90.7 2.0 %project.2.refs_0_ = f32[8,128,128]{2,1,0:T(8,128)S(1)} custom-call(f32[1024,128]{1,0:T(8,128)S(1)} %bitcast.8, bf16[1024,1024]{1,0:T(8,128)(2,1)S(1)} %get-tuple-element.44.high_ref, bf16[1024,1024]{1,0:T(8,128)(2,1)S(1)} %get-tuple-element.45.middle_ref, bf16[1024,1024]{1,0:T(8,128)(2,1)S(1)} %get-tuple-element.46.low_ref), custom_call_target="tpu_custom_call" | custom-call | flops 2147483648 | bytes 4194304 | tf_op jit(solution)/shard_map/project/pallas_call | solution.py:189
  92.7 0.1 join.1
  92.8 23.8 %all_to_all.39.refs_0_.refs_1_ = f32[8,168,128]{2,1,0:T(8,128)S(1)} all-to-all(f32[8,168,128]{2,1,0:T(8,128)S(1)} %join.1), channel_id=1, replica_groups=mesh['y'=4,'x'=4,'z'=8,'core'=2] {'z'}, dimensions={0} | all-to-all | bytes 1376256 | tf_op jit(solution)/shard_map/all_to_all | solution.py:30
  116.5 0.9 collective-permute-start.4
  117.4 0.8 collective-permute-done.4.refs_3_
  118.3 4.3 %middle.1 = (f32[128,128]{1,0:T(8,128)S(1)}, f32[128,128]{1,0:T(8,128)S(1)}, f32[40,128]{1,0:T(8,128)S(1)}, f32[40,128]{1,0:T(8,128)S(1)}) custom-call(s32[1]{0:T(128)} %bitcast.half_ref.refs_0_, f32[8,168,128]{2,1,0:T(8,128)S(1)} %all_to_all.39.refs_0_.refs_1_, f32[40,128]{1,0:T(8,128)S(1)} %tail.1.refs_2_, f32[40,128]{1,0:T(8,128)S(1)} %collective-permute-done.4.refs_3_), custom_call_target="tpu_custom_call" | custom-call | flops 4300000256 | bytes 512 | tf_op jit(solution)/shard_map/middle/pallas_call | solution.py:344
  122.6 0.4 collective-permute-start.5
  123.1 0.8 collective-permute-done.5.refs_1_
  123.9 11.5 %all_to_all.40.refs_0_ = f32[16,40,128]{2,1,0:T(8,128)S(1)} all-to-all(f32[16,40,128]{2,1,0:T(8,128)S(1)} %pair.1), channel_id=1, replica_groups=mesh['y'=4,'x'=4,'z'=8,'core'=2] {'y','x'}, dimensions={0} | all-to-all | bytes 655360 | tf_op jit(solution)/shard_map/all_to_all | solution.py:30
  135.5 10.8 %all_to_all.41.refs_0_ = f32[8,40,128]{2,1,0:T(8,128)S(1)} all-to-all(f32[8,40,128]{2,1,0:T(8,128)S(1)} %total.6), channel_id=1, replica_groups=mesh['y'=4,'x'=4,'z'=8,'core'=2] {'z'}, dimensions={0} | all-to-all | bytes 327680 | tf_op jit(solution)/shard_map/all_to_all | solution.py:30
  146.3 2.6 %collective-permute-start.6 = (f32[40,128]{1,0:T(8,128)S(1)}, f32[40,128]{1,0:T(8,128)S(1)}, u32[]{:S(2)}, u32[]{:S(2)}) collective-permute-start(f32[40,128]{1,0:T(8,128)S(1)} %bitcast.9), channel_id=1, source_target_pairs={{0,1},{1,0},{2,3},{3,2},{4,5},{5,4},{6,7},{7,6},{8,9},{9,8},{10,11... | collective-permute-start | bytes 61448 | tf_op jit(solution)/shard_map/ppermute | solution.py:26
  148.9 0.8 collective-permute-done.6.refs_2_
  149.8 4.6 %last.1 = (f32[128,128]{1,0:T(8,128)}, f32[128,128]{1,0:T(8,128)}) custom-call(s32[1]{0:T(128)} %bitcast.half_ref.refs_0_, f32[40,128]{1,0:T(8,128)S(1)} %bitcast.10, f32[40,128]{1,0:T(8,128)S(1)} %collective-permute-done.6.refs_2_, f32[128,128]{1,0:T(8,128)S(1)} %get-tuple-element.54.refs_3_, f32[128,128]{1,0:T(8,128)S(1)} %get-tuple-element.55.refs_4_), custom_call_target="tpu_custom_call" | custom-call | flops 4600000000 | bytes 512 | tf_op jit(solution)/shard_map/last/pallas_call | solution.py:344
  (8 shorter events, 0.1 us)
Async XLA Ops:
  3.8 6.7 %collective-permute-start = (f32[8,128,128]{2,1,0:T(8,128)S(1)}, f32[8,128,128]{2,1,0:T(8,128)S(1)}, u32[]{:S(2)}, u32[]{:S(2)}) collective-permute-start(f32[8,128,128]{2,1,0:T(8,128)S(1)} %multiply.3), channel_id=1, source_target_pairs={{0,1},{1,0},{2,3},{3,2},{4,5},{5,4},{6,7},{7,6},{8,9},{9,8},{10,11... | collective-permute-start | bytes 1572872 | tf_op jit(solution)/shard_map/ppermute | solution.py:26
  49.5 4.1 %collective-permute-start.1 = (f32[8,128,128]{2,1,0:T(8,128)S(1)}, f32[8,128,128]{2,1,0:T(8,128)S(1)}, u32[]{:S(2)}, u32[]{:S(2)}) collective-permute-start(f32[8,128,128]{2,1,0:T(8,128)S(1)} %get-tuple-element.39.left_ref), channel_id=1, source_target_pairs={{0,1},{1,0},{2,3},{3,2},{4,5},{5,4},{6,7},{7,6},{8,9},{9,8},{10,11... | collective-permute-start | bytes 1572872 | tf_op jit(solution)/shard_map/ppermute | solution.py:26
  87.4 5.2 %collective-permute-start.2 = (f32[8,128,128]{2,1,0:T(8,128)S(1)}, f32[8,128,128]{2,1,0:T(8,128)S(1)}, u32[]{:S(2)}, u32[]{:S(2)}) collective-permute-start(f32[8,128,128]{2,1,0:T(8,128)S(1)} %project.3), channel_id=1, source_target_pairs={{0,1},{1,0},{2,3},{3,2},{4,5},{5,4},{6,7},{7,6},{8,9},{9,8},{10,11... | collective-permute-start | bytes 1572872 | tf_op jit(solution)/shard_map/ppermute | solution.py:26
  90.6 2.1 %collective-permute-start.3 = (f32[40,128]{1,0:T(8,128)S(1)}, f32[40,128]{1,0:T(8,128)S(1)}, u32[]{:S(2)}, u32[]{:S(2)}) collective-permute-start(f32[40,128]{1,0:T(8,128)S(1)} %get-tuple-element.51), channel_id=1, source_target_pairs={{0,1},{1,0},{2,3},{3,2},{4,5},{5,4},{6,7},{7,6},{8,9},{9,8},{10,11... | collective-permute-start | bytes 61448 | tf_op jit(solution)/shard_map/ppermute | solution.py:26
  116.5 1.8 %collective-permute-start.4 = (f32[40,128]{1,0:T(8,128)S(1)}, f32[40,128]{1,0:T(8,128)S(1)}, u32[]{:S(2)}, u32[]{:S(2)}) collective-permute-start(f32[40,128]{1,0:T(8,128)S(1)} %tail.1.refs_2_), channel_id=1, source_target_pairs={{0,1},{1,0},{2,3},{3,2},{4,5},{5,4},{6,7},{7,6},{8,9},{9,8},{10,11... | collective-permute-start | bytes 61448 | tf_op jit(solution)/shard_map/ppermute | solution.py:26
  122.6 1.3 collective-permute-start.5
  146.3 3.5 %collective-permute-start.6 = (f32[40,128]{1,0:T(8,128)S(1)}, f32[40,128]{1,0:T(8,128)S(1)}, u32[]{:S(2)}, u32[]{:S(2)}) collective-permute-start(f32[40,128]{1,0:T(8,128)S(1)} %bitcast.9), channel_id=1, source_target_pairs={{0,1},{1,0},{2,3},{3,2},{4,5},{5,4},{6,7},{7,6},{8,9},{9,8},{10,11... | collective-permute-start | bytes 61448 | tf_op jit(solution)/shard_map/ppermute | solution.py:26

commit v9 on v8

--- a/solution.py
+++ b/solution.py
@@ -9,7 +9,7 @@
 from jax.sharding import Mesh
 from jax.sharding import PartitionSpec as P
 
-HIGHEST = lax.Precision.HIGHEST
+PLAIN = (((1,), (0,)), ((), ()))
 CONTRACT = (((0,), (0,)), ((), ()))
 TRANSPOSED = (((1,), (1,)), ((), ()))
 ROW = ("y", "x")
@@ -30,8 +30,8 @@
     return lax.all_to_all(value, axes, 0, 0, tiled=False)
 
 
-def dot(a, b, dims=(((1,), (0,)), ((), ())), precision=None):
-    return lax.dot_general(a, b, dims, precision=precision, preferred_element_type=jnp.float32)
+def dot(a, b, dims=PLAIN):
+    return lax.dot_general(a, b, dims, preferred_element_type=jnp.float32)
 
 
 def split(value, count):
@@ -43,6 +43,23 @@
 
 
 keep = pltpu.with_memory_space_constraint
+
+
+def stacked(a, b, dims):
+    (first,), (second,) = dims[0]
+    a1, a2, a3 = split(a, 3)
+    b1, b2, b3 = split(b, 3)
+    left = jnp.concatenate([a1, a1, a2, a2, a1, a3], axis=first)
+    return dot(left, jnp.concatenate([b1, b2, b1, b2, b3, b1], axis=second), dims)
+
+
+def gram_of(value):
+    wide = value.shape[1]
+    high, middle, low = split(value, 3)
+    pair = jnp.concatenate([high, middle], axis=1)
+    four, cross = dot(pair, pair, CONTRACT), dot(high, low, CONTRACT)
+    small = four[wide:, wide:] + (cross + jnp.transpose(cross))
+    return four[:wide, :wide] + (four[:wide, wide:] + four[wide:, :wide] + small)
 
 
 def params():
@@ -281,7 +298,7 @@
             panel = range(start, start + per)
             u = jnp.concatenate([left[i] * scale[i] for i in panel], axis=0)
             v = jnp.concatenate([right[i] * scale[i] for i in panel], axis=0)
-            change = dot(u, jnp.concatenate([u, v], axis=1), CONTRACT, HIGHEST)
+            change = stacked(u, jnp.concatenate([u, v], axis=1), CONTRACT)
             for q in range(rest, count):
                 rows = change[TILE * q : TILE * (q + 1)]
                 left[q] = left[q] - rows[:, :n]
@@ -362,7 +379,7 @@
 
 def gram_kernel(core_ref, value_ref, own_ref, other_ref):
     value = value_ref[...]
-    store_halves(core_ref[0], dot(value, value, CONTRACT, HIGHEST), own_ref, other_ref)
+    store_halves(core_ref[0], gram_of(value), own_ref, other_ref)
 
 
 def add_kernel(first_ref, second_ref, out_ref):
@@ -412,9 +429,9 @@
     sketch = pieces_ref[0, :height]
     for place in range(1, pieces_ref.shape[0]):
         sketch += pieces_ref[place, :height]
-    inner = dot(sketch, lower, TRANSPOSED, HIGHEST)
+    inner = stacked(sketch, lower, TRANSPOSED)
     inner_ref[...] = inner
-    store_halves(core_ref[0], dot(inner, inner, CONTRACT, HIGHEST), own_ref, other_ref)
+    store_halves(core_ref[0], stacked(inner, inner, CONTRACT), own_ref, other_ref)
 
 
 def last_kernel(
@@ -422,8 +439,8 @@
 ):
     gram = load_halves(core_ref[0], own_ref[...], other_ref[...])
     upper, lower = eliminate(gram, floor_of(gram))
-    basis_ref[...] = dot(inner_ref[...], lower, TRANSPOSED, HIGHEST) * root_rows
-    factor_ref[...] = dot(upper, before_ref[...], precision=HIGHEST) / root_rows
+    basis_ref[...] = stacked(inner_ref[...], lower, TRANSPOSED) * root_rows
+    factor_ref[...] = stacked(upper, before_ref[...], PLAIN) / root_rows
 
 
 def local(slab, test_matrix):

time: 155 us -> 153 us (0.987)
  Pallas kernels: 28.5 us -> 26.7 us
    pallas_call x11, Pallas kernels: 10 us -> 8.18 us  [small_call(): pl.pallas_call(without(kernel, len(scalars) + len(operands), len(after)),...]
where the time goes in v9:
time: 153 us
  blocking collectives  110 us (72%)
  Pallas kernels  26.7 us (17%)
  starting transfers between devices  12.4 us (8%)
  waiting for transfers between devices  2.94 us (2%)
    all_to_all x7, blocking collectives, exchange(): return lax.all_to_all(value, axes, 0, 0, tiled=False)  110 us
    ppermute x7, starting transfers between devices, swap(): return lax.ppermute(value, 'core', SWAP)  12.4 us
    pallas_call x11, Pallas kernels, small_call(): pl.pallas_call(without(kernel, len(scalars) + len(operands), len(after)),...  8.18 us
    pallas_call x2, Pallas kernels, multiply(): pl.pallas_call(multiply_kernel, in_specs=[pl.BlockSpec(memory_space=pltpu...  6.4 us
    pallas_call x2, Pallas kernels, parts_of(): pl.pallas_call(kernel, in_specs=[pl.BlockSpec(memory_space=pltpu.SMEM), h...  5.93 us
    pallas_call x2, Pallas kernels, project(): pl.pallas_call(project_kernel, in_specs=[memory] * 4, out_specs=memory, o...  3.91 us
  transfers between devices with their start and end apart: 7, of which 4 were waited for; matrix products, arithmetic and copies ran while one was open for 0% of the time, Pallas kernels for 5%

profile of v9, /device:TPU:1, one launch (start us, length us, event | category | flops | bytes accessed | tf_op | source)
XLA Modules:
  0.0 152.6 jit_solution(728987659861462142)
XLA Ops:
  0.6 3.2 %multiply.3 = f32[8,128,128]{2,1,0:T(8,128)S(1)} custom-call(s32[1]{0:T(128)S(6)} %sub.3.half_ref, f32[8,2,128,1024]{3,2,1,0:T(8,128)} %bitcast.11, f32[1024,128]{1,0:T(8,128)} %right_ref.3), custom_call_target="tpu_custom_call" | custom-call | flops 1073741824 | bytes 4194304 | tf_op jit(solution)/shard_map/multiply/pallas_call | solution.py:100
  3.8 3.3 %collective-permute-start = (f32[8,128,128]{2,1,0:T(8,128)S(1)}, f32[8,128,128]{2,1,0:T(8,128)S(1)}, u32[]{:S(2)}, u32[]{:S(2)}) collective-permute-start(f32[8,128,128]{2,1,0:T(8,128)S(1)} %multiply.3), channel_id=1, source_target_pairs={{0,1},{1,0},{2,3},{3,2},{4,5},{5,4},{6,7},{7,6},{8,9},{9,8},{10,11... | collective-permute-start | bytes 1572872 | tf_op jit(solution)/shard_map/ppermute | solution.py:26
  7.2 3.2 %multiply.2.refs_0_ = f32[8,128,128]{2,1,0:T(8,128)S(1)} custom-call(s32[1]{0:T(128)} %bitcast.half_ref.refs_0_, f32[8,2,128,1024]{3,2,1,0:T(8,128)} %bitcast.12, f32[1024,128]{1,0:T(8,128)} %right_ref.3), custom_call_target="tpu_custom_call" | custom-call | flops 1073741824 | bytes 4194304 | tf_op jit(solution)/shard_map/multiply/pallas_call | solution.py:100
  10.4 0.2 parts.2
  10.5 0.1 add.1
  10.6 18.5 %all_to_all.35.refs_0_ = f32[8,128,128]{2,1,0:T(8,128)S(1)} all-to-all(f32[8,128,128]{2,1,0:T(8,128)S(1)} %add.1), channel_id=1, replica_groups=mesh['y'=4,'x'=4,'z'=8,'core'=2] {'z'}, dimensions={0} | all-to-all | bytes 1048576 | tf_op jit(solution)/shard_map/all_to_all | solution.py:30
  29.1 14.5 %all_to_all.36.refs_2_ = f32[8,128,128]{2,1,0:T(8,128)S(1)} all-to-all(f32[8,128,128]{2,1,0:T(8,128)S(1)} %total.4), channel_id=1, replica_groups=mesh['y'=4,'x'=4,'z'=8,'core'=2] {'z'}, dimensions={0} | all-to-all | bytes 1048576 | tf_op jit(solution)/shard_map/all_to_all | solution.py:30
  43.7 5.8 %parts.3 = (bf16[8,128,1024]{2,1,0:T(8,128)(2,1)S(1)}, bf16[8,128,1024]{2,1,0:T(8,128)(2,1)S(1)}, bf16[1024,1024]{1,0:T(8,128)(2,1)S(1)}, bf16[1024,1024]{1,0:T(...) custom-call(s32[1]{0:T(128)} %bitcast.half_ref.refs_0_, ...), custom_call_target="tpu_custom_call", output_to_operand_aliasing={{10}: (2, {}), {0}: (3, {}), {1}: (4, {}), {2}: (5, {}), {3... | custom-call | flops 2147483648 | bytes 8388608 | tf_op jit(solution)/shard_map/parts/pallas_call | solution.py:163
  49.5 2.6 %collective-permute-start.1 = (f32[8,128,128]{2,1,0:T(8,128)S(1)}, f32[8,128,128]{2,1,0:T(8,128)S(1)}, u32[]{:S(2)}, u32[]{:S(2)}) collective-permute-start(f32[8,128,128]{2,1,0:T(8,128)S(1)} %get-tuple-element.39.left_ref), channel_id=1, source_target_pairs={{0,1},{1,0},{2,3},{3,2},{4,5},{5,4},{6,7},{7,6},{8,9},{9,8},{10,11... | collective-permute-start | bytes 1572872 | tf_op jit(solution)/shard_map/ppermute | solution.py:26
  52.1 1.1 pull.2.refs_0_
  53.2 0.4 collective-permute-done.1.left_ref
  53.6 1.1 pull.3
  54.7 17.3 %all_to_all.37.refs_0_ = f32[16,64,128]{2,1,0:T(8,128)S(1)} all-to-all(f32[16,64,128]{2,1,0:T(8,128)S(1)} %bitcast.5), channel_id=1, replica_groups=mesh['y'=4,'x'=4,'z'=8,'core'=2] {'y','x'}, dimensions={0} | all-to-all | bytes 1048576 | tf_op jit(solution)/shard_map/all_to_all | solution.py:30
  72.0 0.1 total.5
  72.1 13.4 %all_to_all.38 = f32[16,64,128]{2,1,0:T(8,128)S(1)} all-to-all(f32[16,64,128]{2,1,0:T(8,128)S(1)} %total.5), channel_id=1, replica_groups=mesh['y'=4,'x'=4,'z'=8,'core'=2] {'y','x'}, dimensions={0} | all-to-all | bytes 1048576 | tf_op jit(solution)/shard_map/all_to_all | solution.py:30
  85.5 2.0 %project.3 = f32[8,128,128]{2,1,0:T(8,128)S(1)} custom-call(f32[1024,128]{1,0:T(8,128)S(1)} %bitcast.6, bf16[1024,1024]{1,0:T(8,128)(2,1)S(1)} %get-tuple-element.47.high_ref, bf16[1024,1024]{1,0:T(8,128)(2,1)S(1)} %get-tuple-element.48.middle_ref, bf16[1024,1024]{1,0:T(8,128)(2,1)S(1)} %get-tuple-element.49.low_ref), custom_call_target="tpu_custom_call" | custom-call | flops 2147483648 | bytes 4194304 | tf_op jit(solution)/shard_map/project/pallas_call | solution.py:206
  87.4 2.4 %collective-permute-start.2 = (f32[8,128,128]{2,1,0:T(8,128)S(1)}, f32[8,128,128]{2,1,0:T(8,128)S(1)}, u32[]{:S(2)}, u32[]{:S(2)}) collective-permute-start(f32[8,128,128]{2,1,0:T(8,128)S(1)} %project.3), channel_id=1, source_target_pairs={{0,1},{1,0},{2,3},{3,2},{4,5},{5,4},{6,7},{7,6},{8,9},{9,8},{10,11... | collective-permute-start | bytes 1572872 | tf_op jit(solution)/shard_map/ppermute | solution.py:26
  89.9 0.5 gram.1
  90.4 0.1 collective-permute-start.3
  90.5 2.0 %project.2.refs_0_ = f32[8,128,128]{2,1,0:T(8,128)S(1)} custom-call(f32[1024,128]{1,0:T(8,128)S(1)} %bitcast.8, bf16[1024,1024]{1,0:T(8,128)(2,1)S(1)} %get-tuple-element.44.high_ref, bf16[1024,1024]{1,0:T(8,128)(2,1)S(1)} %get-tuple-element.45.middle_ref, bf16[1024,1024]{1,0:T(8,128)(2,1)S(1)} %get-tuple-element.46.low_ref), custom_call_target="tpu_custom_call" | custom-call | flops 2147483648 | bytes 4194304 | tf_op jit(solution)/shard_map/project/pallas_call | solution.py:206
  92.5 0.1 join.1
  92.6 23.8 %all_to_all.39.refs_0_.refs_1_ = f32[8,168,128]{2,1,0:T(8,128)S(1)} all-to-all(f32[8,168,128]{2,1,0:T(8,128)S(1)} %join.1), channel_id=1, replica_groups=mesh['y'=4,'x'=4,'z'=8,'core'=2] {'z'}, dimensions={0} | all-to-all | bytes 1376256 | tf_op jit(solution)/shard_map/all_to_all | solution.py:30
  116.3 0.9 collective-permute-start.4
  117.2 0.8 collective-permute-done.4.refs_3_
  118.1 3.5 %middle.1 = (f32[128,128]{1,0:T(8,128)S(1)}, f32[128,128]{1,0:T(8,128)S(1)}, f32[40,128]{1,0:T(8,128)S(1)}, f32[40,128]{1,0:T(8,128)S(1)}) custom-call(s32[1]{0:T(128)} %bitcast.half_ref.refs_0_, f32[8,168,128]{2,1,0:T(8,128)S(1)} %all_to_all.39.refs_0_.refs_1_, f32[40,128]{1,0:T(8,128)S(1)} %tail.1.refs_2_, f32[40,128]{1,0:T(8,128)S(1)} %collective-permute-done.4.refs_3_), custom_call_target="tpu_custom_call" | custom-call | flops 4300000256 | bytes 512 | tf_op jit(solution)/shard_map/middle/pallas_call | solution.py:361
  121.6 0.4 collective-permute-start.5
  122.0 0.8 collective-permute-done.5.refs_1_
  122.9 11.5 %all_to_all.40.refs_0_ = f32[16,40,128]{2,1,0:T(8,128)S(1)} all-to-all(f32[16,40,128]{2,1,0:T(8,128)S(1)} %pair.1), channel_id=1, replica_groups=mesh['y'=4,'x'=4,'z'=8,'core'=2] {'y','x'}, dimensions={0} | all-to-all | bytes 655360 | tf_op jit(solution)/shard_map/all_to_all | solution.py:30
  134.4 10.8 %all_to_all.41.refs_0_ = f32[8,40,128]{2,1,0:T(8,128)S(1)} all-to-all(f32[8,40,128]{2,1,0:T(8,128)S(1)} %total.6), channel_id=1, replica_groups=mesh['y'=4,'x'=4,'z'=8,'core'=2] {'z'}, dimensions={0} | all-to-all | bytes 327680 | tf_op jit(solution)/shard_map/all_to_all | solution.py:30
  145.2 2.6 %collective-permute-start.6 = (f32[40,128]{1,0:T(8,128)S(1)}, f32[40,128]{1,0:T(8,128)S(1)}, u32[]{:S(2)}, u32[]{:S(2)}) collective-permute-start(f32[40,128]{1,0:T(8,128)S(1)} %bitcast.9), channel_id=1, source_target_pairs={{0,1},{1,0},{2,3},{3,2},{4,5},{5,4},{6,7},{7,6},{8,9},{9,8},{10,11... | collective-permute-start | bytes 61448 | tf_op jit(solution)/shard_map/ppermute | solution.py:26
  147.9 0.8 collective-permute-done.6.refs_2_
  148.7 3.9 %last.1 = (f32[128,128]{1,0:T(8,128)}, f32[128,128]{1,0:T(8,128)}) custom-call(s32[1]{0:T(128)} %bitcast.half_ref.refs_0_, f32[40,128]{1,0:T(8,128)S(1)} %bitcast.10, f32[40,128]{1,0:T(8,128)S(1)} %collective-permute-done.6.refs_2_, f32[128,128]{1,0:T(8,128)S(1)} %get-tuple-element.54.refs_3_, f32[128,128]{1,0:T(8,128)S(1)} %get-tuple-element.55.refs_4_), custom_call_target="tpu_custom_call" | custom-call | flops 4600000000 | bytes 512 | tf_op jit(solution)/shard_map/last/pallas_call | solution.py:361
  (8 shorter events, 0.1 us)
Async XLA Ops:
  3.8 6.7 %collective-permute-start = (f32[8,128,128]{2,1,0:T(8,128)S(1)}, f32[8,128,128]{2,1,0:T(8,128)S(1)}, u32[]{:S(2)}, u32[]{:S(2)}) collective-permute-start(f32[8,128,128]{2,1,0:T(8,128)S(1)} %multiply.3), channel_id=1, source_target_pairs={{0,1},{1,0},{2,3},{3,2},{4,5},{5,4},{6,7},{7,6},{8,9},{9,8},{10,11... | collective-permute-start | bytes 1572872 | tf_op jit(solution)/shard_map/ppermute | solution.py:26
  49.5 4.1 %collective-permute-start.1 = (f32[8,128,128]{2,1,0:T(8,128)S(1)}, f32[8,128,128]{2,1,0:T(8,128)S(1)}, u32[]{:S(2)}, u32[]{:S(2)}) collective-permute-start(f32[8,128,128]{2,1,0:T(8,128)S(1)} %get-tuple-element.39.left_ref), channel_id=1, source_target_pairs={{0,1},{1,0},{2,3},{3,2},{4,5},{5,4},{6,7},{7,6},{8,9},{9,8},{10,11... | collective-permute-start | bytes 1572872 | tf_op jit(solution)/shard_map/ppermute | solution.py:26
  87.4 5.0 %collective-permute-start.2 = (f32[8,128,128]{2,1,0:T(8,128)S(1)}, f32[8,128,128]{2,1,0:T(8,128)S(1)}, u32[]{:S(2)}, u32[]{:S(2)}) collective-permute-start(f32[8,128,128]{2,1,0:T(8,128)S(1)} %project.3), channel_id=1, source_target_pairs={{0,1},{1,0},{2,3},{3,2},{4,5},{5,4},{6,7},{7,6},{8,9},{9,8},{10,11... | collective-permute-start | bytes 1572872 | tf_op jit(solution)/shard_map/ppermute | solution.py:26
  90.4 2.1 %collective-permute-start.3 = (f32[40,128]{1,0:T(8,128)S(1)}, f32[40,128]{1,0:T(8,128)S(1)}, u32[]{:S(2)}, u32[]{:S(2)}) collective-permute-start(f32[40,128]{1,0:T(8,128)S(1)} %get-tuple-element.51), channel_id=1, source_target_pairs={{0,1},{1,0},{2,3},{3,2},{4,5},{5,4},{6,7},{7,6},{8,9},{9,8},{10,11... | collective-permute-start | bytes 61448 | tf_op jit(solution)/shard_map/ppermute | solution.py:26
  116.3 1.8 %collective-permute-start.4 = (f32[40,128]{1,0:T(8,128)S(1)}, f32[40,128]{1,0:T(8,128)S(1)}, u32[]{:S(2)}, u32[]{:S(2)}) collective-permute-start(f32[40,128]{1,0:T(8,128)S(1)} %tail.1.refs_2_), channel_id=1, source_target_pairs={{0,1},{1,0},{2,3},{3,2},{4,5},{5,4},{6,7},{7,6},{8,9},{9,8},{10,11... | collective-permute-start | bytes 61448 | tf_op jit(solution)/shard_map/ppermute | solution.py:26
  121.6 1.3 collective-permute-start.5
  145.2 3.5 %collective-permute-start.6 = (f32[40,128]{1,0:T(8,128)S(1)}, f32[40,128]{1,0:T(8,128)S(1)}, u32[]{:S(2)}, u32[]{:S(2)}) collective-permute-start(f32[40,128]{1,0:T(8,128)S(1)} %bitcast.9), channel_id=1, source_target_pairs={{0,1},{1,0},{2,3},{3,2},{4,5},{5,4},{6,7},{7,6},{8,9},{9,8},{10,11... | collective-permute-start | bytes 61448 | tf_op jit(solution)/shard_map/ppermute | solution.py:26

commit v10 on v9

--- a/solution.py
+++ b/solution.py
@@ -17,7 +17,6 @@
 TILE = 8
 PANEL = 16
 STEP = 2
-PULL = 8
 PARTS = 5
 VMEM = 12 * 1024 * 1024
 
@@ -148,13 +147,16 @@
     shapes = [pltpu.VMEM((zs, height, depth), jnp.bfloat16)] * 2
     shapes += [pltpu.VMEM((depth, zs * height), jnp.bfloat16)] * 3
     shapes = shapes * 2
-    shapes += [jax.ShapeDtypeStruct(value.shape, value.dtype) for value in through]
+    for value in through:
+        shapes += [jax.ShapeDtypeStruct((zs // 2,) + value.shape[1:], value.dtype)] * 2
     place = 2 + len(through)
-    aliases = {2: count} if through else {}
-    aliases |= {place + i: i for i in range(len(before))}
+    aliases = {place + i: i for i in range(len(before))}
 
     def kernel(*refs):
         outs = refs[place + len(before) :]
+        if through:
+            outs[count][...] = refs[2][: zs // 2]
+            outs[count + 1][...] = refs[2][zs // 2 :]
 
         @pl.when(refs[0][0] == turn)
         def _():
@@ -164,7 +166,7 @@
         kernel,
         in_specs=[pl.BlockSpec(memory_space=pltpu.SMEM), high_memory]
         + [memory] * (len(through) + len(before)),
-        out_specs=[memory] * (count + len(through)),
+        out_specs=[memory] * len(shapes),
         scratch_shapes=[
             pltpu.VMEM((zs, 2, height, depth), jnp.float32),
             pltpu.SemaphoreType.DMA((zs, 2)),
@@ -214,42 +216,40 @@
     )(right, *[keep(part, pltpu.VMEM) for part in parts])
 
 
-def pull_kernel(more, left_ref, high_ref, low_ref, *refs):
-    out_ref = refs[-1]
-    zs, wide = left_ref.shape[0], left_ref.shape[-1]
-    total = None
-    for place in range(0, zs, PULL):
-        left = jnp.transpose(rows_of(left_ref, place, PULL))
-        high, low = split(left, 2)
-        block = rows_of(high_ref, place, PULL)
-        both = dot(jnp.concatenate([high, low], axis=0), block)
-        value = both[:wide] + (both[wide:] + dot(high, rows_of(low_ref, place, PULL)))
-        total = value if total is None else total + value
-    result = jnp.transpose(total)
-    out_ref[...] = result + refs[0][...] if more else result
-
-
-def pull(left, parts, before=None):
+def pull_kernel(count, start, more, *refs):
+    left_refs, (high_ref, low_ref), out_ref = refs[:count], refs[count : count + 2], refs[-1]
+    wide = out_ref.shape[-1]
+    left = jnp.concatenate([rows_of(ref, 0, ref.shape[0]) for ref in left_refs], axis=0)
+    run = sum(ref.shape[0] for ref in left_refs)
+    high, low = split(jnp.transpose(left), 2)
+    both = dot(jnp.concatenate([high, low], axis=0), rows_of(high_ref, start, run))
+    value = both[:wide] + (both[wide:] + dot(high, rows_of(low_ref, start, run)))
+    result = jnp.transpose(value)
+    out_ref[...] = result + refs[count + 2][...] if more else result
+
+
+def pull(lefts, parts, start=0, before=None):
     zs, height, depth = parts[0].shape
-    wide = left.shape[-1]
+    wide = lefts[0].shape[-1]
     memory = pl.BlockSpec(memory_space=pltpu.VMEM)
     more = before is not None
+    rows = height * sum(left.shape[0] for left in lefts)
     return pl.pallas_call(
-        functools.partial(pull_kernel, more),
-        in_specs=[memory] * (3 + more),
+        functools.partial(pull_kernel, len(lefts), start, more),
+        in_specs=[memory] * (len(lefts) + 2 + more),
         out_specs=memory,
         out_shape=jax.ShapeDtypeStruct((depth, wide), jnp.float32),
         compiler_params=params(),
-        cost_estimate=cost(zs * height, depth, wide, 4),
+        cost_estimate=cost(rows, depth, wide, 4),
         name="pull",
-    )(left, *[keep(part, pltpu.VMEM) for part in parts], *([before] if more else []))
+    )(*lefts, *[keep(part, pltpu.VMEM) for part in parts], *([before] if more else []))
 
 
 def spread(row):
     return jnp.broadcast_to(row, (TILE, row.shape[1]))
 
 
-def eliminate(gram, floor):
+def eliminate(gram, floor=None):
     n = gram.shape[0]
     count, per = n // TILE, PANEL // TILE
     sub = lax.broadcasted_iota(jnp.int32, (TILE, n), 0)
@@ -269,7 +269,9 @@
         pivots = []
         for s in range(PANEL):
             here, at = start + s // TILE, s % TILE
-            pivot = jnp.maximum(spread(column[s, here][at : at + 1]), floor)
+            pivot = spread(column[s, here][at : at + 1])
+            if floor is not None:
+                pivot = jnp.maximum(pivot, floor)
             over = 1.0 / pivot
             pivots.append(pivot)
             entry = {
@@ -438,7 +440,7 @@
     root_rows, core_ref, own_ref, other_ref, inner_ref, before_ref, basis_ref, factor_ref
 ):
     gram = load_halves(core_ref[0], own_ref[...], other_ref[...])
-    upper, lower = eliminate(gram, floor_of(gram))
+    upper, lower = eliminate(gram)
     basis_ref[...] = stacked(inner_ref[...], lower, TRANSPOSED) * root_rows
     factor_ref[...] = stacked(upper, before_ref[...], PLAIN) / root_rows
 
@@ -462,10 +464,12 @@
     part = add(product, sent, made[:1])
     own = exchange(total(exchange(part, "z"), zs), "z")
 
-    *made, own = parts_of(slab, core, 1, made, own)
+    *made, first, second = parts_of(slab, core, 1, made, own)
     parts, far_parts = made[:PARTS], made[PARTS:]
-    other = swap(own)
-    part = pull(other, far_parts[:2], pull(own, parts[:2]))
+    others = [swap(first), swap(second)]
+    part = pull([first, second], parts[:2])
+    for place, other in enumerate(others):
+        part = pull([other], far_parts[:2], place * zs // 2, part)
     pieces = total(exchange(part.reshape(row_count, -1, wide), ROW), row_count, 1.0 / row_total)
     pulled = exchange(pieces, ROW).reshape(-1, wide)
 

time: 153 us -> 153 us (level)
    ppermute x7 -> x8, starting transfers between devices: 12.4 us -> 12.5 us  [swap(): return lax.ppermute(value, 'core', SWAP)]
  transfers between devices with their start and end apart: 7 -> 8, of which waited for: 4 -> 3; matrix products, arithmetic and copies ran while one was open for 0% -> 0% of each run, Pallas kernels for 5% -> 5%
where the time goes in v10:
time: 153 us
  blocking collectives  110 us (72%)
  Pallas kernels  27.1 us (18%)
  starting transfers between devices  12.5 us (8%)
  waiting for transfers between devices  2.55 us (2%)
    all_to_all x7, blocking collectives, exchange(): return lax.all_to_all(value, axes, 0, 0, tiled=False)  110 us
    ppermute x8, starting transfers between devices, swap(): return lax.ppermute(value, 'core', SWAP)  12.5 us
    pallas_call x11, Pallas kernels, small_call(): pl.pallas_call(without(kernel, len(scalars) + len(operands), len(after)),...  8.07 us
    pallas_call x2, Pallas kernels, multiply(): pl.pallas_call(multiply_kernel, in_specs=[pl.BlockSpec(memory_space=pltpu...  6.4 us
    pallas_call x2, Pallas kernels, parts_of(): pl.pallas_call(kernel, in_specs=[pl.BlockSpec(memory_space=pltpu.SMEM), h...  6.14 us
    pallas_call x2, Pallas kernels, project(): pl.pallas_call(project_kernel, in_specs=[memory] * 4, out_specs=memory, o...  3.91 us
  transfers between devices with their start and end apart: 8, of which 3 were waited for; matrix products, arithmetic and copies ran while one was open for 0% of the time, Pallas kernels for 5%

profile of v10, /device:TPU:1, one launch (start us, length us, event | category | flops | bytes accessed | tf_op | source)
XLA Modules:
  0.0 152.7 jit_solution(2472602351470636383)
XLA Ops:
  0.6 3.2 %multiply.3 = f32[8,128,128]{2,1,0:T(8,128)S(1)} custom-call(s32[1]{0:T(128)S(6)} %sub.3.half_ref, f32[8,2,128,1024]{3,2,1,0:T(8,128)} %bitcast.11, f32[1024,128]{1,0:T(8,128)} %right_ref.3), custom_call_target="tpu_custom_call" | custom-call | flops 1073741824 | bytes 4194304 | tf_op jit(solution)/shard_map/multiply/pallas_call | solution.py:99
  3.8 3.3 %collective-permute-start = (f32[8,128,128]{2,1,0:T(8,128)S(1)}, f32[8,128,128]{2,1,0:T(8,128)S(1)}, u32[]{:S(2)}, u32[]{:S(2)}) collective-permute-start(f32[8,128,128]{2,1,0:T(8,128)S(1)} %multiply.3), channel_id=1, source_target_pairs={{0,1},{1,0},{2,3},{3,2},{4,5},{5,4},{6,7},{7,6},{8,9},{9,8},{10,11... | collective-permute-start | bytes 1572872 | tf_op jit(solution)/shard_map/ppermute | solution.py:25
  7.2 3.2 %multiply.2.refs_0_ = f32[8,128,128]{2,1,0:T(8,128)S(1)} custom-call(s32[1]{0:T(128)} %bitcast.half_ref.refs_0_, f32[8,2,128,1024]{3,2,1,0:T(8,128)} %bitcast.12, f32[1024,128]{1,0:T(8,128)} %right_ref.3), custom_call_target="tpu_custom_call" | custom-call | flops 1073741824 | bytes 4194304 | tf_op jit(solution)/shard_map/multiply/pallas_call | solution.py:99
  10.4 0.2 parts.2
  10.6 18.5 %all_to_all.35.refs_0_ = f32[8,128,128]{2,1,0:T(8,128)S(1)} all-to-all(f32[8,128,128]{2,1,0:T(8,128)S(1)} %add.1), channel_id=1, replica_groups=mesh['y'=4,'x'=4,'z'=8,'core'=2] {'z'}, dimensions={0} | all-to-all | bytes 1048576 | tf_op jit(solution)/shard_map/all_to_all | solution.py:29
  29.1 14.5 %all_to_all.36.refs_2_ = f32[8,128,128]{2,1,0:T(8,128)S(1)} all-to-all(f32[8,128,128]{2,1,0:T(8,128)S(1)} %total.4), channel_id=1, replica_groups=mesh['y'=4,'x'=4,'z'=8,'core'=2] {'z'}, dimensions={0} | all-to-all | bytes 1048576 | tf_op jit(solution)/shard_map/all_to_all | solution.py:29
  43.7 6.0 %parts.3 = (bf16[8,128,1024]{2,1,0:T(8,128)(2,1)S(1)}, bf16[8,128,1024]{2,1,0:T(8,128)(2,1)S(1)}, bf16[1024,1024]{1,0:T(8,128)(2,1)S(1)}, bf16[1024,1024]{1,0:T(...) custom-call(s32[1]{0:T(128)} %bitcast.half_ref.refs_0_, ...), custom_call_target="tpu_custom_call", output_to_operand_aliasing={{0}: (3, {}), {1}: (4, {}), {2}: (5, {}), {3}: (6, {}), {4}... | custom-call | flops 2147483648 | bytes 8388608 | tf_op jit(solution)/shard_map/parts/pallas_call | solution.py:165
  49.7 2.6 %collective-permute-start.2 = (f32[4,128,128]{2,1,0:T(8,128)S(1)}, f32[4,128,128]{2,1,0:T(8,128)S(1)}, u32[]{:S(2)}, u32[]{:S(2)}) collective-permute-start(f32[4,128,128]{2,1,0:T(8,128)S(1)} %get-tuple-element.43.refs_0_), channel_id=1, source_target_pairs={{0,1},{1,0},{2,3},{3,2},{4,5},{5,4},{6,7},{7,6},{8,9},{9,8},{10,11... | collective-permute-start | bytes 786440 | tf_op jit(solution)/shard_map/ppermute | solution.py:25
  52.3 0.1 collective-permute-start.1
  52.4 1.1 pull.3.refs_3_
  53.5 0.7 pull.4.refs_3_
  54.3 0.7 pull.5
  55.0 17.2 %all_to_all.37.refs_0_ = f32[16,64,128]{2,1,0:T(8,128)S(1)} all-to-all(f32[16,64,128]{2,1,0:T(8,128)S(1)} %bitcast.5), channel_id=1, replica_groups=mesh['y'=4,'x'=4,'z'=8,'core'=2] {'y','x'}, dimensions={0} | all-to-all | bytes 1048576 | tf_op jit(solution)/shard_map/all_to_all | solution.py:29
  72.2 0.1 total.5
  72.3 13.4 %all_to_all.38 = f32[16,64,128]{2,1,0:T(8,128)S(1)} all-to-all(f32[16,64,128]{2,1,0:T(8,128)S(1)} %total.5), channel_id=1, replica_groups=mesh['y'=4,'x'=4,'z'=8,'core'=2] {'y','x'}, dimensions={0} | all-to-all | bytes 1048576 | tf_op jit(solution)/shard_map/all_to_all | solution.py:29
  85.7 2.0 %project.3 = f32[8,128,128]{2,1,0:T(8,128)S(1)} custom-call(f32[1024,128]{1,0:T(8,128)S(1)} %bitcast.6, bf16[1024,1024]{1,0:T(8,128)(2,1)S(1)} %get-tuple-element.49.high_ref, bf16[1024,1024]{1,0:T(8,128)(2,1)S(1)} %get-tuple-element.50.middle_ref, bf16[1024,1024]{1,0:T(8,128)(2,1)S(1)} %get-tuple-element.51.low_ref), custom_call_target="tpu_custom_call" | custom-call | flops 2147483648 | bytes 4194304 | tf_op jit(solution)/shard_map/project/pallas_call | solution.py:208
  87.7 2.4 %collective-permute-start.3 = (f32[8,128,128]{2,1,0:T(8,128)S(1)}, f32[8,128,128]{2,1,0:T(8,128)S(1)}, u32[]{:S(2)}, u32[]{:S(2)}) collective-permute-start(f32[8,128,128]{2,1,0:T(8,128)S(1)} %project.3), channel_id=1, source_target_pairs={{0,1},{1,0},{2,3},{3,2},{4,5},{5,4},{6,7},{7,6},{8,9},{9,8},{10,11... | collective-permute-start | bytes 1572872 | tf_op jit(solution)/shard_map/ppermute | solution.py:25
  90.1 0.5 gram.1
  90.6 0.3 collective-permute-start.4
  91.0 2.0 %project.2.refs_0_ = f32[8,128,128]{2,1,0:T(8,128)S(1)} custom-call(f32[1024,128]{1,0:T(8,128)S(1)} %bitcast.8, bf16[1024,1024]{1,0:T(8,128)(2,1)S(1)} %get-tuple-element.46.high_ref, bf16[1024,1024]{1,0:T(8,128)(2,1)S(1)} %get-tuple-element.47.middle_ref, bf16[1024,1024]{1,0:T(8,128)(2,1)S(1)} %get-tuple-element.48.low_ref), custom_call_target="tpu_custom_call" | custom-call | flops 2147483648 | bytes 4194304 | tf_op jit(solution)/shard_map/project/pallas_call | solution.py:208
  92.9 0.1 join.1
  93.0 23.8 %all_to_all.39.refs_0_.refs_1_ = f32[8,168,128]{2,1,0:T(8,128)S(1)} all-to-all(f32[8,168,128]{2,1,0:T(8,128)S(1)} %join.1), channel_id=1, replica_groups=mesh['y'=4,'x'=4,'z'=8,'core'=2] {'z'}, dimensions={0} | all-to-all | bytes 1376256 | tf_op jit(solution)/shard_map/all_to_all | solution.py:29
  116.8 0.7 collective-permute-start.5
  117.5 0.8 collective-permute-done.5.refs_3_
  118.3 3.5 %middle.1 = (f32[128,128]{1,0:T(8,128)S(1)}, f32[128,128]{1,0:T(8,128)S(1)}, f32[40,128]{1,0:T(8,128)S(1)}, f32[40,128]{1,0:T(8,128)S(1)}) custom-call(s32[1]{0:T(128)} %bitcast.half_ref.refs_0_, f32[8,168,128]{2,1,0:T(8,128)S(1)} %all_to_all.39.refs_0_.refs_1_, f32[40,128]{1,0:T(8,128)S(1)} %tail.1.refs_2_, f32[40,128]{1,0:T(8,128)S(1)} %collective-permute-done.5.refs_3_), custom_call_target="tpu_custom_call" | custom-call | flops 4300000256 | bytes 512 | tf_op jit(solution)/shard_map/middle/pallas_call | solution.py:363
  121.8 0.4 collective-permute-start.6
  122.3 0.8 collective-permute-done.6.refs_1_
  123.1 11.5 %all_to_all.40.refs_0_ = f32[16,40,128]{2,1,0:T(8,128)S(1)} all-to-all(f32[16,40,128]{2,1,0:T(8,128)S(1)} %pair.1), channel_id=1, replica_groups=mesh['y'=4,'x'=4,'z'=8,'core'=2] {'y','x'}, dimensions={0} | all-to-all | bytes 655360 | tf_op jit(solution)/shard_map/all_to_all | solution.py:29
  134.7 10.8 %all_to_all.41.refs_0_ = f32[8,40,128]{2,1,0:T(8,128)S(1)} all-to-all(f32[8,40,128]{2,1,0:T(8,128)S(1)} %total.6), channel_id=1, replica_groups=mesh['y'=4,'x'=4,'z'=8,'core'=2] {'z'}, dimensions={0} | all-to-all | bytes 327680 | tf_op jit(solution)/shard_map/all_to_all | solution.py:29
  145.5 2.6 %collective-permute-start.7 = (f32[40,128]{1,0:T(8,128)S(1)}, f32[40,128]{1,0:T(8,128)S(1)}, u32[]{:S(2)}, u32[]{:S(2)}) collective-permute-start(f32[40,128]{1,0:T(8,128)S(1)} %bitcast.9), channel_id=1, source_target_pairs={{0,1},{1,0},{2,3},{3,2},{4,5},{5,4},{6,7},{7,6},{8,9},{9,8},{10,11... | collective-permute-start | bytes 61448 | tf_op jit(solution)/shard_map/ppermute | solution.py:25
  148.1 0.8 collective-permute-done.7.refs_2_
  148.9 3.7 %last.1 = (f32[128,128]{1,0:T(8,128)}, f32[128,128]{1,0:T(8,128)}) custom-call(s32[1]{0:T(128)} %bitcast.half_ref.refs_0_, f32[40,128]{1,0:T(8,128)S(1)} %bitcast.10, f32[40,128]{1,0:T(8,128)S(1)} %collective-permute-done.7.refs_2_, f32[128,128]{1,0:T(8,128)S(1)} %get-tuple-element.56.refs_3_, f32[128,128]{1,0:T(8,128)S(1)} %get-tuple-element.57.refs_4_), custom_call_target="tpu_custom_call" | custom-call | flops 4600000000 | bytes 512 | tf_op jit(solution)/shard_map/last/pallas_call | solution.py:363
  (11 shorter events, 0.2 us)
Async XLA Ops:
  3.8 6.7 %collective-permute-start = (f32[8,128,128]{2,1,0:T(8,128)S(1)}, f32[8,128,128]{2,1,0:T(8,128)S(1)}, u32[]{:S(2)}, u32[]{:S(2)}) collective-permute-start(f32[8,128,128]{2,1,0:T(8,128)S(1)} %multiply.3), channel_id=1, source_target_pairs={{0,1},{1,0},{2,3},{3,2},{4,5},{5,4},{6,7},{7,6},{8,9},{9,8},{10,11... | collective-permute-start | bytes 1572872 | tf_op jit(solution)/shard_map/ppermute | solution.py:25
  49.7 3.8 %collective-permute-start.2 = (f32[4,128,128]{2,1,0:T(8,128)S(1)}, f32[4,128,128]{2,1,0:T(8,128)S(1)}, u32[]{:S(2)}, u32[]{:S(2)}) collective-permute-start(f32[4,128,128]{2,1,0:T(8,128)S(1)} %get-tuple-element.43.refs_0_), channel_id=1, source_target_pairs={{0,1},{1,0},{2,3},{3,2},{4,5},{5,4},{6,7},{7,6},{8,9},{9,8},{10,11... | collective-permute-start | bytes 786440 | tf_op jit(solution)/shard_map/ppermute | solution.py:25
  52.3 2.0 %collective-permute-start.1 = (f32[4,128,128]{2,1,0:T(8,128)S(1)}, f32[4,128,128]{2,1,0:T(8,128)S(1)}, u32[]{:S(2)}, u32[]{:S(2)}) collective-permute-start(f32[4,128,128]{2,1,0:T(8,128)S(1)} %get-tuple-element.40.refs_1_), channel_id=1, source_target_pairs={{0,1},{1,0},{2,3},{3,2},{4,5},{5,4},{6,7},{7,6},{8,9},{9,8},{10,11... | collective-permute-start | bytes 786440 | tf_op jit(solution)/shard_map/ppermute | solution.py:25
  87.7 5.3 %collective-permute-start.3 = (f32[8,128,128]{2,1,0:T(8,128)S(1)}, f32[8,128,128]{2,1,0:T(8,128)S(1)}, u32[]{:S(2)}, u32[]{:S(2)}) collective-permute-start(f32[8,128,128]{2,1,0:T(8,128)S(1)} %project.3), channel_id=1, source_target_pairs={{0,1},{1,0},{2,3},{3,2},{4,5},{5,4},{6,7},{7,6},{8,9},{9,8},{10,11... | collective-permute-start | bytes 1572872 | tf_op jit(solution)/shard_map/ppermute | solution.py:25
  90.6 2.3 %collective-permute-start.4 = (f32[40,128]{1,0:T(8,128)S(1)}, f32[40,128]{1,0:T(8,128)S(1)}, u32[]{:S(2)}, u32[]{:S(2)}) collective-permute-start(f32[40,128]{1,0:T(8,128)S(1)} %get-tuple-element.53), channel_id=1, source_target_pairs={{0,1},{1,0},{2,3},{3,2},{4,5},{5,4},{6,7},{7,6},{8,9},{9,8},{10,11... | collective-permute-start | bytes 61448 | tf_op jit(solution)/shard_map/ppermute | solution.py:25
  116.8 1.5 %collective-permute-start.5 = (f32[40,128]{1,0:T(8,128)S(1)}, f32[40,128]{1,0:T(8,128)S(1)}, u32[]{:S(2)}, u32[]{:S(2)}) collective-permute-start(f32[40,128]{1,0:T(8,128)S(1)} %tail.1.refs_2_), channel_id=1, source_target_pairs={{0,1},{1,0},{2,3},{3,2},{4,5},{5,4},{6,7},{7,6},{8,9},{9,8},{10,11... | collective-permute-start | bytes 61448 | tf_op jit(solution)/shard_map/ppermute | solution.py:25
  121.8 1.3 collective-permute-start.6
  145.5 3.5 %collective-permute-start.7 = (f32[40,128]{1,0:T(8,128)S(1)}, f32[40,128]{1,0:T(8,128)S(1)}, u32[]{:S(2)}, u32[]{:S(2)}) collective-permute-start(f32[40,128]{1,0:T(8,128)S(1)} %bitcast.9), channel_id=1, source_target_pairs={{0,1},{1,0},{2,3},{3,2},{4,5},{5,4},{6,7},{7,6},{8,9},{9,8},{10,11... | collective-permute-start | bytes 61448 | tf_op jit(solution)/shard_map/ppermute | solution.py:25

commit v11 on v10

--- a/solution.py
+++ b/solution.py
@@ -16,7 +16,7 @@
 SWAP = [(0, 1), (1, 0)]
 TILE = 8
 PANEL = 16
-STEP = 2
+STEP = 4
 PARTS = 5
 VMEM = 12 * 1024 * 1024
 

time: 153 us -> 153 us (level)
  no operation moved by 1% of the time
where the time goes in v11:
time: 153 us
  blocking collectives  110 us (72%)
  Pallas kernels  26.9 us (18%)
  starting transfers between devices  12.7 us (8%)
  waiting for transfers between devices  2.55 us (2%)
    all_to_all x7, blocking collectives, exchange(): return lax.all_to_all(value, axes, 0, 0, tiled=False)  110 us
    ppermute x8, starting transfers between devices, swap(): return lax.ppermute(value, 'core', SWAP)  12.7 us
    pallas_call x11, Pallas kernels, small_call(): pl.pallas_call(without(kernel, len(scalars) + len(operands), len(after)),...  8.08 us
    pallas_call x2, Pallas kernels, multiply(): pl.pallas_call(multiply_kernel, in_specs=[pl.BlockSpec(memory_space=pltpu...  6.37 us
    pallas_call x2, Pallas kernels, parts_of(): pl.pallas_call(kernel, in_specs=[pl.BlockSpec(memory_space=pltpu.SMEM), h...  5.96 us
    pallas_call x2, Pallas kernels, project(): pl.pallas_call(project_kernel, in_specs=[memory] * 4, out_specs=memory, o...  3.91 us
  transfers between devices with their start and end apart: 8, of which 3 were waited for; matrix products, arithmetic and copies ran while one was open for 0% of the time, Pallas kernels for 5%

profile of v11, /device:TPU:1, one launch (start us, length us, event | category | flops | bytes accessed | tf_op | source)
XLA Modules:
  0.0 152.7 jit_solution(5392379306038423813)
XLA Ops:
  0.6 3.2 %multiply.3 = f32[8,128,128]{2,1,0:T(8,128)S(1)} custom-call(s32[1]{0:T(128)S(6)} %sub.3.half_ref, f32[8,2,128,1024]{3,2,1,0:T(8,128)} %bitcast.11, f32[1024,128]{1,0:T(8,128)} %right_ref.3), custom_call_target="tpu_custom_call" | custom-call | flops 1073741824 | bytes 4194304 | tf_op jit(solution)/shard_map/multiply/pallas_call | solution.py:99
  3.8 3.3 %collective-permute-start = (f32[8,128,128]{2,1,0:T(8,128)S(1)}, f32[8,128,128]{2,1,0:T(8,128)S(1)}, u32[]{:S(2)}, u32[]{:S(2)}) collective-permute-start(f32[8,128,128]{2,1,0:T(8,128)S(1)} %multiply.3), channel_id=1, source_target_pairs={{0,1},{1,0},{2,3},{3,2},{4,5},{5,4},{6,7},{7,6},{8,9},{9,8},{10,11... | collective-permute-start | bytes 1572872 | tf_op jit(solution)/shard_map/ppermute | solution.py:25
  7.2 3.2 %multiply.2.refs_0_ = f32[8,128,128]{2,1,0:T(8,128)S(1)} custom-call(s32[1]{0:T(128)} %bitcast.half_ref.refs_0_, f32[8,2,128,1024]{3,2,1,0:T(8,128)} %bitcast.12, f32[1024,128]{1,0:T(8,128)} %right_ref.3), custom_call_target="tpu_custom_call" | custom-call | flops 1073741824 | bytes 4194304 | tf_op jit(solution)/shard_map/multiply/pallas_call | solution.py:99
  10.3 0.2 parts.2
  10.6 18.5 %all_to_all.35.refs_0_ = f32[8,128,128]{2,1,0:T(8,128)S(1)} all-to-all(f32[8,128,128]{2,1,0:T(8,128)S(1)} %add.1), channel_id=1, replica_groups=mesh['y'=4,'x'=4,'z'=8,'core'=2] {'z'}, dimensions={0} | all-to-all | bytes 1048576 | tf_op jit(solution)/shard_map/all_to_all | solution.py:29
  29.1 14.5 %all_to_all.36.refs_2_ = f32[8,128,128]{2,1,0:T(8,128)S(1)} all-to-all(f32[8,128,128]{2,1,0:T(8,128)S(1)} %total.4), channel_id=1, replica_groups=mesh['y'=4,'x'=4,'z'=8,'core'=2] {'z'}, dimensions={0} | all-to-all | bytes 1048576 | tf_op jit(solution)/shard_map/all_to_all | solution.py:29
  43.7 5.8 %parts.3 = (bf16[8,128,1024]{2,1,0:T(8,128)(2,1)S(1)}, bf16[8,128,1024]{2,1,0:T(8,128)(2,1)S(1)}, bf16[1024,1024]{1,0:T(8,128)(2,1)S(1)}, bf16[1024,1024]{1,0:T(...) custom-call(s32[1]{0:T(128)} %bitcast.half_ref.refs_0_, ...), custom_call_target="tpu_custom_call", output_to_operand_aliasing={{0}: (3, {}), {1}: (4, {}), {2}: (5, {}), {3}: (6, {}), {4}... | custom-call | flops 2147483648 | bytes 8388608 | tf_op jit(solution)/shard_map/parts/pallas_call | solution.py:165
  49.5 2.7 %collective-permute-start.2 = (f32[4,128,128]{2,1,0:T(8,128)S(1)}, f32[4,128,128]{2,1,0:T(8,128)S(1)}, u32[]{:S(2)}, u32[]{:S(2)}) collective-permute-start(f32[4,128,128]{2,1,0:T(8,128)S(1)} %get-tuple-element.43.refs_0_), channel_id=1, source_target_pairs={{0,1},{1,0},{2,3},{3,2},{4,5},{5,4},{6,7},{7,6},{8,9},{9,8},{10,11... | collective-permute-start | bytes 786440 | tf_op jit(solution)/shard_map/ppermute | solution.py:25
  52.3 0.1 collective-permute-start.1
  52.4 1.1 pull.3.refs_3_
  53.5 0.7 pull.4.refs_3_
  54.3 0.7 pull.5
  55.0 17.2 %all_to_all.37.refs_0_ = f32[16,64,128]{2,1,0:T(8,128)S(1)} all-to-all(f32[16,64,128]{2,1,0:T(8,128)S(1)} %bitcast.5), channel_id=1, replica_groups=mesh['y'=4,'x'=4,'z'=8,'core'=2] {'y','x'}, dimensions={0} | all-to-all | bytes 1048576 | tf_op jit(solution)/shard_map/all_to_all | solution.py:29
  72.2 0.1 total.5
  72.3 13.4 %all_to_all.38 = f32[16,64,128]{2,1,0:T(8,128)S(1)} all-to-all(f32[16,64,128]{2,1,0:T(8,128)S(1)} %total.5), channel_id=1, replica_groups=mesh['y'=4,'x'=4,'z'=8,'core'=2] {'y','x'}, dimensions={0} | all-to-all | bytes 1048576 | tf_op jit(solution)/shard_map/all_to_all | solution.py:29
  85.7 2.0 %project.3 = f32[8,128,128]{2,1,0:T(8,128)S(1)} custom-call(f32[1024,128]{1,0:T(8,128)S(1)} %bitcast.6, bf16[1024,1024]{1,0:T(8,128)(2,1)S(1)} %get-tuple-element.49.high_ref, bf16[1024,1024]{1,0:T(8,128)(2,1)S(1)} %get-tuple-element.50.middle_ref, bf16[1024,1024]{1,0:T(8,128)(2,1)S(1)} %get-tuple-element.51.low_ref), custom_call_target="tpu_custom_call" | custom-call | flops 2147483648 | bytes 4194304 | tf_op jit(solution)/shard_map/project/pallas_call | solution.py:208
  87.7 2.4 %collective-permute-start.3 = (f32[8,128,128]{2,1,0:T(8,128)S(1)}, f32[8,128,128]{2,1,0:T(8,128)S(1)}, u32[]{:S(2)}, u32[]{:S(2)}) collective-permute-start(f32[8,128,128]{2,1,0:T(8,128)S(1)} %project.3), channel_id=1, source_target_pairs={{0,1},{1,0},{2,3},{3,2},{4,5},{5,4},{6,7},{7,6},{8,9},{9,8},{10,11... | collective-permute-start | bytes 1572872 | tf_op jit(solution)/shard_map/ppermute | solution.py:25
  90.1 0.5 gram.1
  90.6 0.1 collective-permute-start.4
  90.7 2.0 %project.2.refs_0_ = f32[8,128,128]{2,1,0:T(8,128)S(1)} custom-call(f32[1024,128]{1,0:T(8,128)S(1)} %bitcast.8, bf16[1024,1024]{1,0:T(8,128)(2,1)S(1)} %get-tuple-element.46.high_ref, bf16[1024,1024]{1,0:T(8,128)(2,1)S(1)} %get-tuple-element.47.middle_ref, bf16[1024,1024]{1,0:T(8,128)(2,1)S(1)} %get-tuple-element.48.low_ref), custom_call_target="tpu_custom_call" | custom-call | flops 2147483648 | bytes 4194304 | tf_op jit(solution)/shard_map/project/pallas_call | solution.py:208
  92.7 0.1 join.1
  92.8 23.8 %all_to_all.39.refs_0_.refs_1_ = f32[8,168,128]{2,1,0:T(8,128)S(1)} all-to-all(f32[8,168,128]{2,1,0:T(8,128)S(1)} %join.1), channel_id=1, replica_groups=mesh['y'=4,'x'=4,'z'=8,'core'=2] {'z'}, dimensions={0} | all-to-all | bytes 1376256 | tf_op jit(solution)/shard_map/all_to_all | solution.py:29
  116.6 0.7 collective-permute-start.5
  117.3 0.8 collective-permute-done.5.refs_3_
  118.1 3.5 %middle.1 = (f32[128,128]{1,0:T(8,128)S(1)}, f32[128,128]{1,0:T(8,128)S(1)}, f32[40,128]{1,0:T(8,128)S(1)}, f32[40,128]{1,0:T(8,128)S(1)}) custom-call(s32[1]{0:T(128)} %bitcast.half_ref.refs_0_, f32[8,168,128]{2,1,0:T(8,128)S(1)} %all_to_all.39.refs_0_.refs_1_, f32[40,128]{1,0:T(8,128)S(1)} %tail.1.refs_2_, f32[40,128]{1,0:T(8,128)S(1)} %collective-permute-done.5.refs_3_), custom_call_target="tpu_custom_call" | custom-call | flops 4300000256 | bytes 512 | tf_op jit(solution)/shard_map/middle/pallas_call | solution.py:363
  121.6 0.4 collective-permute-start.6
  122.0 0.8 collective-permute-done.6.refs_1_
  122.9 11.5 %all_to_all.40.refs_0_ = f32[16,40,128]{2,1,0:T(8,128)S(1)} all-to-all(f32[16,40,128]{2,1,0:T(8,128)S(1)} %pair.1), channel_id=1, replica_groups=mesh['y'=4,'x'=4,'z'=8,'core'=2] {'y','x'}, dimensions={0} | all-to-all | bytes 655360 | tf_op jit(solution)/shard_map/all_to_all | solution.py:29
  134.5 10.8 %all_to_all.41.refs_0_ = f32[8,40,128]{2,1,0:T(8,128)S(1)} all-to-all(f32[8,40,128]{2,1,0:T(8,128)S(1)} %total.6), channel_id=1, replica_groups=mesh['y'=4,'x'=4,'z'=8,'core'=2] {'z'}, dimensions={0} | all-to-all | bytes 327680 | tf_op jit(solution)/shard_map/all_to_all | solution.py:29
  145.2 2.9 %collective-permute-start.7 = (f32[40,128]{1,0:T(8,128)S(1)}, f32[40,128]{1,0:T(8,128)S(1)}, u32[]{:S(2)}, u32[]{:S(2)}) collective-permute-start(f32[40,128]{1,0:T(8,128)S(1)} %bitcast.9), channel_id=1, source_target_pairs={{0,1},{1,0},{2,3},{3,2},{4,5},{5,4},{6,7},{7,6},{8,9},{9,8},{10,11... | collective-permute-start | bytes 61448 | tf_op jit(solution)/shard_map/ppermute | solution.py:25
  148.1 0.8 collective-permute-done.7.refs_2_
  148.9 3.8 %last.1 = (f32[128,128]{1,0:T(8,128)}, f32[128,128]{1,0:T(8,128)}) custom-call(s32[1]{0:T(128)} %bitcast.half_ref.refs_0_, f32[40,128]{1,0:T(8,128)S(1)} %bitcast.10, f32[40,128]{1,0:T(8,128)S(1)} %collective-permute-done.7.refs_2_, f32[128,128]{1,0:T(8,128)S(1)} %get-tuple-element.56.refs_3_, f32[128,128]{1,0:T(8,128)S(1)} %get-tuple-element.57.refs_4_), custom_call_target="tpu_custom_call" | custom-call | flops 4600000000 | bytes 512 | tf_op jit(solution)/shard_map/last/pallas_call | solution.py:363
  (11 shorter events, 0.2 us)
Async XLA Ops:
  3.8 6.7 %collective-permute-start = (f32[8,128,128]{2,1,0:T(8,128)S(1)}, f32[8,128,128]{2,1,0:T(8,128)S(1)}, u32[]{:S(2)}, u32[]{:S(2)}) collective-permute-start(f32[8,128,128]{2,1,0:T(8,128)S(1)} %multiply.3), channel_id=1, source_target_pairs={{0,1},{1,0},{2,3},{3,2},{4,5},{5,4},{6,7},{7,6},{8,9},{9,8},{10,11... | collective-permute-start | bytes 1572872 | tf_op jit(solution)/shard_map/ppermute | solution.py:25
  49.5 4.0 %collective-permute-start.2 = (f32[4,128,128]{2,1,0:T(8,128)S(1)}, f32[4,128,128]{2,1,0:T(8,128)S(1)}, u32[]{:S(2)}, u32[]{:S(2)}) collective-permute-start(f32[4,128,128]{2,1,0:T(8,128)S(1)} %get-tuple-element.43.refs_0_), channel_id=1, source_target_pairs={{0,1},{1,0},{2,3},{3,2},{4,5},{5,4},{6,7},{7,6},{8,9},{9,8},{10,11... | collective-permute-start | bytes 786440 | tf_op jit(solution)/shard_map/ppermute | solution.py:25
  52.3 2.0 %collective-permute-start.1 = (f32[4,128,128]{2,1,0:T(8,128)S(1)}, f32[4,128,128]{2,1,0:T(8,128)S(1)}, u32[]{:S(2)}, u32[]{:S(2)}) collective-permute-start(f32[4,128,128]{2,1,0:T(8,128)S(1)} %get-tuple-element.40.refs_1_), channel_id=1, source_target_pairs={{0,1},{1,0},{2,3},{3,2},{4,5},{5,4},{6,7},{7,6},{8,9},{9,8},{10,11... | collective-permute-start | bytes 786440 | tf_op jit(solution)/shard_map/ppermute | solution.py:25
  87.7 5.0 %collective-permute-start.3 = (f32[8,128,128]{2,1,0:T(8,128)S(1)}, f32[8,128,128]{2,1,0:T(8,128)S(1)}, u32[]{:S(2)}, u32[]{:S(2)}) collective-permute-start(f32[8,128,128]{2,1,0:T(8,128)S(1)} %project.3), channel_id=1, source_target_pairs={{0,1},{1,0},{2,3},{3,2},{4,5},{5,4},{6,7},{7,6},{8,9},{9,8},{10,11... | collective-permute-start | bytes 1572872 | tf_op jit(solution)/shard_map/ppermute | solution.py:25
  90.6 2.1 %collective-permute-start.4 = (f32[40,128]{1,0:T(8,128)S(1)}, f32[40,128]{1,0:T(8,128)S(1)}, u32[]{:S(2)}, u32[]{:S(2)}) collective-permute-start(f32[40,128]{1,0:T(8,128)S(1)} %get-tuple-element.53), channel_id=1, source_target_pairs={{0,1},{1,0},{2,3},{3,2},{4,5},{5,4},{6,7},{7,6},{8,9},{9,8},{10,11... | collective-permute-start | bytes 61448 | tf_op jit(solution)/shard_map/ppermute | solution.py:25
  116.6 1.5 %collective-permute-start.5 = (f32[40,128]{1,0:T(8,128)S(1)}, f32[40,128]{1,0:T(8,128)S(1)}, u32[]{:S(2)}, u32[]{:S(2)}) collective-permute-start(f32[40,128]{1,0:T(8,128)S(1)} %tail.1.refs_2_), channel_id=1, source_target_pairs={{0,1},{1,0},{2,3},{3,2},{4,5},{5,4},{6,7},{7,6},{8,9},{9,8},{10,11... | collective-permute-start | bytes 61448 | tf_op jit(solution)/shard_map/ppermute | solution.py:25
  121.6 1.3 collective-permute-start.6
  145.2 3.7 %collective-permute-start.7 = (f32[40,128]{1,0:T(8,128)S(1)}, f32[40,128]{1,0:T(8,128)S(1)}, u32[]{:S(2)}, u32[]{:S(2)}) collective-permute-start(f32[40,128]{1,0:T(8,128)S(1)} %bitcast.9), channel_id=1, source_target_pairs={{0,1},{1,0},{2,3},{3,2},{4,5},{5,4},{6,7},{7,6},{8,9},{9,8},{10,11... | collective-permute-start | bytes 61448 | tf_op jit(solution)/shard_map/ppermute | solution.py:25

commit v12 on v9

--- a/solution.py
+++ b/solution.py
@@ -249,7 +249,7 @@
     return jnp.broadcast_to(row, (TILE, row.shape[1]))
 
 
-def eliminate(gram, floor):
+def eliminate(gram, floor=None):
     n = gram.shape[0]
     count, per = n // TILE, PANEL // TILE
     sub = lax.broadcasted_iota(jnp.int32, (TILE, n), 0)
@@ -269,7 +269,9 @@
         pivots = []
         for s in range(PANEL):
             here, at = start + s // TILE, s % TILE
-            pivot = jnp.maximum(spread(column[s, here][at : at + 1]), floor)
+            pivot = spread(column[s, here][at : at + 1])
+            if floor is not None:
+                pivot = jnp.maximum(pivot, floor)
             over = 1.0 / pivot
             pivots.append(pivot)
             entry = {
@@ -438,7 +440,7 @@
     root_rows, core_ref, own_ref, other_ref, inner_ref, before_ref, basis_ref, factor_ref
 ):
     gram = load_halves(core_ref[0], own_ref[...], other_ref[...])
-    upper, lower = eliminate(gram, floor_of(gram))
+    upper, lower = eliminate(gram)
     basis_ref[...] = stacked(inner_ref[...], lower, TRANSPOSED) * root_rows
     factor_ref[...] = stacked(upper, before_ref[...], PLAIN) / root_rows
 

time: 153 us -> 153 us (level)
  no operation moved by 1% of the time
where the time goes in v12:
time: 153 us; the launch traced here: 152 us
  blocking collectives  110 us (72%)
  Pallas kernels  26.6 us (17%)
  starting transfers between devices  12.4 us (8%)
  waiting for transfers between devices  2.94 us (2%)
    all_to_all x7, blocking collectives, exchange(): return lax.all_to_all(value, axes, 0, 0, tiled=False)  110 us
    ppermute x7, starting transfers between devices, swap(): return lax.ppermute(value, 'core', SWAP)  12.4 us
    pallas_call x11, Pallas kernels, small_call(): pl.pallas_call(without(kernel, len(scalars) + len(operands), len(after)),...  8.08 us
    pallas_call x2, Pallas kernels, multiply(): pl.pallas_call(multiply_kernel, in_specs=[pl.BlockSpec(memory_space=pltpu...  6.4 us
    pallas_call x2, Pallas kernels, parts_of(): pl.pallas_call(kernel, in_specs=[pl.BlockSpec(memory_space=pltpu.SMEM), h...  5.93 us
    pallas_call x2, Pallas kernels, project(): pl.pallas_call(project_kernel, in_specs=[memory] * 4, out_specs=memory, o...  3.91 us
  transfers between devices with their start and end apart: 7, of which 4 were waited for; matrix products, arithmetic and copies ran while one was open for 0% of the time, Pallas kernels for 5%

profile of v12, /device:TPU:1, one launch (start us, length us, event | category | flops | bytes accessed | tf_op | source)
XLA Modules:
  0.0 152.5 jit_solution(2845735301770851996)
XLA Ops:
  0.6 3.2 %multiply.3 = f32[8,128,128]{2,1,0:T(8,128)S(1)} custom-call(s32[1]{0:T(128)S(6)} %sub.3.half_ref, f32[8,2,128,1024]{3,2,1,0:T(8,128)} %bitcast.11, f32[1024,128]{1,0:T(8,128)} %right_ref.3), custom_call_target="tpu_custom_call" | custom-call | flops 1073741824 | bytes 4194304 | tf_op jit(solution)/shard_map/multiply/pallas_call | solution.py:100
  3.8 3.3 %collective-permute-start = (f32[8,128,128]{2,1,0:T(8,128)S(1)}, f32[8,128,128]{2,1,0:T(8,128)S(1)}, u32[]{:S(2)}, u32[]{:S(2)}) collective-permute-start(f32[8,128,128]{2,1,0:T(8,128)S(1)} %multiply.3), channel_id=1, source_target_pairs={{0,1},{1,0},{2,3},{3,2},{4,5},{5,4},{6,7},{7,6},{8,9},{9,8},{10,11... | collective-permute-start | bytes 1572872 | tf_op jit(solution)/shard_map/ppermute | solution.py:26
  7.2 3.2 %multiply.2.refs_0_ = f32[8,128,128]{2,1,0:T(8,128)S(1)} custom-call(s32[1]{0:T(128)} %bitcast.half_ref.refs_0_, f32[8,2,128,1024]{3,2,1,0:T(8,128)} %bitcast.12, f32[1024,128]{1,0:T(8,128)} %right_ref.3), custom_call_target="tpu_custom_call" | custom-call | flops 1073741824 | bytes 4194304 | tf_op jit(solution)/shard_map/multiply/pallas_call | solution.py:100
  10.4 0.2 parts.2
  10.5 0.1 add.1
  10.6 18.5 %all_to_all.35.refs_0_ = f32[8,128,128]{2,1,0:T(8,128)S(1)} all-to-all(f32[8,128,128]{2,1,0:T(8,128)S(1)} %add.1), channel_id=1, replica_groups=mesh['y'=4,'x'=4,'z'=8,'core'=2] {'z'}, dimensions={0} | all-to-all | bytes 1048576 | tf_op jit(solution)/shard_map/all_to_all | solution.py:30
  29.1 14.5 %all_to_all.36.refs_2_ = f32[8,128,128]{2,1,0:T(8,128)S(1)} all-to-all(f32[8,128,128]{2,1,0:T(8,128)S(1)} %total.4), channel_id=1, replica_groups=mesh['y'=4,'x'=4,'z'=8,'core'=2] {'z'}, dimensions={0} | all-to-all | bytes 1048576 | tf_op jit(solution)/shard_map/all_to_all | solution.py:30
  43.7 5.8 %parts.3 = (bf16[8,128,1024]{2,1,0:T(8,128)(2,1)S(1)}, bf16[8,128,1024]{2,1,0:T(8,128)(2,1)S(1)}, bf16[1024,1024]{1,0:T(8,128)(2,1)S(1)}, bf16[1024,1024]{1,0:T(...) custom-call(s32[1]{0:T(128)} %bitcast.half_ref.refs_0_, ...), custom_call_target="tpu_custom_call", output_to_operand_aliasing={{10}: (2, {}), {0}: (3, {}), {1}: (4, {}), {2}: (5, {}), {3... | custom-call | flops 2147483648 | bytes 8388608 | tf_op jit(solution)/shard_map/parts/pallas_call | solution.py:163
  49.5 2.6 %collective-permute-start.1 = (f32[8,128,128]{2,1,0:T(8,128)S(1)}, f32[8,128,128]{2,1,0:T(8,128)S(1)}, u32[]{:S(2)}, u32[]{:S(2)}) collective-permute-start(f32[8,128,128]{2,1,0:T(8,128)S(1)} %get-tuple-element.39.left_ref), channel_id=1, source_target_pairs={{0,1},{1,0},{2,3},{3,2},{4,5},{5,4},{6,7},{7,6},{8,9},{9,8},{10,11... | collective-permute-start | bytes 1572872 | tf_op jit(solution)/shard_map/ppermute | solution.py:26
  52.1 1.1 pull.2.refs_0_
  53.2 0.4 collective-permute-done.1.left_ref
  53.6 1.1 pull.3
  54.7 17.3 %all_to_all.37.refs_0_ = f32[16,64,128]{2,1,0:T(8,128)S(1)} all-to-all(f32[16,64,128]{2,1,0:T(8,128)S(1)} %bitcast.5), channel_id=1, replica_groups=mesh['y'=4,'x'=4,'z'=8,'core'=2] {'y','x'}, dimensions={0} | all-to-all | bytes 1048576 | tf_op jit(solution)/shard_map/all_to_all | solution.py:30
  72.0 0.1 total.5
  72.1 13.4 %all_to_all.38 = f32[16,64,128]{2,1,0:T(8,128)S(1)} all-to-all(f32[16,64,128]{2,1,0:T(8,128)S(1)} %total.5), channel_id=1, replica_groups=mesh['y'=4,'x'=4,'z'=8,'core'=2] {'y','x'}, dimensions={0} | all-to-all | bytes 1048576 | tf_op jit(solution)/shard_map/all_to_all | solution.py:30
  85.5 2.0 %project.3 = f32[8,128,128]{2,1,0:T(8,128)S(1)} custom-call(f32[1024,128]{1,0:T(8,128)S(1)} %bitcast.6, bf16[1024,1024]{1,0:T(8,128)(2,1)S(1)} %get-tuple-element.47.high_ref, bf16[1024,1024]{1,0:T(8,128)(2,1)S(1)} %get-tuple-element.48.middle_ref, bf16[1024,1024]{1,0:T(8,128)(2,1)S(1)} %get-tuple-element.49.low_ref), custom_call_target="tpu_custom_call" | custom-call | flops 2147483648 | bytes 4194304 | tf_op jit(solution)/shard_map/project/pallas_call | solution.py:206
  87.4 2.4 %collective-permute-start.2 = (f32[8,128,128]{2,1,0:T(8,128)S(1)}, f32[8,128,128]{2,1,0:T(8,128)S(1)}, u32[]{:S(2)}, u32[]{:S(2)}) collective-permute-start(f32[8,128,128]{2,1,0:T(8,128)S(1)} %project.3), channel_id=1, source_target_pairs={{0,1},{1,0},{2,3},{3,2},{4,5},{5,4},{6,7},{7,6},{8,9},{9,8},{10,11... | collective-permute-start | bytes 1572872 | tf_op jit(solution)/shard_map/ppermute | solution.py:26
  89.9 0.5 gram.1
  90.4 0.1 collective-permute-start.3
  90.5 2.0 %project.2.refs_0_ = f32[8,128,128]{2,1,0:T(8,128)S(1)} custom-call(f32[1024,128]{1,0:T(8,128)S(1)} %bitcast.8, bf16[1024,1024]{1,0:T(8,128)(2,1)S(1)} %get-tuple-element.44.high_ref, bf16[1024,1024]{1,0:T(8,128)(2,1)S(1)} %get-tuple-element.45.middle_ref, bf16[1024,1024]{1,0:T(8,128)(2,1)S(1)} %get-tuple-element.46.low_ref), custom_call_target="tpu_custom_call" | custom-call | flops 2147483648 | bytes 4194304 | tf_op jit(solution)/shard_map/project/pallas_call | solution.py:206
  92.5 0.1 join.1
  92.6 23.8 %all_to_all.39.refs_0_.refs_1_ = f32[8,168,128]{2,1,0:T(8,128)S(1)} all-to-all(f32[8,168,128]{2,1,0:T(8,128)S(1)} %join.1), channel_id=1, replica_groups=mesh['y'=4,'x'=4,'z'=8,'core'=2] {'z'}, dimensions={0} | all-to-all | bytes 1376256 | tf_op jit(solution)/shard_map/all_to_all | solution.py:30
  116.3 0.9 collective-permute-start.4
  117.2 0.8 collective-permute-done.4.refs_3_
  118.1 3.5 %middle.1 = (f32[128,128]{1,0:T(8,128)S(1)}, f32[128,128]{1,0:T(8,128)S(1)}, f32[40,128]{1,0:T(8,128)S(1)}, f32[40,128]{1,0:T(8,128)S(1)}) custom-call(s32[1]{0:T(128)} %bitcast.half_ref.refs_0_, f32[8,168,128]{2,1,0:T(8,128)S(1)} %all_to_all.39.refs_0_.refs_1_, f32[40,128]{1,0:T(8,128)S(1)} %tail.1.refs_2_, f32[40,128]{1,0:T(8,128)S(1)} %collective-permute-done.4.refs_3_), custom_call_target="tpu_custom_call" | custom-call | flops 4300000256 | bytes 512 | tf_op jit(solution)/shard_map/middle/pallas_call | solution.py:363
  121.6 0.4 collective-permute-start.5
  122.0 0.8 collective-permute-done.5.refs_1_
  122.9 11.5 %all_to_all.40.refs_0_ = f32[16,40,128]{2,1,0:T(8,128)S(1)} all-to-all(f32[16,40,128]{2,1,0:T(8,128)S(1)} %pair.1), channel_id=1, replica_groups=mesh['y'=4,'x'=4,'z'=8,'core'=2] {'y','x'}, dimensions={0} | all-to-all | bytes 655360 | tf_op jit(solution)/shard_map/all_to_all | solution.py:30
  134.4 10.8 %all_to_all.41.refs_0_ = f32[8,40,128]{2,1,0:T(8,128)S(1)} all-to-all(f32[8,40,128]{2,1,0:T(8,128)S(1)} %total.6), channel_id=1, replica_groups=mesh['y'=4,'x'=4,'z'=8,'core'=2] {'z'}, dimensions={0} | all-to-all | bytes 327680 | tf_op jit(solution)/shard_map/all_to_all | solution.py:30
  145.2 2.6 %collective-permute-start.6 = (f32[40,128]{1,0:T(8,128)S(1)}, f32[40,128]{1,0:T(8,128)S(1)}, u32[]{:S(2)}, u32[]{:S(2)}) collective-permute-start(f32[40,128]{1,0:T(8,128)S(1)} %bitcast.9), channel_id=1, source_target_pairs={{0,1},{1,0},{2,3},{3,2},{4,5},{5,4},{6,7},{7,6},{8,9},{9,8},{10,11... | collective-permute-start | bytes 61448 | tf_op jit(solution)/shard_map/ppermute | solution.py:26
  147.9 0.8 collective-permute-done.6.refs_2_
  148.7 3.8 %last.1 = (f32[128,128]{1,0:T(8,128)}, f32[128,128]{1,0:T(8,128)}) custom-call(s32[1]{0:T(128)} %bitcast.half_ref.refs_0_, f32[40,128]{1,0:T(8,128)S(1)} %bitcast.10, f32[40,128]{1,0:T(8,128)S(1)} %collective-permute-done.6.refs_2_, f32[128,128]{1,0:T(8,128)S(1)} %get-tuple-element.54.refs_3_, f32[128,128]{1,0:T(8,128)S(1)} %get-tuple-element.55.refs_4_), custom_call_target="tpu_custom_call" | custom-call | flops 4600000000 | bytes 512 | tf_op jit(solution)/shard_map/last/pallas_call | solution.py:363
  (8 shorter events, 0.1 us)
Async XLA Ops:
  3.8 6.7 %collective-permute-start = (f32[8,128,128]{2,1,0:T(8,128)S(1)}, f32[8,128,128]{2,1,0:T(8,128)S(1)}, u32[]{:S(2)}, u32[]{:S(2)}) collective-permute-start(f32[8,128,128]{2,1,0:T(8,128)S(1)} %multiply.3), channel_id=1, source_target_pairs={{0,1},{1,0},{2,3},{3,2},{4,5},{5,4},{6,7},{7,6},{8,9},{9,8},{10,11... | collective-permute-start | bytes 1572872 | tf_op jit(solution)/shard_map/ppermute | solution.py:26
  49.5 4.1 %collective-permute-start.1 = (f32[8,128,128]{2,1,0:T(8,128)S(1)}, f32[8,128,128]{2,1,0:T(8,128)S(1)}, u32[]{:S(2)}, u32[]{:S(2)}) collective-permute-start(f32[8,128,128]{2,1,0:T(8,128)S(1)} %get-tuple-element.39.left_ref), channel_id=1, source_target_pairs={{0,1},{1,0},{2,3},{3,2},{4,5},{5,4},{6,7},{7,6},{8,9},{9,8},{10,11... | collective-permute-start | bytes 1572872 | tf_op jit(solution)/shard_map/ppermute | solution.py:26
  87.4 5.0 %collective-permute-start.2 = (f32[8,128,128]{2,1,0:T(8,128)S(1)}, f32[8,128,128]{2,1,0:T(8,128)S(1)}, u32[]{:S(2)}, u32[]{:S(2)}) collective-permute-start(f32[8,128,128]{2,1,0:T(8,128)S(1)} %project.3), channel_id=1, source_target_pairs={{0,1},{1,0},{2,3},{3,2},{4,5},{5,4},{6,7},{7,6},{8,9},{9,8},{10,11... | collective-permute-start | bytes 1572872 | tf_op jit(solution)/shard_map/ppermute | solution.py:26
  90.4 2.1 %collective-permute-start.3 = (f32[40,128]{1,0:T(8,128)S(1)}, f32[40,128]{1,0:T(8,128)S(1)}, u32[]{:S(2)}, u32[]{:S(2)}) collective-permute-start(f32[40,128]{1,0:T(8,128)S(1)} %get-tuple-element.51), channel_id=1, source_target_pairs={{0,1},{1,0},{2,3},{3,2},{4,5},{5,4},{6,7},{7,6},{8,9},{9,8},{10,11... | collective-permute-start | bytes 61448 | tf_op jit(solution)/shard_map/ppermute | solution.py:26
  116.3 1.8 %collective-permute-start.4 = (f32[40,128]{1,0:T(8,128)S(1)}, f32[40,128]{1,0:T(8,128)S(1)}, u32[]{:S(2)}, u32[]{:S(2)}) collective-permute-start(f32[40,128]{1,0:T(8,128)S(1)} %tail.1.refs_2_), channel_id=1, source_target_pairs={{0,1},{1,0},{2,3},{3,2},{4,5},{5,4},{6,7},{7,6},{8,9},{9,8},{10,11... | collective-permute-start | bytes 61448 | tf_op jit(solution)/shard_map/ppermute | solution.py:26
  121.6 1.3 collective-permute-start.5
  145.2 3.5 %collective-permute-start.6 = (f32[40,128]{1,0:T(8,128)S(1)}, f32[40,128]{1,0:T(8,128)S(1)}, u32[]{:S(2)}, u32[]{:S(2)}) collective-permute-start(f32[40,128]{1,0:T(8,128)S(1)} %bitcast.9), channel_id=1, source_target_pairs={{0,1},{1,0},{2,3},{3,2},{4,5},{5,4},{6,7},{7,6},{8,9},{9,8},{10,11... | collective-permute-start | bytes 61448 | tf_op jit(solution)/shard_map/ppermute | solution.py:26
